TPU v7x, 32 devices: a whole 2x2x4 slice. The times are simulated.
32 devices in a mesh: dp: 4 (over x, core), tile: 8 (over z, y).
Axes of the slice: x: 2, y: 2, z: 4, core: 2. Of those that a mesh axis runs over, the one named last changes fastest.
Arguments:
- embeddings: bfloat16 [4, 1024, 512], P('dp', 'tile'), may hold values from -6 to 6
- page_images: bfloat16 [4, 3, 128, 512], P('dp', None, 'tile'), may hold values from -6 to 6
- token_boxes: int32 [4, 4, 1024], P(None, 'dp', 'tile'), may hold values from 0 to 512, as said below
- segment_ids: int32 [4, 1024], P('dp', 'tile'), may hold values from 0 to 1, as said below
- down_first: bfloat16 [3, 3, 32, 3], replicated, may hold values from -1.25 to 1.25
- down_second: bfloat16 [3, 3, 64, 32], replicated, may hold values from -0.375 to 0.375
- down_third: bfloat16 [3, 3, 128, 64], replicated, may hold values from -0.25 to 0.25
- down_fourth: bfloat16 [3, 3, 256, 128], replicated, may hold values from -0.1875 to 0.1875
- down_fifth: bfloat16 [3, 3, 512, 256], replicated, may hold values from -0.125 to 0.125
- up_fourth: bfloat16 [3, 3, 256, 512], replicated, may hold values from -0.09375 to 0.09375
- up_third: bfloat16 [3, 3, 128, 256], replicated, may hold values from -0.125 to 0.125
- up_second: bfloat16 [3, 3, 64, 128], replicated, may hold values from -0.1875 to 0.1875
- up_first: bfloat16 [3, 3, 32, 64], replicated, may hold values from -0.25 to 0.25
- roi_proj: bfloat16 [128, 512], replicated, may hold values from -1 to 1
- gain_attn: bfloat16 [512], replicated, may hold values from 0.5 to 1.5
- w_query: bfloat16 [512, 512], replicated, may hold values from -0.25 to 0.25
- w_key: bfloat16 [512, 512], replicated, may hold values from -0.25 to 0.25
- w_value: bfloat16 [512, 512], replicated, may hold values from -0.25 to 0.25
- w_output: bfloat16 [512, 512], replicated, may hold values from -6 to 6
- bias_table: bfloat16 [8, 96], replicated, may hold values from -3 to 3
- gain_ffn: bfloat16 [512], replicated, may hold values from 0.5 to 1.5
- ffn_in: bfloat16 [512, 2048], replicated, may hold values from -0.25 to 0.25
- ffn_out: bfloat16 [2048, 512], replicated, may hold values from -0.125 to 0.125
- cotangent: bfloat16 [4, 1024, 512], P('dp', 'tile'), may hold values from -6 to 6
Outputs:
- output: bfloat16 [4, 1024, 512], P('dp', 'tile')
- input_grad: float32 [4, 1024, 512], P('dp', 'tile')
- grad_down_first: float32 [3, 3, 32, 3], replicated
- grad_down_second: float32 [3, 3, 64, 32], replicated
- grad_down_third: float32 [3, 3, 128, 64], replicated
- grad_down_fourth: float32 [3, 3, 256, 128], replicated
- grad_down_fifth: float32 [3, 3, 512, 256], replicated
- grad_up_fourth: float32 [3, 3, 256, 512], replicated
- grad_up_third: float32 [3, 3, 128, 256], replicated
- grad_up_second: float32 [3, 3, 64, 128], replicated
- grad_up_first: float32 [3, 3, 32, 64], replicated
- grad_roi_proj: float32 [128, 512], replicated
- grad_gain_attn: float32 [512], replicated
- grad_query: float32 [512, 512], replicated
- grad_key: float32 [512, 512], replicated
- grad_value: float32 [512, 512], replicated
- grad_output: float32 [512, 512], replicated
- grad_bias_table: float32 [8, 96], replicated
- grad_gain_ffn: float32 [512], replicated
- grad_ffn_in: float32 [512, 2048], replicated
- grad_ffn_out: float32 [2048, 512], replicated
Inputs may be any that keep to these rules, and one draw needn't show every extreme that they name: `token_boxes`: each box has x1 - x0 and y1 - y0 at least 2, x1 <= 512, and its rows y0 to y1 - 1 inside one block of 16 pixel rows. In each row, of the boxes of the 128 tokens of one device at most 64 fall in any one block, and every device's tokens have exactly 64 in one common block, which so holds 512 boxes; no block holds more. `segment_ids`: never falling along a row; each row has two documents, one of fewer than 64 tokens at its start or its end.
All inputs are finite; a program needn't handle non-finite values.
Results may differ from a plain program's by a relative error of at most 0.018.
Values may be sent and summed in bfloat16 or wider, within the bound.
No kernel may reach another device: no remote copies, remote signals or barrier semaphores. Data moves between devices by JAX's collectives and lax.ppermute only.
A program may use at most 192 MiB of HBM per device.

v0:
```python
import math

import jax
import jax.numpy as jnp
from jax import lax
from jax.sharding import PartitionSpec as P

HEADS = 8
HD = 64
NB = 32


eps = 1e-06
bounds = (12, 16, 23, 32, 46, 64, 91)
highest = lax.Precision.HIGHEST
neg_large = -1000000000.0


def with_halo(block, sides, width):
    for axis, dim in sides:
        count = lax.axis_size(axis)
        forward = [(i, i + 1) for i in range(count - 1)]
        backward = [(target, source) for source, target in forward]
        low = lax.ppermute(
            lax.slice_in_dim(block, block.shape[dim] - width, None, axis=dim), axis, forward
        )
        high = lax.ppermute(lax.slice_in_dim(block, 0, width, axis=dim), axis, backward)
        block = jnp.concatenate([low, block, high], axis=dim)
    return block


def split_up(array, dim, peers):
    before, after = (array.shape[:dim], array.shape[dim + 1 :])
    return jnp.moveaxis(array.reshape(*before, peers, -1, *after), dim, 0)


def sent_and_summed(array, axis, dim):
    peers = lax.axis_size(axis)
    pieces = lax.all_to_all(split_up(array, dim, peers), axis, 0, 0, tiled=True)
    return jnp.sum(pieces.astype(jnp.float32), axis=0)


def bucket_of(signed_gap):
    distance = jnp.abs(signed_gap)
    far_steps = jnp.zeros_like(distance)
    for threshold in bounds:
        far_steps = far_steps + (distance >= threshold).astype(jnp.int32)
    nearness = jnp.where(distance < 8, distance, 8 + far_steps)
    return nearness + jnp.where(signed_gap > 0, 16, 0).astype(jnp.int32)


def rms_scale(value, gain):
    return value * lax.rsqrt(jnp.mean(value * value, axis=-1, keepdims=True) + eps) * gain


def gelu_back(pre_act, upstream):
    return jax.vjp(jax.nn.gelu, pre_act)[1](upstream)[0]


def pool_half(value):
    chans, rows_in, cols_in = value.shape
    return jnp.mean(value.reshape(chans, rows_in // 2, 2, cols_in // 2, 2), axis=(2, 4))


def pool_back(upstream):
    return jnp.repeat(jnp.repeat(upstream, 2, axis=1), 2, axis=2) * 0.25


def double_up(value):
    return jnp.repeat(jnp.repeat(value, 2, axis=1), 2, axis=2)


def double_back(upstream):
    chans, rows_in, cols_in = upstream.shape
    return jnp.sum(upstream.reshape(chans, rows_in // 2, 2, cols_in // 2, 2), axis=(2, 4))


def conv_apply(padded, weight):
    rows_out = padded.shape[1] - 2
    cols_out = padded.shape[2] - 2
    total = jnp.zeros((weight.shape[2], rows_out, cols_out), jnp.float32)
    for row_off in range(3):
        for col_off in range(3):
            window = padded[:, row_off : row_off + rows_out, col_off : col_off + cols_out]
            total = total + jnp.einsum(
                "oc,chw->ohw", weight[row_off, col_off], window, preferred_element_type=jnp.float32
            )
    return total


def conv_forward(value, weight):
    padded = with_halo(value, (("tile", 1),), 1)
    padded = jnp.pad(padded, ((0, 0), (0, 0), (1, 1)))
    return (conv_apply(padded, weight), padded)


def conv_weight_grad(padded, grad_low):
    rows_out = grad_low.shape[1]
    cols_out = grad_low.shape[2]
    stacked = []
    for row_off in range(3):
        line_grads = []
        for col_off in range(3):
            window = padded[:, row_off : row_off + rows_out, col_off : col_off + cols_out]
            line_grads.append(
                jnp.einsum("ohw,chw->oc", grad_low, window, preferred_element_type=jnp.float32)
            )
        stacked.append(jnp.stack(line_grads))
    return jnp.stack(stacked)


def conv_input_grad(weight, grad_low):
    rows_out = grad_low.shape[1]
    cols_out = grad_low.shape[2]
    total = jnp.zeros((weight.shape[3], rows_out + 2, cols_out + 2), jnp.float32)
    for row_off in range(3):
        for col_off in range(3):
            term = jnp.einsum(
                "oc,ohw->chw",
                weight[row_off, col_off],
                grad_low,
                preferred_element_type=jnp.float32,
            )
            total = total + jnp.pad(term, ((0, 0), (row_off, 2 - row_off), (col_off, 2 - col_off)))
    inner_rows = total[:, :, 1:-1]
    rims = jnp.concatenate([inner_rows[:, :1], inner_rows[:, -1:]], axis=1)
    arrived = with_halo(rims.astype(jnp.bfloat16), (("tile", 1),), 1).astype(rims.dtype)
    middle = inner_rows[:, 1:-1]
    middle = middle.at[:, 0].add(arrived[:, 0])
    middle = middle.at[:, -1].add(arrived[:, 3])
    return middle


def block_scores(query_heads, key_heads, query_meta, key_meta, bias_table, score_scale):
    query_pos, query_cx, query_cy, query_seg = query_meta
    key_pos, key_cx, key_cy, key_seg = key_meta
    rel_bucket = bucket_of(key_pos[None, :] - query_pos[:, None])
    hor_bucket = bucket_of(key_cx[None, :] - query_cx[:, None]) + NB
    ver_bucket = bucket_of(key_cy[None, :] - query_cy[:, None]) + 2 * NB
    slot_ids = jnp.arange(3 * NB)
    one_hot = (
        (rel_bucket[..., None] == slot_ids)
        | (hor_bucket[..., None] == slot_ids)
        | (ver_bucket[..., None] == slot_ids)
    ).astype(jnp.bfloat16)
    scores = (
        jnp.einsum("hqd,hkd->hqk", query_heads, key_heads, preferred_element_type=jnp.float32)
        * score_scale
    )
    scores = scores + jnp.einsum(
        "qkn,hn->hqk", one_hot, bias_table, preferred_element_type=jnp.float32
    )
    allowed = query_seg[:, None] == key_seg[None, :]
    return (scores, allowed, one_hot)


def on_device(
    embeddings,
    page_images,
    token_boxes,
    segment_ids,
    down_first,
    down_second,
    down_third,
    down_fourth,
    down_fifth,
    up_fourth,
    up_third,
    up_second,
    up_first,
    roi_proj,
    gain_attn,
    w_query,
    w_key,
    w_value,
    w_output,
    bias_table,
    gain_ffn,
    ffn_in,
    ffn_out,
    cotangent,
):
    tok_rows = embeddings.shape[1]
    model_width = embeddings.shape[2]
    tile_rows = page_images.shape[2]
    my_tile = lax.axis_index("tile")
    tile_count = lax.axis_size("tile")
    pair_most = max(2, 4 * tok_rows // tile_count)
    own_most = tile_count * pair_most
    score_scale = HD ** (-0.5)
    page_tile = page_images[0]
    pre_zero, pad_zero = conv_forward(page_tile, down_first)
    enc_zero = jax.nn.gelu(pre_zero)
    pre_one, pad_one = conv_forward(pool_half(enc_zero).astype(jnp.bfloat16), down_second)
    enc_one = jax.nn.gelu(pre_one)
    pre_two, pad_two = conv_forward(pool_half(enc_one).astype(jnp.bfloat16), down_third)
    enc_two = jax.nn.gelu(pre_two)
    pre_three, pad_three = conv_forward(pool_half(enc_two).astype(jnp.bfloat16), down_fourth)
    enc_three = jax.nn.gelu(pre_three)
    pre_four, pad_four = conv_forward(pool_half(enc_three).astype(jnp.bfloat16), down_fifth)
    enc_four = jax.nn.gelu(pre_four)
    pre_up_three, pad_up_three = conv_forward(double_up(enc_four).astype(jnp.bfloat16), up_fourth)
    dec_three = jax.nn.gelu(pre_up_three) + enc_three
    pre_up_two, pad_up_two = conv_forward(double_up(dec_three).astype(jnp.bfloat16), up_third)
    dec_two = jax.nn.gelu(pre_up_two) + enc_two
    pre_up_one, pad_up_one = conv_forward(double_up(dec_two).astype(jnp.bfloat16), up_second)
    dec_one = jax.nn.gelu(pre_up_one) + enc_one
    pre_up_zero, pad_up_zero = conv_forward(double_up(dec_one).astype(jnp.bfloat16), up_first)
    features = (jax.nn.gelu(pre_up_zero) + enc_zero).astype(jnp.bfloat16)
    all_boxes, all_seg = (
        lax.all_gather(token_boxes, "tile", axis=2, tiled=True),
        lax.all_gather(segment_ids, "tile", axis=1, tiled=True),
    )
    left_all = all_boxes[0, 0]
    top_all = all_boxes[1, 0]
    right_all = all_boxes[2, 0]
    bottom_all = all_boxes[3, 0]
    seg_all = all_seg[0]
    seq_all = seg_all.shape[0]
    is_owned = top_all // tile_rows == my_tile
    chosen = jnp.nonzero(is_owned, size=own_most, fill_value=0)[0]
    filled = (jnp.arange(own_most) < jnp.sum(is_owned.astype(jnp.int32))).astype(jnp.float32)
    sel_left = left_all[chosen]
    sel_top = top_all[chosen]
    sel_right = right_all[chosen]
    sel_bottom = bottom_all[chosen]
    mid_row = (sel_top + sel_bottom) // 2
    mid_col = (sel_left + sel_right) // 2
    row_ids = (my_tile * tile_rows + jnp.arange(tile_rows))[None, :]
    col_ids = jnp.arange(page_tile.shape[2])[None, :]
    row_mask = jnp.stack(
        [
            (row_ids >= sel_top[:, None]) & (row_ids < mid_row[:, None]),
            (row_ids >= mid_row[:, None]) & (row_ids < sel_bottom[:, None]),
        ],
        axis=1,
    ).astype(jnp.float32)
    col_mask = jnp.stack(
        [
            (col_ids >= sel_left[:, None]) & (col_ids < mid_col[:, None]),
            (col_ids >= mid_col[:, None]) & (col_ids < sel_right[:, None]),
        ],
        axis=1,
    ).astype(jnp.float32)
    heights = jnp.stack([mid_row - sel_top, sel_bottom - mid_row], axis=1).astype(jnp.float32)
    widths_box = jnp.stack([mid_col - sel_left, sel_right - mid_col], axis=1).astype(jnp.float32)
    band_area = heights[:, :, None] * widths_box[:, None, :]
    partial_cols = jnp.einsum(
        "obx,cyx->obcy", col_mask.astype(jnp.bfloat16), features, preferred_element_type=jnp.float32
    )
    totals = jnp.einsum("oay,obcy->oabc", row_mask, partial_cols, precision=highest)
    pooled_own = totals / band_area[..., None] * filled[:, None, None, None]
    pool_width = pooled_own.shape[1] * pooled_own.shape[2] * pooled_own.shape[3]
    pool_flat = pooled_own.reshape(own_most, pool_width)
    dense_rows = jnp.zeros((seq_all, pool_width), jnp.float32).at[chosen].add(pool_flat)
    pooled = sent_and_summed(dense_rows.astype(jnp.bfloat16), "tile", 0)
    pooled_low = pooled.astype(jnp.bfloat16)
    residual = embeddings[0].astype(jnp.float32) + jnp.dot(
        pooled_low, roi_proj, preferred_element_type=jnp.float32
    )
    gain_one = gain_attn.astype(jnp.float32)
    normed_low = rms_scale(residual, gain_one).astype(jnp.bfloat16)
    query_low = jnp.dot(normed_low, w_query, preferred_element_type=jnp.float32).astype(
        jnp.bfloat16
    )
    key_low = jnp.dot(normed_low, w_key, preferred_element_type=jnp.float32).astype(jnp.bfloat16)
    value_low = jnp.dot(normed_low, w_value, preferred_element_type=jnp.float32).astype(
        jnp.bfloat16
    )

    def to_heads(flat_rows):
        return flat_rows.reshape(tok_rows, HEADS, HD).transpose(1, 0, 2)

    def from_heads(head_rows):
        return head_rows.transpose(1, 0, 2).reshape(tok_rows, model_width)

    query_heads = to_heads(query_low)
    own_keys = to_heads(key_low)
    own_values = to_heads(value_low)
    key_all, value_all = (
        lax.all_gather(own_keys, "tile", axis=1, tiled=True),
        lax.all_gather(own_values, "tile", axis=1, tiled=True),
    )
    center_x = (left_all + right_all) // 2
    center_y = (top_all + bottom_all) // 2
    key_meta = (jnp.arange(seq_all), center_x, center_y, seg_all)
    first_tok = my_tile * tok_rows
    query_meta = tuple(
        (lax.dynamic_slice_in_dim(member, first_tok, tok_rows, 0) for member in key_meta)
    )
    key_block = math.gcd(seq_all, 1024)
    block_count = seq_all // key_block

    def key_slice(block_id):
        first_key = block_id * key_block
        keys_blk = lax.dynamic_slice_in_dim(key_all, first_key, key_block, 1)
        values_blk = lax.dynamic_slice_in_dim(value_all, first_key, key_block, 1)
        meta_blk = tuple(
            (lax.dynamic_slice_in_dim(member, first_key, key_block, 0) for member in key_meta)
        )
        return (keys_blk, values_blk, meta_blk)

    def stats_step(running, block_id):
        run_max, run_sum = running
        keys_blk, values_blk, meta_blk = key_slice(block_id)
        scores, allowed, one_hot = block_scores(
            query_heads, keys_blk, query_meta, meta_blk, bias_table, score_scale
        )
        scores = jnp.where(allowed[None], scores, neg_large)
        new_max = jnp.maximum(run_max, jnp.max(scores, axis=-1))
        run_sum = run_sum * jnp.exp(run_max - new_max) + jnp.sum(
            jnp.exp(scores - new_max[..., None]), axis=-1
        )
        return ((new_max, run_sum), None)

    start_stats = (
        jnp.full((HEADS, tok_rows), neg_large, jnp.float32),
        jnp.zeros((HEADS, tok_rows), jnp.float32),
    )
    (run_max, run_sum), _ = lax.scan(stats_step, start_stats, jnp.arange(block_count))
    log_total = run_max + jnp.log(run_sum)

    def out_step(attn_acc, block_id):
        keys_blk, values_blk, meta_blk = key_slice(block_id)
        scores, allowed, one_hot = block_scores(
            query_heads, keys_blk, query_meta, meta_blk, bias_table, score_scale
        )
        attn_prob = jnp.where(allowed[None], jnp.exp(scores - log_total[..., None]), 0.0)
        attn_acc = attn_acc + jnp.einsum(
            "hqk,hkd->hqd",
            attn_prob.astype(jnp.bfloat16),
            values_blk,
            preferred_element_type=jnp.float32,
        )
        return (attn_acc, None)

    attn_heads, _ = lax.scan(
        out_step, jnp.zeros((HEADS, tok_rows, HD), jnp.float32), jnp.arange(block_count)
    )
    attn_low = from_heads(attn_heads).astype(jnp.bfloat16)
    mixed_rows = residual + jnp.dot(attn_low, w_output, preferred_element_type=jnp.float32)
    gain_two = gain_ffn.astype(jnp.float32)
    ffn_low = rms_scale(mixed_rows, gain_two).astype(jnp.bfloat16)
    pre_ffn = jnp.dot(ffn_low, ffn_in, preferred_element_type=jnp.float32)
    act_low = jax.nn.gelu(pre_ffn).astype(jnp.bfloat16)
    result_rows = mixed_rows + jnp.dot(act_low, ffn_out, preferred_element_type=jnp.float32)
    upstream = cotangent[0]
    grad_ffn_out = jnp.einsum("tf,td->fd", act_low, upstream, preferred_element_type=jnp.float32)
    d_act = jnp.einsum("td,fd->tf", upstream, ffn_out, preferred_element_type=jnp.float32)
    d_pre = gelu_back(pre_ffn, d_act).astype(jnp.bfloat16)
    grad_ffn_in = jnp.einsum("td,tf->df", ffn_low, d_pre, preferred_element_type=jnp.float32)
    d_ffn_norm = jnp.einsum("tf,df->td", d_pre, ffn_in, preferred_element_type=jnp.float32)
    d_mixed_norm, grad_gain_ffn = jax.vjp(rms_scale, mixed_rows, gain_two)[1](d_ffn_norm)
    d_mixed = upstream.astype(jnp.float32) + d_mixed_norm
    d_mixed_low = d_mixed.astype(jnp.bfloat16)
    grad_output = jnp.einsum("tc,td->cd", attn_low, d_mixed_low, preferred_element_type=jnp.float32)
    d_attn = jnp.einsum(
        "td,cd->tc", d_mixed_low, w_output, preferred_element_type=jnp.float32
    ).astype(jnp.bfloat16)
    dout_heads = to_heads(d_attn)
    row_delta = jnp.sum(dout_heads.astype(jnp.float32) * attn_heads, axis=-1)

    def back_step(running, block_id):
        keys_blk, values_blk, meta_blk = key_slice(block_id)
        scores, allowed, one_hot = block_scores(
            query_heads, keys_blk, query_meta, meta_blk, bias_table, score_scale
        )
        attn_prob = jnp.where(allowed[None], jnp.exp(scores - log_total[..., None]), 0.0)
        d_prob = jnp.einsum(
            "hqd,hkd->hqk", dout_heads, values_blk, preferred_element_type=jnp.float32
        )
        d_score = (attn_prob * (d_prob - row_delta[..., None])).astype(jnp.bfloat16)
        query_acc = running[0] + jnp.einsum(
            "hqk,hkd->hqd", d_score, keys_blk, preferred_element_type=jnp.float32
        )
        table_acc = running[1] + jnp.einsum(
            "hqk,qkn->hn", d_score, one_hot, preferred_element_type=jnp.float32
        )
        first_key = block_id * key_block
        key_part = (
            jnp.einsum("hqk,hqd->hkd", d_score, query_heads, preferred_element_type=jnp.float32)
            * score_scale
        )
        value_part = jnp.einsum(
            "hqk,hqd->hkd",
            attn_prob.astype(jnp.bfloat16),
            dout_heads,
            preferred_element_type=jnp.float32,
        )
        key_acc = lax.dynamic_update_slice_in_dim(running[2], key_part, first_key, 1)
        value_acc = lax.dynamic_update_slice_in_dim(running[3], value_part, first_key, 1)
        return ((query_acc, table_acc, key_acc, value_acc), None)

    start_back = (
        jnp.zeros((HEADS, tok_rows, HD), jnp.float32),
        jnp.zeros((HEADS, 3 * NB), jnp.float32),
    )
    start_back = start_back + (
        jnp.zeros((HEADS, seq_all, HD), jnp.float32),
        jnp.zeros((HEADS, seq_all, HD), jnp.float32),
    )
    back_out, _ = lax.scan(back_step, start_back, jnp.arange(block_count))
    query_acc = back_out[0]
    grad_bias_table = back_out[1]
    key_grad, value_grad = (
        lax.psum_scatter(back_out[2], "tile", scatter_dimension=1, tiled=True),
        lax.psum_scatter(back_out[3], "tile", scatter_dimension=1, tiled=True),
    )
    dq_low = from_heads(query_acc * score_scale).astype(jnp.bfloat16)
    dk_low = from_heads(key_grad).astype(jnp.bfloat16)
    dv_low = from_heads(value_grad).astype(jnp.bfloat16)
    grad_query = jnp.einsum("td,te->de", normed_low, dq_low, preferred_element_type=jnp.float32)
    grad_key = jnp.einsum("td,te->de", normed_low, dk_low, preferred_element_type=jnp.float32)
    grad_value = jnp.einsum("td,te->de", normed_low, dv_low, preferred_element_type=jnp.float32)
    d_normed = (
        jnp.einsum("te,de->td", dq_low, w_query, preferred_element_type=jnp.float32)
        + jnp.einsum("te,de->td", dk_low, w_key, preferred_element_type=jnp.float32)
        + jnp.einsum("te,de->td", dv_low, w_value, preferred_element_type=jnp.float32)
    )
    d_resid_norm, grad_gain_attn = jax.vjp(rms_scale, residual, gain_one)[1](d_normed)
    d_residual = d_mixed + d_resid_norm
    d_resid_low = d_residual.astype(jnp.bfloat16)
    grad_roi_proj = jnp.einsum(
        "tp,td->pd", pooled_low, d_resid_low, preferred_element_type=jnp.float32
    )
    d_pooled = jnp.einsum("td,pd->tp", d_resid_low, roi_proj, preferred_element_type=jnp.float32)
    pooled_grads = lax.all_gather(d_pooled.astype(jnp.bfloat16), "tile", axis=0, tiled=True).astype(
        d_pooled.dtype
    )
    picked_rows = pooled_grads[chosen]
    picked = picked_rows.reshape(own_most, 2, 2, pool_width // 4)
    picked = picked * (filled[:, None, None, None] / band_area[..., None])
    over_rows = jnp.einsum("oabc,oay->obcy", picked, row_mask, precision=highest)
    d_features = jnp.einsum("obcy,obx->cyx", over_rows, col_mask, precision=highest)
    grad_low = gelu_back(pre_up_zero, d_features).astype(jnp.bfloat16)
    grad_up_first = conv_weight_grad(pad_up_zero, grad_low)
    d_dec_one = double_back(conv_input_grad(up_first, grad_low))
    d_enc_zero = d_features
    grad_low = gelu_back(pre_up_one, d_dec_one).astype(jnp.bfloat16)
    grad_up_second = conv_weight_grad(pad_up_one, grad_low)
    d_dec_two = double_back(conv_input_grad(up_second, grad_low))
    d_enc_one = d_dec_one
    grad_low = gelu_back(pre_up_two, d_dec_two).astype(jnp.bfloat16)
    grad_up_third = conv_weight_grad(pad_up_two, grad_low)
    d_dec_three = double_back(conv_input_grad(up_third, grad_low))
    d_enc_two = d_dec_two
    grad_low = gelu_back(pre_up_three, d_dec_three).astype(jnp.bfloat16)
    grad_up_fourth = conv_weight_grad(pad_up_three, grad_low)
    d_enc_four = double_back(conv_input_grad(up_fourth, grad_low))
    d_enc_three = d_dec_three
    grad_low = gelu_back(pre_four, d_enc_four).astype(jnp.bfloat16)
    grad_down_fifth = conv_weight_grad(pad_four, grad_low)
    d_enc_three = d_enc_three + pool_back(conv_input_grad(down_fifth, grad_low))
    grad_low = gelu_back(pre_three, d_enc_three).astype(jnp.bfloat16)
    grad_down_fourth = conv_weight_grad(pad_three, grad_low)
    d_enc_two = d_enc_two + pool_back(conv_input_grad(down_fourth, grad_low))
    grad_low = gelu_back(pre_two, d_enc_two).astype(jnp.bfloat16)
    grad_down_third = conv_weight_grad(pad_two, grad_low)
    d_enc_one = d_enc_one + pool_back(conv_input_grad(down_third, grad_low))
    grad_low = gelu_back(pre_one, d_enc_one).astype(jnp.bfloat16)
    grad_down_second = conv_weight_grad(pad_one, grad_low)
    d_enc_zero = d_enc_zero + pool_back(conv_input_grad(down_second, grad_low))
    grad_low = gelu_back(pre_zero, d_enc_zero).astype(jnp.bfloat16)
    grad_down_first = conv_weight_grad(pad_zero, grad_low)
    local_grads = (
        grad_down_first,
        grad_down_second,
        grad_down_third,
        grad_down_fourth,
        grad_down_fifth,
        grad_up_fourth,
        grad_up_third,
        grad_up_second,
        grad_up_first,
        grad_roi_proj,
        grad_gain_attn,
        grad_query,
        grad_key,
        grad_value,
        grad_output,
        grad_bias_table,
        grad_gain_ffn,
        grad_ffn_in,
        grad_ffn_out,
    )
    flat_grads = jnp.concatenate([member.reshape(-1) for member in local_grads])
    device_total = lax.axis_size("dp") * lax.axis_size("tile")
    flat_len = flat_grads.shape[0]
    padded_len = -(-flat_len // device_total) * device_total
    flat_grads = jnp.pad(flat_grads, (0, padded_len - flat_len))
    grad_shard = lax.psum_scatter(flat_grads, ("dp", "tile"), scatter_dimension=0, tiled=True)
    grad_whole = lax.all_gather(
        grad_shard.astype(jnp.bfloat16), ("dp", "tile"), axis=0, tiled=True
    ).astype(grad_shard.dtype)
    summed = []
    cursor = 0
    for member in local_grads:
        length = member.size
        summed.append(grad_whole[cursor : cursor + length].reshape(member.shape))
        cursor = cursor + length
    return (
        result_rows.astype(jnp.bfloat16)[None],
        d_residual[None],
        summed[0],
        summed[1],
        summed[2],
        summed[3],
        summed[4],
        summed[5],
        summed[6],
        summed[7],
        summed[8],
        summed[9],
        summed[10],
        summed[11],
        summed[12],
        summed[13],
        summed[14],
        summed[15],
        summed[16],
        summed[17],
        summed[18],
    )


def solution(mesh):
    return jax.shard_map(
        on_device,
        mesh=mesh,
        in_specs=(
            P("dp", "tile", None),
            P("dp", None, "tile", None),
            P(None, "dp", "tile"),
            P("dp", "tile"),
            P(),
            P(),
            P(),
            P(),
            P(),
            P(),
            P(),
            P(),
            P(),
            P(),
            P(),
            P(),
            P(),
            P(),
            P(),
            P(),
            P(),
            P(),
            P(),
            P("dp", "tile", None),
        ),
        out_specs=(
            P("dp", "tile", None),
            P("dp", "tile", None),
            P(),
            P(),
            P(),
            P(),
            P(),
            P(),
            P(),
            P(),
            P(),
            P(),
            P(),
            P(),
            P(),
            P(),
            P(),
            P(),
            P(),
            P(),
            P(),
        ),
        check_vma=False,
    )
```

profile of v0, /device:TPU:0, one launch (start us, length us, event | category | flops | bytes accessed | tf_op | source)
XLA Modules:
  0.0 1675.4 jit_solution(6028506707181272142)
XLA Ops:
  8.2 4.9 collective-permute-start
  14.4 22.3 %all_gather.20 = s32[4,1,1024]{2,1,0:T(1,128)S(1)} all-gather(s32[4,1,128]{2,1,0:T(1,128)} %param.58), channel_id=1, replica_groups=mesh['dp'=4,'tile'=8] {'tile'}, dimensions={2}, use_global_device_ids=true | all-gather | bytes 18432 | tf_op jit(solution)/shard_map/all_gather | solution.py:211
  37.3 7.6 scatter_custom_fusion
  66.0 6.0 reduce_sum.209
  134.4 4.8 collective-permute-start.10
  154.4 5.5 collective-permute-done.13
  170.0 12.1 collective-permute-start.15
  220.3 8.4 copy.281
  228.6 7.5 fusion.34
  240.0 5.0 scatter_custom_fusion.1
  266.8 15.7 fusion.4
  282.5 5.4 copy.288
  287.8 17.9 %all_gather.21 = s32[1,1024]{1,0:T(1,128)S(1)} all-gather(s32[1,128]{1,0:T(1,128)S(1)} %copy-done.165), channel_id=1, replica_groups=mesh['dp'=4,'tile'=8] {'tile'}, dimensions={1}, use_global_device_ids=true | all-gather | bytes 4608 | tf_op jit(solution)/shard_map/all_gather | solution.py:212
  320.8 25.6 %all-gather.5.cloned.1.call-done = bf16[8,1024,64]{1,2,0:T(8,128)(2,1)} async-done(((bf16[8,128,64]{1,2,0:T(8,128)(2,1)}), bf16[8,1024,64]{1,2,0:T(8,128)(2,1)}) %all-gather.5.cloned.1.call-update) | async-done | bytes 1048592 | tf_op jit(solution)/shard_map/all_gather | solution.py:282
  378.2 14.5 fusion.55
  403.1 24.2 %reduce-scatter.5.cloned.1.call-done = f32[8,128,64]{1,2,0:T(8,128)} async-done(((f32[8,1024,64]{1,2,0:T(8,128)}), f32[8,128,64]{1,2,0:T(8,128)}) %reduce-scatter.5.cloned.1.call-update) | async-done | bytes 262160 | tf_op jit(solution)/shard_map/reduce_scatter | solution.py:407
  429.5 69.0 %reduce-scatter.3.cloned.1.call-done = f32[8,128,64]{1,2,0:T(8,128)} async-done(((f32[8,1024,64]{1,2,0:T(8,128)}), f32[8,128,64]{1,2,0:T(8,128)}) %reduce-scatter.3.cloned.1.call-update) | async-done | bytes 262160 | tf_op jit(solution)/shard_map/reduce_scatter | solution.py:406
  504.6 30.8 %all_gather.25 = bf16[1024,128]{1,0:T(8,128)(2,1)S(1)} all-gather(bf16[128,128]{1,0:T(8,128)(2,1)S(1)} %convolution_convert_fusion.4), channel_id=1, replica_groups=mesh['dp'=4,'tile'=8] {'tile'}, dimensions={0}, use_global_device_ids=true | all-gather | bytes 294912 | tf_op jit(solution)/shard_map/all_gather | solution.py:427
  542.1 12.1 fusion.71
  565.5 5.9 fusion.787
  585.3 6.8 reduce_sum.222
  735.7 218.0 %concatenate.199 = f32[6347360]{0:T(1024)} concatenate(f32[864]{0:T(1024)S(1)} %reshape.1759, f32[18432]{0:T(1024)} %reshape.1760, f32[73728]{0:T(1024)S(1)} %copy-done.77, f32[294912]{0:T(1024)S(1)} %bitcast.1470, f32[1179648]{0:T(1024)} %bitcast.1460, f32[1179648]{0:T(1024)} %bitcast.1459, f32[294912]{0:T(1024)S(1)} %bitcast.1469, f32[73728]{0:T(1024)S(1)} %bitcast.1493, ...), dimensions={0} | concatenate | bytes 50778880 | tf_op jit(solution)/shard_map/concatenate | solution.py:486
  953.7 407.2 %all-reduce.87 = bf16[6347360]{0:T(1024)(128)(2,1)} all-reduce(f32[6347360]{0:T(1024)} %concatenate.199), channel_id=4, replica_groups=mesh['dp'=4,'tile'=8] {'dp','tile'}, use_global_device_ids=true, to_apply=%region_29.30.clone | all-reduce | flops 6347360 | bytes 38084160
  1362.2 4.8 broadcast.1623
  1367.0 7.3 dynamic-update-slice.46
  1378.5 228.2 %all-reduce.86.cloned.1.call-done = bf16[6347360]{0:T(1024)(128)(2,1)} async-done(((bf16[6347360]{0:T(1024)(128)(2,1)}), bf16[6347360]{0:T(1024)(128)(2,1)}) %all-reduce.86.cloned.1.call-update) | async-done | bytes 12694736
  1630.5 6.5 fusion.796
  1637.0 6.2 reshape.1781
  1643.2 7.7 fusion.790
  1650.9 4.9 reshape.1792
  1655.8 4.9 reshape.1791
  1660.7 6.4 reshape.1780
  (941 shorter events, 442.4 us)
Async XLA Ops:
  8.2 50.3 %collective-permute-start = (bf16[3,1,512]{2,0,1:T(4,128)(2,1)S(1)}, bf16[3,1,512]{2,0,1:T(4,128)(2,1)S(1)}, u32[]{:S(2)}, u32[]{:S(2)}) collective-permute-start(bf16[3,1,512]{2,0,1:T(4,128)(2,1)S(1)} %get-tuple-element.491), channel_id=1, source_target_pairs={{0,1},{1,2},{2,3},{3,4},{4,5},{5,6},{6,7},{8,9},{9,10},{10,11},{11... | collective-permute-start | bytes 9224 | tf_op jit(solution)/shard_map/ppermute | solution.py:24
  13.1 45.4 %collective-permute-start.1 = (bf16[3,1,512]{2,0,1:T(4,128)(2,1)S(1)}, bf16[3,1,512]{2,0,1:T(4,128)(2,1)S(1)}, u32[]{:S(2)}, u32[]{:S(2)}) collective-permute-start(bf16[3,1,512]{2,0,1:T(4,128)(2,1)S(1)} %get-tuple-element.492), channel_id=1, source_target_pairs={{1,0},{2,1},{3,2},{4,3},{5,4},{6,5},{7,6},{9,8},{10,9},{11,10},{12... | collective-permute-start | bytes 9224 | tf_op jit(solution)/shard_map/ppermute | solution.py:27
  72.3 7.6 collective-permute-start.2
  73.6 6.3 collective-permute-start.3
  102.7 7.1 collective-permute-start.6
  133.1 6.4 collective-permute-start.11
  134.4 6.7 collective-permute-start.10
  147.4 6.7 collective-permute-start.12
  152.5 7.4 collective-permute-start.13
  165.2 18.1 %collective-permute-start.14 = (bf16[128,1,256]{2,0,1:T(8,128)(2,1)S(1)}, bf16[128,1,256]{2,0,1:T(8,128)(2,1)S(1)}, u32[]{:S(2)}, u32[]{:S(2)}) collective-permute-start(bf16[128,1,256]{2,0,1:T(8,128)(2,1)S(1)} %get-tuple-element.471), channel_id=1, source_target_pairs={{0,1},{1,2},{2,3},{3,4},{4,5},{5,6},{6,7},{8,9},{9,10},{10,11},{11... | collective-permute-start | bytes 196616 | tf_op jit(solution)/shard_map/ppermute | solution.py:24
  170.0 13.9 collective-permute-start.15
  202.0 7.5 collective-permute-start.16
  206.6 6.3 collective-permute-start.17
  246.8 12.6 all-to-all-start
  251.1 62.8 %all-gather.3.cloned.1.call-start = ((), (), s32[]{:S(2)}) async-start(), calls=%async_computation.3 | async-start | bytes 1179648 | tf_op jit(solution)/shard_map/all_gather | solution.py:281
  266.7 79.6 %all-gather.5.cloned.1.call-start = ((), (), s32[]{:S(2)}) async-start(), calls=%async_computation.4 | async-start | bytes 1179648 | tf_op jit(solution)/shard_map/all_gather | solution.py:282
  309.4 117.9 %reduce-scatter.5.cloned.1.call-start = ((), (), s32[]{:S(2)}) async-start(), calls=%async_computation.6 | async-start | bytes 2359296 | tf_op jit(solution)/shard_map/reduce_scatter | solution.py:407
  360.2 138.4 %reduce-scatter.3.cloned.1.call-start = ((), (), s32[]{:S(2)}) async-start(), calls=%async_computation.5 | async-start | bytes 2359296 | tf_op jit(solution)/shard_map/reduce_scatter | solution.py:406
  373.6 1233.0 %all-reduce.86.cloned.1.call-start = ((), (), s32[]{:S(2)}) async-start(), calls=%async_computation.7 | async-start | bytes 25391104
  572.1 7.2 collective-permute-start.18
  574.0 6.5 collective-permute-start.19
  600.8 7.4 collective-permute-start.20
  604.1 6.2 collective-permute-start.21
  616.9 6.1 collective-permute-start.22
  620.8 6.2 collective-permute-start.23
  640.4 10.3 collective-permute-start.24
  643.7 6.9 collective-permute-start.25
  662.9 12.6 collective-permute-start.26
  667.4 8.1 collective-permute-start.27
  678.6 7.5 collective-permute-start.28
  692.6 7.6 collective-permute-start.30
  712.1 7.1 collective-permute-start.32
  (175 other events, 1975.2 us)
Sparse Core Ops, SparseCore 0:
  266.8 37.8 all-gather.2
  309.5 36.7 all-gather.4
  360.3 66.8 reduce-scatter.4
  431.2 67.3 reduce-scatter.2
  1374.5 232.1 all-reduce.85
where the time goes:
time: 1700 us; the launch traced here: 1680 us
  blocking collectives  478 us (28%)
  local copies, waits for them, and re-layouts  408 us (24%)
  waiting for transfers between devices  387 us (23%)
  matrix products  202 us (12%)
  starting transfers between devices  108 us (6%)
  other arithmetic  72.9 us (4%)
  between operations  18.9 us (1%)
    unnamed x1, blocking collectives  407 us
    unnamed x6, waiting for transfers between devices  228 us
    concatenate x1, local copies, waits for them, and re-layouts, on_device(): flat_grads = jnp.concatenate([member.reshape(-1) for member in local_grads])  218 us
    ppermute x17, starting transfers between devices, with_halo(): lax.ppermute(lax.slice_in_dim(block, block.shape[dim] - width, None, axis...  69.4 us
    reduce_scatter x1, waiting for transfers between devices, on_device(): lax.psum_scatter(back_out[2], 'tile', scatter_dimension=1, tiled=True)  69 us
    unnamed x353, local copies, waits for them, and re-layouts  48.5 us
    dot_general x81, matrix products, conv_apply(): jnp.einsum('oc,chw->ohw', weight[row_off, col_off], window, preferred_ele...  45.7 us
  transfers between devices with their start and end apart: 40, of which 20 were waited for; matrix products, arithmetic and copies ran while one was open for 8% of the time, Pallas kernels for 0%

commit v1 on v0

v1 whole, which is shorter than its diff:
```python
import functools
import math

import jax
import jax.numpy as jnp
from jax import lax
from jax.experimental import pallas as pl
from jax.experimental.pallas import tpu as pltpu
from jax.sharding import Mesh
from jax.sharding import PartitionSpec as P

HEADS = 8
HD = 64
NB = 32

eps = 1e-06
bounds = (12, 16, 23, 32, 46, 64, 91)
neg_large = -1000000000.0
HOPS = (("core", 1), ("x", 1), ("tile", 1), ("tile", 4), ("tile", 2))
PAGES = ("x", "core")
f32 = jnp.float32
bf16 = jnp.bfloat16
gelu_scale = math.sqrt(2.0 / math.pi)
VMEM_CAP = 28 * 1024 * 1024


def gelu_of(x):
    x = x.astype(f32)
    half = 0.5 * x
    inner = x * (gelu_scale + (gelu_scale * 0.044715) * (x * x))
    return half + half * jnp.tanh(inner)


def gelu_slope(x):
    x = x.astype(f32)
    sq = x * x
    bent = jnp.tanh(x * (gelu_scale + (gelu_scale * 0.044715) * sq))
    rise = gelu_scale + (3.0 * gelu_scale * 0.044715) * sq
    return 0.5 + 0.5 * bent + (0.5 * x) * (1.0 - bent * bent) * rise


def mm(a, b):
    return jnp.dot(a, b, preferred_element_type=f32)


def mm_tn(a, b):
    return lax.dot_general(a, b, (((0,), (0,)), ((), ())), preferred_element_type=f32)


def mm_nt(a, b):
    return lax.dot_general(a, b, (((1,), (1,)), ((), ())), preferred_element_type=f32)


def mm_fine(a, b):
    high = a.astype(bf16)
    low = (a - high.astype(f32)).astype(bf16)
    return mm(high, b) + mm(low, b)


def lane_ids(shape):
    return lax.broadcasted_iota(jnp.int32, shape, len(shape) - 1)


def row_ids_of(shape):
    return lax.broadcasted_iota(jnp.int32, shape, len(shape) - 2)


def halving(wide, value):
    hit = row_ids_of((wide, wide // 2)) >> 1 == lane_ids((wide, wide // 2))
    return jnp.where(hit, value, 0.0).astype(bf16)


def doubling(narrow):
    hit = row_ids_of((narrow, 2 * narrow)) == lane_ids((narrow, 2 * narrow)) >> 1
    return jnp.where(hit, 1.0, 0.0).astype(bf16)


def pair_halving(value):
    shape = (256, 128)
    source = row_ids_of(shape)
    target = lane_ids(shape)
    hit = source >> 1 == target
    return jnp.where(hit, value, 0.0).astype(bf16)


def side_doubling(side):
    shape = (128, 128)
    hit = row_ids_of(shape) == (lane_ids(shape) >> 1) + 64 * side
    return jnp.where(hit, 1.0, 0.0).astype(bf16)


def quad_map(coarse_lanes, coarse_width):
    shape = (coarse_lanes, 4 * coarse_lanes)
    fine = lane_ids((1, shape[1]))
    shift = coarse_width.bit_length() - 1
    home = (fine >> (shift + 2) << shift) + ((fine & (2 * coarse_width - 1)) >> 1)
    return jnp.where(row_ids_of(shape) == home, 1.0, 0.0).astype(bf16)


def masked(x, keep):
    return x * jnp.where(keep, 1.0, 0.0).astype(x.dtype)


def col_shift(x, step, width):
    if step == 0:
        return x
    lanes = x.shape[1]
    col = lane_ids((1, lanes)) & (width - 1)
    keep = col < width - 1 if step > 0 else col > 0
    return masked(pltpu.roll(x, -step % lanes, 1), keep)


def row_shift(x, step, width):
    if step == 0:
        return x
    lanes = x.shape[1]
    lane = lane_ids((1, lanes))
    keep = lane < lanes - width if step > 0 else lane >= width
    return masked(pltpu.roll(x, (-step * width) % lanes, 1), keep)


def stack_cols(x, width):
    return jnp.concatenate([col_shift(x, step, width) for step in (-1, 0, 1)], axis=0)


def row_ok(first_row, rows, width, low, high):
    row = (lane_ids((1, rows * width)) >> (width.bit_length() - 1)) + first_row
    return (row >= low) & (row < high)


def keep_rows(x, first_row, width, high):
    ok = row_ok(first_row, x.shape[1] // width, width, 0, high)
    return jnp.where(ok, x, 0.0)


def price(micros):
    return pl.CostEstimate(
        flops=int(micros * 5e8), transcendentals=0, bytes_accessed=int(micros * 2e6)
    )


class Fetched:
    def __init__(self, ref, copy):
        self.ref, self.copy, self.waited = ref, copy, False
        self.shape = ref.shape
        copy.start()

    def ready(self):
        if not self.waited:
            self.copy.wait()
            self.waited = True
        return self.ref

    def __getitem__(self, spot):
        return self.ready()[spot]


class Sent:
    def __init__(self, ref, copy):
        self.ref, self.copy, self.started = ref, copy, False
        self.shape = ref.shape

    def send(self):
        if not self.started:
            self.copy.start()
            self.started = True

    def __getitem__(self, spot):
        return self.ref[spot]

    def __setitem__(self, spot, value):
        self.ref[spot] = value


def in_hbm(array):
    return pltpu.with_memory_space_constraint(array, pltpu.HBM)


TOKEN = ((8, 128), f32)


def call(micros, body, outs, scratch, ids, arrays, after=(), late=(), sent=(), table=None):
    count = len(arrays)
    moved = [(arrays[n].shape, arrays[n].dtype) for n in late] + [outs[n] for n in sent]
    arrays = [in_hbm(array) if n in late else array for n, array in enumerate(arrays)]
    after = [in_hbm(token) for token in after]

    scalars = (ids,) if table is None else (ids, table)

    def ordered(*refs):
        refs, heads = refs[len(scalars) :], refs[: len(scalars)]
        ins = list(refs[:count])
        refs = refs[count + len(after) :]
        results = list(refs[: len(outs)])
        own = refs[len(outs) : len(outs) + len(scratch)]
        if moved:
            *stages, marks = refs[len(outs) + len(scratch) :]
        for k, n in enumerate(late):
            ins[n] = Fetched(stages[k], pltpu.make_async_copy(ins[n], stages[k], marks.at[k]))
        for k, n in enumerate(sent, len(late)):
            copy = pltpu.make_async_copy(stages[k], results[n], marks.at[k])
            results[n] = Sent(stages[k], copy)
        body(*heads, *ins, *results, *own)
        for n in late:
            ins[n].ready()
        for n in sent:
            results[n].send()
        for n in sent:
            results[n].copy.wait()

    def place(chosen, total):
        return [
            pl.BlockSpec(memory_space=pltpu.HBM if n in chosen else pltpu.VMEM) for n in range(total)
        ]

    return pl.pallas_call(
        ordered,
        cost_estimate=price(micros),
        out_shape=[
            pltpu.HBM(*out) if n in sent or out == TOKEN else jax.ShapeDtypeStruct(*out)
            for n, out in enumerate(outs)
        ],
        in_specs=[pl.BlockSpec(memory_space=pltpu.SMEM)] * len(scalars)
        + place(late, count)
        + [pl.BlockSpec(memory_space=pltpu.HBM) for _ in after],
        out_specs=place([n for n, out in enumerate(outs) if n in sent or out == TOKEN], len(outs)),
        scratch_shapes=[pltpu.VMEM(shape, kind) for shape, kind in scratch]
        + [pltpu.VMEM(shape, kind) for shape, kind in moved]
        + ([pltpu.SemaphoreType.DMA((len(moved),))] if moved else []),
        compiler_params=pltpu.CompilerParams(vmem_limit_bytes=VMEM_CAP),
    )(*scalars, *arrays, *after)


def lanes_at(start, size):
    return pl.ds(pl.multiple_of(start, 128), size)


def down_body(ids, pages, w_zero, w_one, w_two, pre_zero, pre_one, p_one, pre_two, p_two, p_three, page_own, page, cols, pool_one, stack_one, pool_two):
    tile, high, at = ids[0], ids[1], ids[4]
    page[...] = jnp.zeros_like(page)
    for side in range(-2, 3):
        block = at + side

        @pl.when((block >= 0) & (block < pages.shape[0]))
        def _(block=block, side=side):
            lines = pages[block, :, 0:1024].astype(f32)
            for g in range(8):
                first = (2 + side) * 8192 + 1024 * g
                for c in range(3):
                    page[c : c + 1, first : first + 1024] = lines[8 * c + g : 8 * c + g + 1, :]

    page_full = page[:, 11 * 512 : 69 * 512]
    page_own[...] = page_full[:, 20 * 512 : 38 * 512].astype(bf16)
    for j in range(3):
        cols[j] = col_shift(page_full, j - 1, 512)
    halve = halving(512, 0.25)

    def top(k, keep_pre):
        pieces = [
            cols[j, :, lanes_at((4 * k + i) * 512, 2048)] for i in range(3) for j in range(3)
        ]
        pre = mm(w_zero[...], jnp.concatenate(pieces, axis=0).astype(bf16))
        if keep_pre:
            pre_zero[:, lanes_at((k - 5) * 2048, 2048)] = pre.astype(bf16)
        enc = gelu_of(pre)
        pairs = jnp.concatenate(
            [enc[:, :512] + enc[:, 512:1024], enc[:, 1024:1536] + enc[:, 1536:]], axis=0
        )
        pooled = mm_fine(pairs, halve)
        first = tile * 8 - 10 + 2 * k
        for n in range(2):
            ok = (first + n >= 0) & (first + n < high // 2)
            part = jnp.where(ok, pooled[32 * n : 32 * n + 32], 0.0)
            pool_one[:, lanes_at((2 * k + n) * 256, 256)] = part.astype(bf16)

    for low, end, keep_pre in ((0, 5, False), (5, 9, True), (9, 14, False)):

        @pl.loop(low, end)
        def _(k, keep_pre=keep_pre):
            top(k, keep_pre)

    pre_zero.send()
    page_own.send()
    p_one[...] = pool_one[:, 9 * 256 : 19 * 256]
    p_one.send()
    stack_one[...] = stack_cols(pool_one[...], 256)
    halve_one = halving(256, 0.25)

    @pl.loop(0, 6)
    def _(k):
        pre = sum(
            mm(w_one[i], stack_one[:, lanes_at((4 * k + 1 + i) * 256, 1024)]) for i in range(3)
        )

        @pl.when((k >= 1) & (k < 5))
        def _():
            pre_one[:, lanes_at((k - 1) * 1024, 1024)] = pre.astype(bf16)

        enc = gelu_of(pre)
        pairs = jnp.concatenate(
            [enc[:, :256] + enc[:, 256:512], enc[:, 512:768] + enc[:, 768:]], axis=0
        )
        pooled = mm_fine(pairs, halve_one)
        first = tile * 4 - 4 + 2 * k
        for n in range(2):
            ok = (first + n >= 0) & (first + n < high // 4)
            part = jnp.where(ok, pooled[64 * n : 64 * n + 64], 0.0)
            pool_two[:, lanes_at((2 * k + n) * 128, 128)] = part.astype(bf16)

    pre_one.send()
    p_two[...] = pool_two[:, 3 * 128 : 9 * 128]
    p_two.send()
    stacked = stack_cols(pool_two[...], 128)
    pre = sum(mm(w_two[i], stacked[:, i * 128 : i * 128 + 1280]) for i in range(3))
    pre_two[...] = pre.astype(bf16)
    pre_two.send()
    enc = gelu_of(pre[:, 384:896])
    pairs = jnp.concatenate([enc[:, :128] + enc[:, 128:256], enc[:, 256:384] + enc[:, 384:]], axis=1)
    p_three[...] = mm_fine(pairs, pair_halving(0.25)).astype(bf16)


def run_down(ids, pages, w_zero, w_one, w_two):
    return call(
        10,
        down_body,
        [
            ((32, 16 * 512), bf16),
            ((64, 16 * 256), bf16),
            ((32, 10 * 256), bf16),
            ((128, 10 * 128), bf16),
            ((64, 6 * 128), bf16),
            ((128, 128), bf16),
            ((8, 18 * 512), bf16),
        ],
        [
            ((8, 80 * 512), f32),
            ((3, 8, 58 * 512), f32),
            ((32, 28 * 256), bf16),
            ((96, 28 * 256), bf16),
            ((64, 12 * 128), bf16),
        ],
        ids,
        (pages, w_zero, w_one, w_two),
        sent=(0, 1, 2, 3, 4, 6),
    )


def conv_taps(x, weight, width):
    total = None
    for i in range(3):
        lined = row_shift(x, i - 1, width)
        for j in range(3):
            term = mm(weight[i, j], col_shift(lined, j - 1, width))
            total = term if total is None else total + term
    return total


def conv_taps_back(x, weight, width):
    total = None
    for i in range(3):
        lined = row_shift(x, i - 1, width)
        for j in range(3):
            term = mm_tn(weight[2 - i, 2 - j], col_shift(lined, j - 1, width))
            total = term if total is None else total + term
    return total


def laid_out(blocks):
    return jnp.concatenate([blocks[n] for n in range(blocks.shape[0])], axis=1)


def bottom_body(cut, ids, p_three, w_three, w_four, w_up, pre_three, pre_four, p_four, e_four, pre_up, dec_three):
    lanes = 128 * p_three.shape[0]
    first, high = ids[3], ids[1]

    def kept(x, width, shrink):
        return keep_rows(x, first * (16 // shrink), width, high // shrink) if cut else x

    pre = conv_taps(laid_out(p_three), w_three, 64)
    pre_three[...] = pre.astype(bf16)
    pre_three.send()
    enc_three = kept(gelu_of(pre), 64, 8)
    spread = quad_map(lanes // 4, 32)
    high_part = enc_three.astype(bf16)
    low_part = (enc_three - high_part.astype(f32)).astype(bf16)
    pooled = ((mm_nt(high_part, spread) + mm_nt(low_part, spread)) * 0.25).astype(bf16)
    p_four[...] = pooled
    p_four.send()
    pre = conv_taps(pooled, w_four, 32)
    pre_four[...] = pre.astype(bf16)
    pre_four.send()
    low = kept(gelu_of(pre), 32, 16).astype(bf16)
    e_four[...] = low
    e_four.send()
    pre = conv_taps(mm(low, spread).astype(bf16), w_up, 64)
    pre_up[...] = pre.astype(bf16)
    pre_up.send()
    dec = kept(gelu_of(pre) + enc_three, 64, 8).astype(bf16)
    zero = jnp.zeros((256, 128), bf16)
    dec_three[:, 0:128] = zero
    dec_three[:, 128 : 128 + lanes] = dec
    dec_three[:, 128 + lanes :] = zero


def run_bottom(cut, ids, p_three, w_three, w_four, w_up):
    lanes = 128 * p_three.shape[0]
    return call(
        11,
        functools.partial(bottom_body, cut),
        [
            ((256, lanes), bf16),
            ((512, lanes // 4), bf16),
            ((256, lanes // 4), bf16),
            ((512, lanes // 4), bf16),
            ((256, lanes), bf16),
            ((256, lanes + 256), bf16),
        ],
        [],
        ids,
        (p_three, w_three, w_four, w_up),
        late=(2, 3),
        sent=(0, 1, 2, 3, 4),
    )


def widened(block):
    parts = []
    for n in range(block.shape[1] // 128):
        piece = block[:, 128 * n : 128 * n + 128]
        for side in range(2):
            line = mm(piece, side_doubling(side)).astype(bf16)
            parts += [line, line]
    return jnp.concatenate(parts, axis=1)


def spread_rows(source, target, width):
    spread = doubling(width)
    for n in range(source.shape[1] // width):
        line = mm(source[:, n * width : n * width + width], spread).astype(bf16)
        for m in range(2):
            target[:, (2 * n + m) * 2 * width : (2 * n + m + 1) * 2 * width] = line


def up_body(ids, dec_three, pre_two, pre_one, pre_zero, w_third, w_second, w_first, pre_up_two, pre_up_one, pre_up_zero, u_three, dec_two, dec_one, features, wide_two, stack_two, wide_one, stack_one):
    tile, high, place = ids[0], ids[1], ids[2]
    block = dec_three[:, lanes_at(place * 128, 384)]
    wide = widened(block)
    u_three[...] = wide[:, 384 : 384 + 768]
    u_three.send()
    total = None
    for j in range(3):
        moved = col_shift(wide, j - 1, 128)
        for i in range(3):
            term = mm(w_third[i, j], moved[:, i * 128 : i * 128 + 1280])
            total = term if total is None else total + term
    pre_up_two[...] = total.astype(bf16)
    pre_up_two.send()
    dec = gelu_of(total) + gelu_of(pre_two[...])
    dec = keep_rows(dec, tile * 4 - 3, 128, high // 4).astype(bf16)
    dec_two[...] = dec[:, 128 : 128 + 1024]
    dec_two.send()
    spread_rows(dec, wide_two, 128)
    stack_two[...] = stack_cols(wide_two[...], 256)
    for k in range(3):
        pre = sum(
            mm(w_second[i], stack_two[:, (6 * k + i) * 256 : (6 * k + i) * 256 + 1536])
            for i in range(3)
        )
        pre_up_one[:, 1536 * k : 1536 * k + 1536] = pre.astype(bf16)
    pre_up_one.send()
    dec = gelu_of(pre_up_one[:, 4 * 256 : 14 * 256]) + gelu_of(pre_one[:, 3 * 256 : 13 * 256])
    dec = keep_rows(dec, tile * 8 - 1, 256, high // 2).astype(bf16)
    dec_one[...] = dec
    dec_one.send()
    spread_rows(dec, wide_one, 256)
    stack_one[...] = stack_cols(wide_one[...], 512)
    pre_zero.ready()

    @pl.loop(0, 4)
    def _(k):
        pre = sum(
            mm(w_first[i], stack_one[:, lanes_at((4 * k + 1 + i) * 512, 2048)]) for i in range(3)
        )
        own = lanes_at(k * 2048, 2048)
        pre_up_zero[:, own] = pre.astype(bf16)
        found = (gelu_of(pre) + gelu_of(pre_zero[:, own])).astype(bf16)
        for n in range(4):
            features[pl.ds(pl.multiple_of((4 * k + n) * 32, 32), 32), :] = found[
                :, 512 * n : 512 * n + 512
            ]


def run_up(ids, dec_three, pre_two, pre_one, pre_zero, w_third, w_second, w_first):
    return call(
        9,
        up_body,
        [
            ((128, 10 * 128), bf16),
            ((64, 18 * 256), bf16),
            ((32, 16 * 512), bf16),
            ((256, 6 * 128), bf16),
            ((128, 8 * 128), bf16),
            ((64, 10 * 256), bf16),
            ((16 * 32, 512), bf16),
        ],
        [
            ((128, 20 * 256), bf16),
            ((384, 20 * 256), bf16),
            ((64, 20 * 512), bf16),
            ((192, 20 * 512), bf16),
        ],
        ids,
        (dec_three, pre_two, pre_one, pre_zero, w_third, w_second, w_first),
        late=(1, 2, 3),
        sent=(0, 1, 2, 3, 4, 5),
    )


def band_edges(boxes):
    left, top, right, bottom = (boxes[:, n : n + 1] for n in range(4))
    mid_col = (left + right) >> 1
    mid_row = (top + bottom) >> 1
    return ((left, mid_col, right), (top, mid_row, bottom))


def band_hits(edges, ids_wide, band):
    return (ids_wide >= edges[band]) & (ids_wide < edges[band + 1])


def area_inverse(cols, rows, a, b):
    return 1.0 / ((rows[a + 1] - rows[a]) * (cols[b + 1] - cols[b])).astype(f32)


def pool_body(step, ids, boxes, features, pooled):
    tile = ids[0]
    x_ids = lane_ids((1, 512))
    y_ids = (x_ids >> 5) + tile * 16
    group = lane_ids((1, 128)) >> 5

    @pl.loop(0, boxes.shape[0] // step)
    def _(k):
        own = pl.ds(pl.multiple_of(k * step, step), step)
        cols, rows = band_edges(boxes[own, :])
        result = jnp.zeros((step, 128), f32)
        inside = [jnp.where(band_hits(rows, y_ids, a), 1.0, 0.0) for a in range(2)]
        for b in range(2):
            hits = jnp.where(band_hits(cols, x_ids, b), 1.0, 0.0).astype(bf16)
            lines = mm_nt(hits, features[...])
            for a in range(2):
                part = lines * inside[a]
                part = part[:, :128] + part[:, 128:256] + (part[:, 256:384] + part[:, 384:])
                part = part + pltpu.roll(part, 64, 1)
                part = part + pltpu.roll(part, 32, 1)
                scaled = part * area_inverse(cols, rows, a, b)
                result = jnp.where(group == 2 * a + b, scaled, result)
        pooled[own, :] = result.astype(bf16)


def run_pool(ids, boxes, features, step):
    count = boxes.shape[0]
    return call(
        8, functools.partial(pool_body, step), [((count, 128), bf16)], [], ids, (boxes, features)
    )[0]


def unpool_body(step, ids, boxes, d_pooled, pre_up, d_features, d_low, low_end, low_start, token, total):
    tile = ids[0]
    x_ids = lane_ids((1, 512))
    y_ids = (x_ids >> 5) + tile * 16
    group = lane_ids((1, 128)) >> 5
    source = row_ids_of((128, 512))
    target = lane_ids((1, 512)) & 31
    copies = [
        jnp.where(source == target + 32 * n, 1.0, 0.0).astype(bf16) for n in range(4)
    ]
    total[...] = jnp.zeros_like(total)

    @pl.loop(0, boxes.shape[0] // step)
    def _(k):
        own = pl.ds(pl.multiple_of(k * step, step), step)
        cols, rows = band_edges(boxes[own, :])
        scale = jnp.zeros((step, 128), f32)
        for a in range(2):
            for b in range(2):
                scale = jnp.where(group == 2 * a + b, area_inverse(cols, rows, a, b), scale)
        share = (d_pooled[own, :].astype(f32) * scale).astype(bf16)
        found = None
        inside = [jnp.where(band_hits(rows, y_ids, a), 1.0, 0.0) for a in range(2)]
        for b in range(2):
            placed = mm(share, copies[b]) * inside[0] + mm(share, copies[2 + b]) * inside[1]
            hits = jnp.where(band_hits(cols, x_ids, b), 1.0, 0.0).astype(bf16)
            term = mm_tn(placed.astype(bf16), hits)
            found = term if found is None else found + term
        total[...] += found

    for y in range(16):
        own = slice(512 * y, 512 * y + 512)
        line = total[32 * y : 32 * y + 32, :]
        d_features[:, own] = line
        low = (line * gelu_slope(pre_up[:, own])).astype(bf16)
        d_low[:, own] = low
        if y >= 5:
            low_end[:, 512 * (y - 5) : 512 * (y - 4)] = low
        if y < 11:
            low_start[:, own] = low


def run_unpool(ids, after, boxes, d_pooled, pre_up, step):
    return call(
        8,
        functools.partial(unpool_body, step),
        [
            ((32, 8192), f32),
            ((32, 8192), bf16),
            ((32, 11 * 512), bf16),
            ((32, 11 * 512), bf16),
            TOKEN,
        ],
        [((512, 512), f32)],
        ids,
        (boxes, d_pooled, pre_up),
        after,
        late=(2,),
        sent=(0,),
    )


def up_back_body(ids, before, d_low, behind, pre_up_one, pre_up_two, wd_first, wd_second, w_third, d_dec_one, d_dec_two, d_dec_three, low_one, low_two, token, stack_zero, wide_low):
    tile, high = ids[0], ids[1]
    reach = 11 * 512
    for first, piece in ((0, before), (reach, d_low), (reach + 8192, behind)):
        stack_zero[:, first : first + piece.shape[1]] = stack_cols(piece[...], 512)
    halve = halving(512, 1.0)
    pre_up_one.ready()

    @pl.loop(0, 9)
    def _(k):
        back = sum(
            mm(wd_first[i], stack_zero[:, lanes_at((4 * k + i) * 512, 2048)]) for i in range(3)
        )
        pairs = jnp.concatenate(
            [back[:, :512] + back[:, 512:1024], back[:, 1024:1536] + back[:, 1536:]], axis=0
        )
        summed = mm_fine(pairs, halve)
        first = tile * 8 - 5 + 2 * k
        for n in range(2):
            ok = (first + n >= 0) & (first + n < high // 2)
            own = lanes_at((2 * k + n) * 256, 256)
            part = jnp.where(ok, summed[64 * n : 64 * n + 64], 0.0)
            d_dec_one[:, own] = part
            wide_low[:, own] = (part * gelu_slope(pre_up_one[:, own])).astype(bf16)

    d_dec_one.send()
    low_one[...] = wide_low[:, 5 * 256 : 13 * 256]
    low_one.send()
    stacked = stack_cols(wide_low[...], 256)
    halve_one = halving(256, 1.0)
    for k in range(4):
        back = sum(
            mm(wd_second[i], stacked[:, (4 * k + i) * 256 : (4 * k + i) * 256 + 1024])
            for i in range(3)
        )
        pairs = jnp.concatenate(
            [back[:, :256] + back[:, 256:512], back[:, 512:768] + back[:, 768:]], axis=0
        )
        summed = mm_fine(pairs, halve_one)
        for n in range(2):
            line = 2 * k + n
            row = tile * 4 - 2 + line
            ok = (row >= 0) & (row < high // 4)
            part = jnp.where(ok, summed[128 * n : 128 * n + 128], 0.0)
            d_dec_two[:, 128 * line : 128 * line + 128] = part
    low = d_dec_two[:, 128 : 7 * 128] * gelu_slope(pre_up_two[:, 2 * 128 : 8 * 128])
    low = low.astype(bf16)
    d_dec_two.send()
    low_two[...] = low[:, 128 : 5 * 128]
    low_two.send()
    total = None
    for j in range(3):
        moved = col_shift(low, j - 1, 128)
        for i in range(3):
            term = mm_tn(w_third[2 - i, 2 - j], moved[:, i * 128 : i * 128 + 512])
            total = term if total is None else total + term
    pairs = jnp.concatenate(
        [total[:, :128] + total[:, 128:256], total[:, 256:384] + total[:, 384:]], axis=1
    )
    d_dec_three[...] = mm_fine(pairs, pair_halving(1.0)).astype(bf16)


def run_up_back(ids, after, before, d_low, behind, pre_up_one, pre_up_two, wd_first, wd_second, w_third):
    return call(
        9,
        up_back_body,
        [
            ((64, 18 * 256), f32),
            ((128, 8 * 128), f32),
            ((256, 128), bf16),
            ((64, 8 * 256), bf16),
            ((128, 4 * 128), bf16),
            TOKEN,
        ],
        [((96, 38 * 512), bf16), ((64, 18 * 256), bf16)],
        ids,
        (before, d_low, behind, pre_up_one, pre_up_two, wd_first, wd_second, w_third),
        after,
        late=(3, 4),
        sent=(0, 1, 3, 4),
    )


def bottom_back_body(cut, ids, d_dec_three, pre_up, pre_four, pre_three, w_up, w_four, w_three, low_up, low_four, low_three, d_pool, token, padded):
    lanes = 128 * d_dec_three.shape[0]
    first, high, place = ids[3], ids[1], ids[2]

    def kept(x, width, shrink):
        return keep_rows(x, first * (16 // shrink), width, high // shrink) if cut else x

    d_dec = laid_out(d_dec_three).astype(f32)
    low = (d_dec * gelu_slope(pre_up[...])).astype(bf16)
    low_up[...] = low
    spread = quad_map(lanes // 4, 32)
    back = conv_taps_back(low, w_up, 64)
    high_part = back.astype(bf16)
    low_part = (back - high_part.astype(f32)).astype(bf16)
    d_enc = kept(mm_nt(high_part, spread) + mm_nt(low_part, spread), 32, 16)
    low = (d_enc * gelu_slope(pre_four[...])).astype(bf16)
    low_four[...] = low
    back = conv_taps_back(low, w_four, 32) * 0.25
    d_enc = kept(d_dec + mm_fine(back, spread), 64, 8)
    low = (d_enc * gelu_slope(pre_three[...])).astype(bf16)
    low_three[...] = low
    zero = jnp.zeros((256, 128), bf16)
    padded[:, 0:128] = zero
    padded[:, 128 : 128 + lanes] = low
    padded[:, 128 + lanes :] = zero
    window = padded[:, lanes_at(place * 128, 384)]
    d_pool[...] = conv_taps_back(window, w_three, 64)[:, 0:384]


def run_bottom_back(cut, ids, after, d_dec_three, pre_up, pre_four, pre_three, w_up, w_four, w_three):
    lanes = 128 * d_dec_three.shape[0]
    return call(
        10,
        functools.partial(bottom_back_body, cut),
        [
            ((256, lanes), bf16),
            ((512, lanes // 4), bf16),
            ((256, lanes), bf16),
            ((128, 384), f32),
            TOKEN,
        ],
        [((256, lanes + 256), bf16)],
        ids,
        (d_dec_three, pre_up, pre_four, pre_three, w_up, w_four, w_three),
        after,
        late=(1, 4, 2, 5, 3, 6),
        sent=(3,),
    )


def down_back_body(ids, d_pool_three, d_dec_two, pre_two, d_dec_one, pre_one, d_features, pre_zero, w_two, wd_one, low_two, low_one, low_zero, wide_one):
    tile, high = ids[0], ids[1]
    d_dec_one.ready()
    pre_one.ready()
    d_features.ready()
    pre_zero.ready()
    quarter = d_pool_three[...] * 0.25
    parts = []
    for n in range(3):
        piece = quarter[:, 128 * n : 128 * n + 128]
        for side in range(2):
            line = mm_fine(piece, side_doubling(side))
            parts += [line, line]
    spread = jnp.concatenate(parts[2:10], axis=1)
    d_enc = keep_rows(d_dec_two[...] + spread, tile * 4 - 2, 128, high // 4)
    low = (d_enc * gelu_slope(pre_two[:, 128 : 9 * 128])).astype(bf16)
    low_two[...] = low[:, 2 * 128 : 6 * 128]
    total = None
    for j in range(3):
        moved = col_shift(low, j - 1, 128)
        for i in range(3):
            term = mm_tn(w_two[2 - i, 2 - j], moved[:, i * 128 : i * 128 + 768])
            total = term if total is None else total + term
    total = total * 0.25
    wide = doubling(128)
    for n in range(6):
        line = mm_fine(total[:, 128 * n : 128 * n + 128], wide)
        for m in range(2):
            row = 2 * n + m
            value = d_dec_one[:, (3 + row) * 256 : (4 + row) * 256] + line
            ok = (tile * 8 - 2 + row >= 0) & (tile * 8 - 2 + row < high // 2)
            value = jnp.where(ok, value, 0.0)
            slope = gelu_slope(pre_one[:, (2 + row) * 256 : (3 + row) * 256])
            wide_one[:, row * 256 : row * 256 + 256] = (value * slope).astype(bf16)
    low_one[...] = wide_one[:, 2 * 256 : 10 * 256]
    stacked = stack_cols(wide_one[...], 256)
    back = sum(mm(wd_one[i], stacked[:, (1 + i) * 256 : (9 + i) * 256]) for i in range(3)) * 0.25
    wider = doubling(256)
    for n in range(8):
        line = mm_fine(back[:, 256 * n : 256 * n + 256], wider)
        for m in range(2):
            own = slice((2 * n + m) * 512, (2 * n + m + 1) * 512)
            value = (d_features[:, own] + line) * gelu_slope(pre_zero[:, own])
            low_zero[:, own] = value.astype(bf16)


def run_down_back(ids, after, *arrays):
    return call(
        4,
        down_back_body,
        [
            ((128, 4 * 128), bf16),
            ((64, 8 * 256), bf16),
            ((32, 16 * 512), bf16),
        ],
        [((64, 12 * 256), bf16)],
        ids,
        arrays,
        after,
        late=(0, 1, 2, 3, 4, 5, 6),
    )


def grad_up_first_body(ids, dec_one, d_low, grad, wide_one, stack_one):
    spread_rows(dec_one[...], wide_one, 256)
    stack_one[...] = stack_cols(wide_one[...], 512)
    for i in range(3):
        grad[i] = mm_nt(d_low[...], stack_one[:, (1 + i) * 512 : (17 + i) * 512])


def run_grad_up_first(ids, after, dec_one, d_low):
    return call(
        4,
        grad_up_first_body,
        [((3, 32, 192), f32)],
        [((64, 20 * 512), bf16), ((192, 20 * 512), bf16)],
        ids,
        (dec_one, d_low),
        after,
        late=(0,),
    )[0]


def grad_up_body(ids, grad_first, dec_two, low_one, u_three, low_two, table, token, wide_two, stack_two):
    spread_rows(dec_two[...], wide_two, 128)
    stack_two[...] = stack_cols(wide_two[...], 256)
    for j in range(3):
        moved = col_shift(u_three[...], j - 1, 128)
        for i in range(3):
            first = (3 * i + j) * 128
            grad = mm_nt(low_two[...], moved[:, i * 128 : i * 128 + 512])
            table[first : first + 128, :] = grad.astype(bf16)
    rest = []
    for i in range(3):
        grad = mm_nt(low_one[...], stack_two[:, (3 + i) * 256 : (11 + i) * 256]).astype(bf16)
        table[1152 + 64 * i : 1216 + 64 * i, :] = grad[:, :256]
        rest.append(grad[:, 256:])
    rest = jnp.concatenate(rest, axis=0)
    table[1344:1440, :] = jnp.concatenate([rest[:96], rest[96:]], axis=1)
    table[1440:1536, :] = jnp.zeros((96, 256), bf16)
    for i in range(3):
        table[1440 + 32 * i : 1472 + 32 * i, 0:192] = grad_first[i].astype(bf16)


def run_grad_up(ids, after, *arrays):
    return call(
        4,
        grad_up_body,
        [((1536, 256), bf16), TOKEN],
        [((128, 16 * 256), bf16), ((384, 16 * 256), bf16)],
        ids,
        arrays,
        after,
        late=(1, 2, 3, 4),
    )


def halve_body(ids, kept, got, mine, other, token):
    half = mine.shape[0]
    for bit in range(2):

        @pl.when(ids[5] == bit)
        def _(bit=bit):
            for out, side in ((mine, bit), (other, 1 - bit)):
                own = slice(half * side, half * side + half)
                out[...] = (kept[own, :].astype(f32) + got[own, :].astype(f32)).astype(bf16)


def run_halve(ids, bit, kept, got, after):
    rows, width = kept.shape
    return call(
        max(1, rows // 1500),
        halve_body,
        [((rows // 2, width), bf16)] * 2 + [TOKEN],
        [],
        ids.at[5].set(bit),
        (kept, got),
        after,
    )


def finish_body(ids, kept, got, share):
    share[...] = (kept[...].astype(f32) + got[...].astype(f32)).astype(bf16)


def total_body(ids, parts, share, token):
    total = parts[0].astype(f32)
    for n in range(1, parts.shape[0]):
        total = total + parts[n].astype(f32)
    half = total.shape[0] // 2
    share[...] = jnp.concatenate([total[:half], total[half:]], axis=1).astype(bf16)


def run_total(ids, parts):
    rows, width = parts.shape[1:]
    outs = [((rows // 2, 2 * width), bf16), TOKEN]
    return call(1, total_body, outs, [], ids, (parts,))


def gather_body(ids, heavy, embed, early, share):
    rows, width = heavy.shape[1:]
    total = heavy[0].astype(f32)
    for n in range(1, heavy.shape[0]):
        total = total + heavy[n].astype(f32)
    share[0:rows, :] = total.astype(bf16)
    share[rows : rows + 64, :] = embed[...]
    pad = jnp.zeros((8, width), f32)
    share[rows + 64 :, :] = jnp.concatenate([early[...].astype(f32), pad], axis=0).astype(bf16)


def run_gather(ids, heavy, embed, early):
    rows, width = heavy.shape[1:]
    outs = [((rows + 96, width), bf16)]
    return call(1, gather_body, outs, [], ids, (heavy, embed, early))[0]


def run_finish(ids, kept, got, after):
    return call(1, finish_body, [(kept.shape, bf16)], [], ids, (kept, got), after)[0]


def taps_of(x, width):
    for i in range(3):
        lined = row_shift(x, i - 1, width)
        for j in range(3):
            yield 3 * i + j, col_shift(lined, j - 1, width)


def grad_bottom_body(split, ids, low_up, e_four, low_four, p_four, low_three, p_three, table, token, up_part, four_part, three_part):
    place = ids[2]
    lanes = low_up.shape[1]
    spread = quad_map(lanes // 4, 32)
    shares = table.shape[0]

    def own_part(low):
        rows = low.shape[0] // split
        return low[pl.ds(pl.multiple_of(place * rows, rows), rows), :]

    low = own_part(low_up)
    for tap, x in taps_of(mm(e_four[...], spread).astype(bf16), 64):
        up_part[tap] = mm_nt(low, x)
    low = own_part(low_four)
    for tap, x in taps_of(p_four[...], 32):
        four_part[tap] = mm_nt(low, x)
    low = own_part(low_three)
    for tap, x in taps_of(laid_out(p_three), 64):
        three_part[tap] = mm_nt(low, x)
    for n in range(shares):
        for tap in range(9):
            fifth = jnp.concatenate(
                [
                    four_part[tap, 16 * n : 16 * n + 8, :],
                    four_part[tap, 16 * n + 8 : 16 * n + 16, :],
                ],
                axis=1,
            )
            main = jnp.concatenate([up_part[tap, 8 * n : 8 * n + 8, :], fifth], axis=0)
            table[n, 16 * tap : 16 * tap + 16, :] = main.astype(bf16)
        zero = jnp.zeros((8, 128), f32)
        sides = [three_part[tap, 8 * n : 8 * n + 8, :] for tap in range(9)] + [zero] * 7
        sides = [jnp.concatenate(sides[4 * k : 4 * k + 4], axis=1) for k in range(4)]
        table[n, 144:176, :] = jnp.concatenate(sides, axis=0).astype(bf16)


def run_grad_bottom(split, shares, ids, after, *arrays):
    return call(
        6,
        functools.partial(grad_bottom_body, split),
        [((shares, 176, 512), bf16), TOKEN],
        [
            ((9, 256 // split, 512), f32),
            ((9, 512 // split, 256), f32),
            ((9, 256 // split, 128), f32),
        ],
        ids,
        arrays,
        after,
        late=(1, 3),
    )


def unpack_body(split, whole, *refs):
    stage, marks = refs[-2:]
    plain = list(refs[:-2])
    step = pl.program_id(0)
    last = pl.num_programs(0) - 1

    def fetch(n):
        return pltpu.make_async_copy(whole.at[n], stage.at[n % 4], marks.at[n % 4])

    @pl.when(step == 0)
    def _():
        for n in range(3):
            fetch(n).start()

    @pl.when(step + 3 <= last)
    def _():
        fetch(step + 3).start()

    fetch(step).wait()
    held = stage.at[step % 4]
    first = 0
    if split:
        up, fifth, fourth, *plain, early = plain
        for tap in range(9):
            block = held[16 * tap : 16 * tap + 16, :].astype(f32)
            up[tap] = block[0:8, :]
            fifth[tap, 0:8, :] = block[8:16, 0:256]
            fifth[tap, 8:16, :] = block[8:16, 256:512]
        sides = held[144:176, :].astype(f32)
        for tap in range(9):
            rows = slice(8 * (tap // 4), 8 * (tap // 4) + 8)
            fourth[tap] = sides[rows, 128 * (tap % 4) : 128 * (tap % 4) + 128]
        first = 176
    for out in plain:
        rows = out.shape[0]
        out[...] = held[first : first + rows, :].astype(f32)
        first = first + rows
    if split:
        block = held[first : first + 32, :].astype(f32)
        early[0:24, :] = block[0:24, 0:256]
        early[24:48, :] = block[0:24, 256:512]


def run_unpack(whole, split, rows):
    tiles = whole.shape[0] // 4

    def by_page(n):
        return (0, n % tiles * 4 + n // tiles, 0)

    def chunk_of(n):
        tile, page = n % tiles, n // tiles
        return page % 2 * 16 + page // 2 * 8 + tile % 2 * 4 + tile // 4 * 2 + tile // 2 % 2

    def by_chunk(n):
        return (chunk_of(n), 0)

    def by_column(n):
        return (chunk_of(n) % 8, chunk_of(n) // 8)

    outs = [
        (
            jax.ShapeDtypeStruct((total, width), f32),
            pl.BlockSpec((size, 512), by_column if width > 512 else by_chunk),
        )
        for total, width, size in rows
    ]
    if split:
        outs = (
            [
                (jax.ShapeDtypeStruct((9, 256, 512), f32), pl.BlockSpec((9, 8, 512), by_page)),
                (jax.ShapeDtypeStruct((9, 512, 256), f32), pl.BlockSpec((9, 16, 256), by_page)),
                (jax.ShapeDtypeStruct((9, 256, 128), f32), pl.BlockSpec((9, 8, 128), by_page)),
            ]
            + outs
            + [(jax.ShapeDtypeStruct((1536, 256), f32), pl.BlockSpec((48, 256), lambda n: (n, 0)))]
        )
    return pl.pallas_call(
        functools.partial(unpack_body, split),
        cost_estimate=price(8),
        grid=(whole.shape[0],),
        out_shape=[out for out, _ in outs],
        in_specs=[pl.BlockSpec(memory_space=pltpu.HBM)],
        out_specs=[spec for _, spec in outs],
        scratch_shapes=[
            pltpu.VMEM((4, *whole.shape[1:]), bf16),
            pltpu.SemaphoreType.DMA((4,)),
        ],
        compiler_params=pltpu.CompilerParams(vmem_limit_bytes=VMEM_CAP),
    )(in_hbm(whole))


def grad_bottom_all_body(ids, low_up, e_four, low_four, p_four, low_three, p_three, grad_up, grad_four, grad_three):
    lanes = low_up.shape[1]
    spread = quad_map(lanes // 4, 32)

    def own_part(low):
        size = low.shape[1] // (lanes // 128)
        own = lane_ids(low.shape) // size == ids[2]
        return jnp.where(own, low[...], jnp.zeros((), bf16))

    low = own_part(low_up)
    for tap, x in taps_of(mm(e_four[...], spread).astype(bf16), 64):
        grad_up[tap] = mm_nt(low, x).astype(bf16)
    low = own_part(low_four)
    for tap, x in taps_of(p_four[...], 32):
        grad_four[tap] = mm_nt(low, x).astype(bf16)
    low = own_part(low_three)
    for tap, x in taps_of(laid_out(p_three), 64):
        grad_three[tap] = mm_nt(low, x).astype(bf16)


def run_grad_bottom_all(ids, *arrays):
    return call(
        6,
        grad_bottom_all_body,
        [((9, 256, 512), bf16), ((9, 512, 256), bf16), ((9, 256, 128), bf16)],
        [],
        ids,
        arrays,
    )


def grad_down_body(ids, p_two, low_two, p_one, low_one, page, low_zero, table, cols):
    stacked = stack_cols(p_two[...], 128)
    for i in range(3):
        grad = mm_nt(low_two[...], stacked[:, i * 128 : i * 128 + 512]).astype(bf16)
        table[128 * i : 128 * i + 128, 0:192] = grad
    table[0:384, 192:256] = jnp.zeros((384, 64), bf16)
    table[384:512, :] = jnp.zeros((128, 256), bf16)
    stacked = stack_cols(p_one[...], 256)
    parts = [
        mm_nt(low_one[...], stacked[:, i * 256 : i * 256 + 2048]).astype(bf16) for i in range(3)
    ]
    grad = jnp.concatenate(parts, axis=0)
    table[384:480, 0:96] = grad[:96]
    table[384:480, 128:224] = grad[96:]
    rows = page[...].astype(f32)
    for j in range(3):
        cols[j] = col_shift(rows, j - 1, 512)
    pieces = [cols[j, :, i * 512 : i * 512 + 8192] for i in range(3) for j in range(3)]
    grad = mm_nt(low_zero[...], jnp.concatenate(pieces, axis=0).astype(bf16))
    table[480:512, 0:72] = grad.astype(bf16)


def run_grad_down(ids, *arrays):
    return call(
        3,
        grad_down_body,
        [((512, 256), bf16)],
        [((3, 8, 18 * 512), f32)],
        ids,
        arrays,
        late=(0, 2, 4),
    )[0]


def bucket_of(signed_gap):
    distance = jnp.abs(signed_gap)
    far_steps = jnp.zeros_like(distance)
    for threshold in bounds:
        far_steps = far_steps + (distance >= threshold).astype(jnp.int32)
    nearness = jnp.where(distance < 8, distance, 8 + far_steps)
    return nearness + jnp.where(signed_gap > 0, 16, 0).astype(jnp.int32)


def rms_scale(value, gain):
    return value * lax.rsqrt(jnp.mean(value * value, axis=-1, keepdims=True) + eps) * gain


def gelu_back(pre_act, upstream):
    return jax.vjp(jax.nn.gelu, pre_act)[1](upstream)[0]


def block_scores(query_heads, key_heads, query_meta, key_meta, bias_table, score_scale):
    query_pos, query_cx, query_cy, query_seg = query_meta
    key_pos, key_cx, key_cy, key_seg = key_meta
    rel_bucket = bucket_of(key_pos[None, :] - query_pos[:, None])
    hor_bucket = bucket_of(key_cx[None, :] - query_cx[:, None]) + NB
    ver_bucket = bucket_of(key_cy[None, :] - query_cy[:, None]) + 2 * NB
    slot_ids = jnp.arange(3 * NB)
    one_hot = (
        (rel_bucket[..., None] == slot_ids)
        | (hor_bucket[..., None] == slot_ids)
        | (ver_bucket[..., None] == slot_ids)
    ).astype(jnp.bfloat16)
    scores = (
        jnp.einsum("hqd,hkd->hqk", query_heads, key_heads, preferred_element_type=jnp.float32)
        * score_scale
    )
    scores = scores + jnp.einsum(
        "qkn,hn->hqk", one_hot, bias_table, preferred_element_type=jnp.float32
    )
    allowed = query_seg[:, None] == key_seg[None, :]
    return (scores, allowed, one_hot)


def norm_parts(value):
    scale = lax.rsqrt(jnp.mean(value * value, axis=-1, keepdims=True) + eps)
    return scale


def norm_back(value, gain, upstream):
    scale = norm_parts(value)
    weighted = upstream * gain
    inner = jnp.mean(weighted * value, axis=-1, keepdims=True)
    d_value = weighted * scale - value * (inner * scale * scale * scale)
    d_gain = jnp.sum(upstream * value * scale, axis=0, keepdims=True)
    return d_value, d_gain


def embed_body(ids, pieces, emb, roi, gain, wq, wk, wv, residual, normed, pooled, shared):
    total = pieces[0].astype(f32)
    for n in range(1, pieces.shape[0]):
        total = total + pieces[n].astype(f32)
    low = total.astype(bf16)
    pooled[...] = low
    resid = emb[...].astype(f32) + mm(low, roi[...])
    residual[...] = resid
    normal = (resid * norm_parts(resid) * gain[...].astype(f32)).astype(bf16)
    normed[...] = normal
    for n, weight in enumerate((wq, wk, wv)):
        turned = mm(normal, weight[...]).T.astype(bf16)
        for h in range(HEADS):
            shared[h, HD * n : HD * n + HD, :] = turned[HD * h : HD * h + HD, :]


def run_embed(ids, pieces, emb, *arrays):
    rows, width = emb.shape
    return call(
        2,
        embed_body,
        [
            ((rows, width), f32),
            ((rows, width), bf16),
            ((rows, pieces.shape[2]), bf16),
            ((HEADS, 3 * HD, rows), bf16),
        ],
        [],
        ids,
        (pieces, emb, *arrays),
    )


def looked_up(bucket, table, head, first):
    value = jnp.zeros(bucket.shape, f32)
    for n in range(NB):
        value = jnp.where(bucket == n, table[head, first + n], value)
    return value


def toeplitz(span, table, head, first):
    lane = lane_ids((1, 2 * span))
    gap = jnp.where(lane < span, -lane, 2 * span - lane)
    line = looked_up(bucket_of(gap), table, head, first)
    square = jnp.broadcast_to(line, (span, 2 * span))
    return pltpu.roll(square, 0, 1, stride=1, stride_axis=0)[:, :span].astype(bf16)


def centers(meta):
    return ((meta[0:1, :] + meta[2:3, :]) >> 1, (meta[1:2, :] + meta[3:4, :]) >> 1)


def one_hot_rows(value, span, turned):
    row = row_ids_of((span, value.shape[1]))
    if turned:
        row = span - 1 - row
    return jnp.where(row == value, 1.0, 0.0).astype(bf16)


def attend_body(tall, ids, table, meta, meta_cols, shared, prob, out_low, out_full, hits, spread, near):
    head = ids[0]
    seq = meta.shape[1]
    count = shared.shape[0]
    spans = (512, tall)
    for n, (value, span) in enumerate(zip(centers(meta), spans)):
        chart = toeplitz(span, table, head, NB * (n + 1))
        low = sum(spans[:n])
        spread[low : low + span, :] = mm(chart, one_hot_rows(value, span, False)).astype(bf16)
    cols = meta_cols[...]
    for n, span in enumerate(spans):
        value = (cols[:, n : n + 1] + cols[:, n + 2 : n + 3]) >> 1
        low = sum(spans[:n])
        same = lane_ids((1, span)) == value
        hits[:, low : low + span] = jnp.where(same, 1.0, 0.0).astype(bf16)
    edge = seq - 128
    near[0 : edge - 128, :] = jnp.full((edge - 128, 128), table[head, NB // 2 - 1], f32)
    near[edge + 256 :, :] = jnp.full((seq - 256, 128), table[head, NB - 1], f32)
    gap = row_ids_of((384, 128)) - 128 - lane_ids((384, 128))
    near[edge - 128 : edge + 256, :] = looked_up(bucket_of(gap), table, head, 0)
    query = jnp.concatenate([shared[n, 0:HD, :] for n in range(count)], axis=1)
    key = jnp.concatenate([shared[n, HD : 2 * HD, :] for n in range(count)], axis=1)
    value = jnp.concatenate([shared[n, 2 * HD :, :] for n in range(count)], axis=1)
    key = (key.astype(f32) * (HD**-0.5)).astype(bf16)
    seg_key = cols[:, 4:5]
    for block in range(seq // 256):
        own = slice(256 * block, 256 * block + 256)
        first = edge - 256 * block
        scores = mm_tn(key, query[:, own]) + mm(hits[...], spread[:, own])
        scores = scores + jnp.concatenate(
            [near[first : first + seq, :], near[first - 128 : first - 128 + seq, :]], axis=1
        )
        scores = jnp.where(seg_key == meta[4:5, own], scores, neg_large)
        weight = jnp.exp(scores - jnp.max(scores, axis=0, keepdims=True))
        weight = weight * (1.0 / jnp.sum(weight, axis=0, keepdims=True))
        low = weight.astype(bf16)
        prob[block] = low
        found = mm(value, low)
        out_full[:, own] = found
        for n in range(2):
            out_low[2 * block + n] = found[:, 128 * n : 128 * n + 128].astype(bf16)


def run_attend(tall, ids, table, meta, meta_cols, shared):
    seq = meta.shape[1]
    count = shared.shape[0]
    return call(
        9,
        functools.partial(attend_body, tall),
        [
            ((seq // 256, seq, 256), bf16),
            ((count, HD, seq // count), bf16),
            ((HD, seq), f32),
        ],
        [
            ((seq, 512 + tall), bf16),
            ((512 + tall, seq), bf16),
            ((2 * seq - 128, 128), f32),
        ],
        ids,
        (meta, meta_cols, shared),
        sent=(0, 2),
        table=table,
    )


def bucket_sums(value, bucket):
    lines = [
        jnp.sum(jnp.where(bucket == n, value, 0.0), axis=0, keepdims=True) for n in range(NB)
    ]
    return jnp.sum(jnp.concatenate(lines, axis=0), axis=1, keepdims=True)


def attend_back_body(tall, ids, meta, shared, prob, out_full, d_out, d_shared, d_table, near, drift, key_sum, value_sum):
    seq = meta.shape[1]
    count = shared.shape[0]
    spans = (512, tall)
    query = jnp.concatenate([shared[n, 0:HD, :] for n in range(count)], axis=1)
    key = jnp.concatenate([shared[n, HD : 2 * HD, :] for n in range(count)], axis=1)
    value = jnp.concatenate([shared[n, 2 * HD :, :] for n in range(count)], axis=1)
    d_found = jnp.concatenate([d_out[n] for n in range(count)], axis=1)
    delta = jnp.sum(d_found.astype(f32) * out_full[...], axis=0, keepdims=True)
    near[...] = jnp.zeros_like(near)
    key_sum[...] = jnp.zeros_like(key_sum)
    value_sum[...] = jnp.zeros_like(value_sum)
    places = centers(meta)
    turned = jnp.concatenate(
        [one_hot_rows(place, span, True) for place, span in zip(places, spans)], axis=0
    )
    edge = seq - 128
    scale = HD**-0.5
    for block in range(seq // 256):
        own = slice(256 * block, 256 * block + 256)
        first = edge - 256 * block
        low = prob[block]
        d_prob = mm_tn(value, d_found[:, own])
        d_score = low.astype(f32) * (d_prob - delta[:, own])
        near[first : first + seq, :] += d_score[:, :128]
        near[first - 128 : first - 128 + seq, :] += d_score[:, 128:]
        d_low = d_score.astype(bf16)
        d_query = (mm(key, d_low) * scale).astype(bf16)
        for n in range(2):
            d_shared[2 * block + n, 0:HD, :] = d_query[:, 128 * n : 128 * n + 128]
        key_sum[...] += mm_nt(query[:, own], d_low)
        value_sum[...] += mm_nt(d_found[:, own], low)
        drift[:, own] = mm(turned, d_low).astype(bf16)
    d_key = (key_sum[...] * scale).astype(bf16)
    d_value = value_sum[...].astype(bf16)
    for n in range(count):
        d_shared[n, HD : 2 * HD, :] = d_key[:, 128 * n : 128 * n + 128]
        d_shared[n, 2 * HD :, :] = d_value[:, 128 * n : 128 * n + 128]
    sums = []
    slot = 3 * ids[0]
    gap = row_ids_of((384, 128)) - 128 - lane_ids((384, 128))
    sums.append(bucket_sums(near[edge - 128 : edge + 256, :], bucket_of(gap)))
    row = row_ids_of((NB, 128))
    lane = lane_ids((NB, 128))
    behind = jnp.sum(near[0 : edge - 128, :], axis=0, keepdims=True)
    ahead = jnp.sum(near[edge + 256 :, :], axis=0, keepdims=True)
    far = jnp.where(row == NB // 2 - 1, behind, jnp.where(row == NB - 1, ahead, 0.0))
    sums[0] = sums[0] + jnp.sum(far, axis=1, keepdims=True)
    for n, (place, span) in enumerate(zip(places, spans)):
        low = sum(spans[:n])
        square = mm_nt(drift[low : low + span, :], one_hot_rows(place, span, False))
        square = jnp.concatenate([square, jnp.zeros_like(square)], axis=1)
        lined = pltpu.roll(square, 0, 1, stride=1, stride_axis=0)
        line = jnp.sum(lined, axis=0, keepdims=True)
        bucket = bucket_of(span - 1 - lane_ids((1, 2 * span)))
        sums.append(bucket_sums(line, bucket))
    d_table[...] = jnp.where(
        lane == slot,
        sums[0],
        jnp.where(lane == slot + 1, sums[1], jnp.where(lane == slot + 2, sums[2], 0.0)),
    )


def run_attend_back(tall, ids, after, meta, *arrays):
    seq = meta.shape[1]
    shared = arrays[0]
    return call(
        6,
        functools.partial(attend_back_body, tall),
        [(shared.shape, bf16), ((NB, 128), f32)],
        [
            ((2 * seq - 128, 128), f32),
            ((512 + tall, seq), bf16),
            ((HD, seq), f32),
            ((HD, seq), f32),
        ],
        ids,
        (meta, *arrays),
        after,
        late=(3, 2),
    )


def mixer_body(ids, found, residual, upstream, w_out, gain, w_in, w_down, result, act, d_pre, ffn_low, d_mixed, d_low, d_found, d_gain):
    attn = jnp.concatenate([found[h] for h in range(HEADS)], axis=0)
    mixed = residual[...] + mm_tn(attn, w_out[...])
    wide_gain = gain[...].astype(f32)
    low = (mixed * norm_parts(mixed) * wide_gain).astype(bf16)
    ffn_low[...] = low
    pre = mm(low, w_in[...])
    hidden = gelu_of(pre).astype(bf16)
    act[...] = hidden
    result[...] = (mixed + mm(hidden, w_down[...])).astype(bf16)
    d_hidden = (mm_nt(upstream[...], w_down[...]) * gelu_slope(pre)).astype(bf16)
    d_pre[...] = d_hidden
    d_norm, gain_sum = norm_back(mixed, wide_gain, mm_nt(d_hidden, w_in[...]))
    d_gain[...] = gain_sum
    d_sum = upstream[...].astype(f32) + d_norm
    d_mixed[...] = d_sum
    narrow = d_sum.astype(bf16)
    d_low[...] = narrow
    back = mm_nt(w_out[...], narrow).astype(bf16)
    for h in range(HEADS):
        d_found[h] = back[HD * h : HD * h + HD, :]


def run_mixer(ids, found, residual, upstream, w_out, gain, w_in, w_down):
    rows, width = residual.shape
    wide = w_in.shape[1]
    return call(
        5,
        mixer_body,
        [
            ((rows, width), bf16),
            ((rows, wide), bf16),
            ((rows, wide), bf16),
            ((rows, width), bf16),
            ((rows, width), f32),
            ((rows, width), bf16),
            ((HEADS, HD, rows), bf16),
            ((1, width), f32),
        ],
        [],
        ids,
        (found, residual, upstream, w_out, gain, w_in, w_down),
        late=(5, 6),
    )


def put_halves(ids, first, second, mine, other):
    for bit in range(2):

        @pl.when(ids[5] == bit)
        def _(bit=bit):
            mine[...] = first[...] if bit == 0 else second[...]
            other[...] = second[...] if bit == 0 else first[...]


def mixer_grads_body(ids, found, act, d_pre, ffn_low, d_low, upstream, mine, other, token, table):
    width = ffn_low.shape[1]
    grad_out = mm_tn(act[...], upstream[...]).astype(bf16)
    grad_in = mm_tn(ffn_low[...], d_pre[...]).astype(bf16)
    attn = jnp.concatenate([found[h] for h in range(HEADS)], axis=0)
    grad_attn = mm(attn, d_low[...]).astype(bf16)
    for c in range(32):
        spot, row = 144 * (c % 16), 64 * (c % 8)
        table[c // 16, spot : spot + 64, :] = grad_out[64 * c : 64 * c + 64, :]
        column = width * (c // 8)
        table[c // 16, spot + 64 : spot + 128, :] = grad_in[row : row + 64, column : column + width]
        table[c // 16, spot + 128 : spot + 144, :] = grad_attn[16 * c : 16 * c + 16, :]
    put_halves(ids, table.at[0], table.at[1], mine, other)


def run_mixer_grads(ids, bit, *arrays):
    return call(
        4,
        mixer_grads_body,
        [((2304, 512), bf16)] * 2 + [TOKEN],
        [((2, 2304, 512), bf16)],
        ids.at[5].set(bit),
        arrays,
    )


def embed_back_body(ids, d_shared, residual, d_mixed, gain, wq, wk, wv, roi, d_resid, d_low, d_pooled, d_gain, d_rows, token):
    turned = None
    for n, weight in enumerate((wq, wk, wv)):
        lines = jnp.concatenate([d_shared[h, HD * n : HD * n + HD, :] for h in range(HEADS)], axis=0)
        d_rows[n] = lines
        term = mm(weight[...], lines)
        turned = term if turned is None else turned + term
    d_norm, gain_sum = norm_back(residual[...], gain[...].astype(f32), turned.T)
    d_gain[...] = gain_sum
    total = d_mixed[...] + d_norm
    d_resid[...] = total
    low = total.astype(bf16)
    d_low[...] = low
    d_pooled[...] = mm_nt(low, roi[...]).astype(bf16)


def run_embed_back(ids, d_shared, residual, *arrays):
    rows, width = residual.shape
    roi = arrays[-1]
    return call(
        2,
        embed_back_body,
        [
            ((rows, width), f32),
            ((rows, width), bf16),
            ((rows, roi.shape[0]), bf16),
            ((1, width), f32),
            ((3, HEADS * HD, rows), bf16),
            TOKEN,
        ],
        [],
        ids,
        (d_shared, residual, *arrays),
    )


def embed_grads_body(ids, normed, d_rows, pooled, d_low, gains_one, gains_two, d_table, mine, other, token, table):
    width = normed.shape[1]
    turned = normed[...].astype(f32).T.astype(bf16)
    grads = [mm_nt(turned, d_rows[n]).astype(bf16) for n in range(3)]
    roi = mm_tn(pooled[...], d_low[...])
    lane = lane_ids((1, width))
    buckets = jnp.concatenate([d_table[...]] * (width // 128), axis=1)
    buckets = jnp.where(lane < 128, buckets, 0.0)
    blank = jnp.zeros((1, width), f32)
    for c in range(32):
        spot = 64 * (c % 16)
        for n in range(3):
            table[c // 16, spot + 16 * n : spot + 16 * n + 16, :] = grads[n][16 * c : 16 * c + 16, :]
        gains = [gains_one[...], gains_two[...]] if c == 0 else [blank, blank]
        lines = [roi[4 * c : 4 * c + 4, :], buckets[c : c + 1, :], *gains, blank]
        lines = jnp.concatenate(lines + [jnp.zeros((8, width), f32)], axis=0)
        table[c // 16, spot + 48 : spot + 64, :] = lines.astype(bf16)
    put_halves(ids, table.at[0], table.at[1], mine, other)


def run_embed_grads(ids, bit, after, *arrays):
    return call(
        3,
        embed_grads_body,
        [((1024, 512), bf16)] * 2 + [TOKEN],
        [((2, 1024, 512), bf16)],
        ids.at[5].set(bit),
        arrays,
        after,
    )


def on_device(
    embeddings,
    page_images,
    token_boxes,
    segment_ids,
    down_first,
    down_second,
    down_third,
    down_fourth,
    down_fifth,
    up_fourth,
    up_third,
    up_second,
    up_first,
    roi_proj,
    gain_attn,
    w_query,
    w_key,
    w_value,
    w_output,
    bias_table,
    gain_ffn,
    ffn_in,
    ffn_out,
    cotangent,
):
    tok_rows = embeddings.shape[1]
    model_width = embeddings.shape[2]
    tile_rows = page_images.shape[2]
    my_tile = lax.axis_index("tile")
    tile_count = lax.axis_size("tile")
    score_scale = HD ** (-0.5)
    cut = tile_count > 12
    window = 12 if cut else tile_count
    place = 6 if cut else my_tile
    ids = jnp.stack(
        [
            my_tile,
            jnp.asarray(tile_rows * tile_count, my_tile.dtype),
            jnp.asarray(place, my_tile.dtype),
            my_tile - place,
            jnp.asarray(2 if cut else my_tile, my_tile.dtype),
            jnp.asarray(0, my_tile.dtype),
        ]
    ).astype(jnp.int32)

    def gathered(block):
        copies = jnp.broadcast_to(block[None], (tile_count, *block.shape))
        return lax.all_to_all(copies, "tile", 0, 0, tiled=True)

    def windowed(block):
        if not cut:
            return gathered(block)
        blocks = lax.all_gather(block, "tile", axis=0)
        blocks = jnp.pad(blocks, ((6, 6), (0, 0), (0, 0)))
        return lax.dynamic_slice_in_dim(blocks, my_tile, window, 0)

    def from_side(block, step):
        hops = [
            (source, source + step) for source in range(tile_count) if 0 <= source + step < tile_count
        ]
        return lax.ppermute(block, "tile", hops)

    def lined(weight):
        return weight.transpose(0, 2, 1, 3).reshape(3, weight.shape[2], -1)

    def lined_back(weight):
        flipped = weight[::-1, ::-1]
        return flipped.transpose(0, 3, 1, 2).reshape(3, weight.shape[3], -1)

    def beside(table, count):
        return jnp.concatenate(jnp.split(table, count, axis=0), axis=1)

    def below(table, count):
        return jnp.concatenate(jnp.split(table, count, axis=1), axis=0)

    def as_rows(member):
        return member.reshape(-1, member.shape[-1])

    def bit_of(axis, mask):
        return (lax.axis_index(axis) & mask) // mask

    def swapped(block, axis, mask):
        hops = [(source, source ^ mask) for source in range(lax.axis_size(axis))]
        return lax.ppermute(block, axis, hops)

    def halved(halves, step, *after):
        mine, other, _ = halves
        got = swapped(other, *HOPS[step])
        if step + 1 == len(HOPS):
            return run_finish(ids, mine, got, after)
        return run_halve(ids, bit_of(*HOPS[step + 1]), mine, got, after)

    line = page_images.shape[3]
    meta = jnp.concatenate([token_boxes[:, 0], segment_ids])
    digits = jnp.concatenate([meta // 256, meta % 256, jnp.zeros((2, tok_rows), jnp.int32)])
    digits = digits.astype(jnp.bfloat16).reshape(24, -1)
    sheet = jnp.concatenate([page_images[0].reshape(24, -1), digits], axis=1)
    sheets = gathered(sheet)
    digits_all = sheets[:, :, 2 * line :].reshape(tile_count, 12, tok_rows)
    digits_all = digits_all.transpose(1, 0, 2).reshape(12, -1).astype(jnp.int32)
    meta_all = jnp.pad(digits_all[:5] * 256 + digits_all[5:10], ((0, 3), (0, 0)))
    if cut:
        sheets = jnp.pad(sheets, ((2, 2), (0, 0), (0, 0)))
        sheets = lax.dynamic_slice_in_dim(sheets, my_tile, 5, 0)
    left_all, top_all, right_all, bottom_all, seg_all = (meta_all[n] for n in range(5))
    box_rows = meta_all.T
    seq_all = seg_all.shape[0]
    w_zero = jnp.pad(down_first.transpose(2, 0, 1, 3), ((0, 0), (0, 0), (0, 0), (0, 5)))
    w_zero = w_zero.reshape(w_zero.shape[0], -1)
    pre_zero, pre_one, p_one, pre_two, p_two, p_three, page_own = run_down(
        ids, sheets, w_zero, lined(down_second), lined(down_third)
    )
    p_three_all = windowed(p_three)
    pre_three, pre_four, p_four, e_four, pre_up_three, dec_three = run_bottom(
        cut, ids, p_three_all, down_fourth, down_fifth, up_fourth
    )
    pre_up_two, pre_up_one, pre_up_zero, u_three, dec_two, dec_one, features = run_up(
        ids, dec_three, pre_two, pre_one, pre_zero, up_third, lined(up_second), lined(up_first)
    )
    pooled_own = run_pool(ids, box_rows, features, 256)
    pieces = lax.all_to_all(
        pooled_own.reshape(tile_count, tok_rows, -1), "tile", 0, 0, tiled=True
    )
    gain_row_one = gain_attn.reshape(1, -1)
    gain_row_two = gain_ffn.reshape(1, -1)
    heads_first = tile_count == HEADS
    if heads_first:
        tall = tile_rows * tile_count
        residual, normed_low, pooled_low, shared = run_embed(
            ids, pieces, embeddings[0], roi_proj, gain_row_one, w_query, w_key, w_value
        )
        shared = lax.all_to_all(shared, "tile", 0, 0, tiled=True)
        prob, found_low, found_full = run_attend(
            tall, ids, bias_table.astype(jnp.float32), meta_all, box_rows, shared
        )
        found = lax.all_to_all(found_low, "tile", 0, 0, tiled=True)
        result_low, act_low, d_pre, ffn_low, d_mixed, d_mixed_low, d_found, grad_gain_ffn = run_mixer(
            ids, found, residual, cotangent[0], w_output, gain_row_two, ffn_in, ffn_out
        )
        d_found = lax.all_to_all(d_found, "tile", 0, 0, tiled=True)
        mixer_halves = run_mixer_grads(
            ids, bit_of(*HOPS[0]), found, act_low, d_pre, ffn_low, d_mixed_low, cotangent[0]
        )
        mixer_halves = halved(mixer_halves, 0)
        d_shared, d_table = run_attend_back(
            tall, ids, mixer_halves[2:], meta_all, shared, prob, found_full, d_found
        )
        d_shared = lax.all_to_all(d_shared, "tile", 0, 0, tiled=True)
        d_residual, d_resid_low, d_pooled, grad_gain_attn, d_rows, embed_token = run_embed_back(
            ids, d_shared, residual, d_mixed, gain_row_one, w_query, w_key, w_value, roi_proj
        )
        embed_halves = run_embed_grads(
            ids,
            bit_of(*HOPS[0]),
            (),
            normed_low,
            d_rows,
            pooled_low,
            d_resid_low,
            grad_gain_attn,
            grad_gain_ffn,
            d_table,
        )
        mixer_halves = halved(mixer_halves, 1, embed_token)
        mixer_halves = halved(mixer_halves, 2)
        embed_halves = halved(embed_halves, 0)
        ordering = (embed_halves[2], mixer_halves[2])
    else:
        ordering = ()
        pooled_low = jnp.sum(pieces.astype(jnp.float32), axis=0).astype(jnp.bfloat16)
        residual = embeddings[0].astype(jnp.float32) + jnp.dot(
            pooled_low, roi_proj, preferred_element_type=jnp.float32
        )
        gain_one = gain_attn.astype(jnp.float32)
        normed_low = rms_scale(residual, gain_one).astype(jnp.bfloat16)
        query_low = jnp.dot(normed_low, w_query, preferred_element_type=jnp.float32).astype(
            jnp.bfloat16
        )
        key_low = jnp.dot(normed_low, w_key, preferred_element_type=jnp.float32).astype(jnp.bfloat16)
        value_low = jnp.dot(normed_low, w_value, preferred_element_type=jnp.float32).astype(
            jnp.bfloat16
        )

        def to_heads(flat_rows):
            return flat_rows.reshape(tok_rows, HEADS, HD).transpose(1, 0, 2)

        def from_heads(head_rows):
            return head_rows.transpose(1, 0, 2).reshape(tok_rows, model_width)

        query_heads = to_heads(query_low)
        own_keys = to_heads(key_low)
        own_values = to_heads(value_low)
        key_all, value_all = (
            lax.all_gather(own_keys, "tile", axis=1, tiled=True),
            lax.all_gather(own_values, "tile", axis=1, tiled=True),
        )
        center_x = (left_all + right_all) // 2
        center_y = (top_all + bottom_all) // 2
        key_meta = (jnp.arange(seq_all), center_x, center_y, seg_all)
        first_tok = my_tile * tok_rows
        query_meta = tuple(
            (lax.dynamic_slice_in_dim(member, first_tok, tok_rows, 0) for member in key_meta)
        )
        key_block = math.gcd(seq_all, 1024)
        block_count = seq_all // key_block

        def key_slice(block_id):
            first_key = block_id * key_block
            keys_blk = lax.dynamic_slice_in_dim(key_all, first_key, key_block, 1)
            values_blk = lax.dynamic_slice_in_dim(value_all, first_key, key_block, 1)
            meta_blk = tuple(
                (lax.dynamic_slice_in_dim(member, first_key, key_block, 0) for member in key_meta)
            )
            return (keys_blk, values_blk, meta_blk)

        def stats_step(running, block_id):
            run_max, run_sum = running
            keys_blk, values_blk, meta_blk = key_slice(block_id)
            scores, allowed, one_hot = block_scores(
                query_heads, keys_blk, query_meta, meta_blk, bias_table, score_scale
            )
            scores = jnp.where(allowed[None], scores, neg_large)
            new_max = jnp.maximum(run_max, jnp.max(scores, axis=-1))
            run_sum = run_sum * jnp.exp(run_max - new_max) + jnp.sum(
                jnp.exp(scores - new_max[..., None]), axis=-1
            )
            return ((new_max, run_sum), None)

        start_stats = (
            jnp.full((HEADS, tok_rows), neg_large, jnp.float32),
            jnp.zeros((HEADS, tok_rows), jnp.float32),
        )
        (run_max, run_sum), _ = lax.scan(stats_step, start_stats, jnp.arange(block_count))
        log_total = run_max + jnp.log(run_sum)

        def out_step(attn_acc, block_id):
            keys_blk, values_blk, meta_blk = key_slice(block_id)
            scores, allowed, one_hot = block_scores(
                query_heads, keys_blk, query_meta, meta_blk, bias_table, score_scale
            )
            attn_prob = jnp.where(allowed[None], jnp.exp(scores - log_total[..., None]), 0.0)
            attn_acc = attn_acc + jnp.einsum(
                "hqk,hkd->hqd",
                attn_prob.astype(jnp.bfloat16),
                values_blk,
                preferred_element_type=jnp.float32,
            )
            return (attn_acc, None)

        attn_heads, _ = lax.scan(
            out_step, jnp.zeros((HEADS, tok_rows, HD), jnp.float32), jnp.arange(block_count)
        )
        attn_low = from_heads(attn_heads).astype(jnp.bfloat16)
        mixed_rows = residual + jnp.dot(attn_low, w_output, preferred_element_type=jnp.float32)
        gain_two = gain_ffn.astype(jnp.float32)
        ffn_low = rms_scale(mixed_rows, gain_two).astype(jnp.bfloat16)
        pre_ffn = jnp.dot(ffn_low, ffn_in, preferred_element_type=jnp.float32)
        act_low = jax.nn.gelu(pre_ffn).astype(jnp.bfloat16)
        result_rows = mixed_rows + jnp.dot(act_low, ffn_out, preferred_element_type=jnp.float32)
        upstream = cotangent[0]
        grad_ffn_out = jnp.einsum("tf,td->fd", act_low, upstream, preferred_element_type=jnp.float32)
        d_act = jnp.einsum("td,fd->tf", upstream, ffn_out, preferred_element_type=jnp.float32)
        d_pre = gelu_back(pre_ffn, d_act).astype(jnp.bfloat16)
        grad_ffn_in = jnp.einsum("td,tf->df", ffn_low, d_pre, preferred_element_type=jnp.float32)
        d_ffn_norm = jnp.einsum("tf,df->td", d_pre, ffn_in, preferred_element_type=jnp.float32)
        d_mixed_norm, grad_gain_ffn = jax.vjp(rms_scale, mixed_rows, gain_two)[1](d_ffn_norm)
        d_mixed = upstream.astype(jnp.float32) + d_mixed_norm
        d_mixed_low = d_mixed.astype(jnp.bfloat16)
        grad_output = jnp.einsum("tc,td->cd", attn_low, d_mixed_low, preferred_element_type=jnp.float32)
        d_attn = jnp.einsum(
            "td,cd->tc", d_mixed_low, w_output, preferred_element_type=jnp.float32
        ).astype(jnp.bfloat16)
        dout_heads = to_heads(d_attn)
        row_delta = jnp.sum(dout_heads.astype(jnp.float32) * attn_heads, axis=-1)

        def back_step(running, block_id):
            keys_blk, values_blk, meta_blk = key_slice(block_id)
            scores, allowed, one_hot = block_scores(
                query_heads, keys_blk, query_meta, meta_blk, bias_table, score_scale
            )
            attn_prob = jnp.where(allowed[None], jnp.exp(scores - log_total[..., None]), 0.0)
            d_prob = jnp.einsum(
                "hqd,hkd->hqk", dout_heads, values_blk, preferred_element_type=jnp.float32
            )
            d_score = (attn_prob * (d_prob - row_delta[..., None])).astype(jnp.bfloat16)
            query_acc = running[0] + jnp.einsum(
                "hqk,hkd->hqd", d_score, keys_blk, preferred_element_type=jnp.float32
            )
            table_acc = running[1] + jnp.einsum(
                "hqk,qkn->hn", d_score, one_hot, preferred_element_type=jnp.float32
            )
            first_key = block_id * key_block
            key_part = (
                jnp.einsum("hqk,hqd->hkd", d_score, query_heads, preferred_element_type=jnp.float32)
                * score_scale
            )
            value_part = jnp.einsum(
                "hqk,hqd->hkd",
                attn_prob.astype(jnp.bfloat16),
                dout_heads,
                preferred_element_type=jnp.float32,
            )
            key_acc = lax.dynamic_update_slice_in_dim(running[2], key_part, first_key, 1)
            value_acc = lax.dynamic_update_slice_in_dim(running[3], value_part, first_key, 1)
            return ((query_acc, table_acc, key_acc, value_acc), None)

        start_back = (
            jnp.zeros((HEADS, tok_rows, HD), jnp.float32),
            jnp.zeros((HEADS, 3 * NB), jnp.float32),
        )
        start_back = start_back + (
            jnp.zeros((HEADS, seq_all, HD), jnp.float32),
            jnp.zeros((HEADS, seq_all, HD), jnp.float32),
        )
        back_out, _ = lax.scan(back_step, start_back, jnp.arange(block_count))
        query_acc = back_out[0]
        grad_bias_table = back_out[1]
        key_grad, value_grad = (
            lax.psum_scatter(back_out[2], "tile", scatter_dimension=1, tiled=True),
            lax.psum_scatter(back_out[3], "tile", scatter_dimension=1, tiled=True),
        )
        dq_low = from_heads(query_acc * score_scale).astype(jnp.bfloat16)
        dk_low = from_heads(key_grad).astype(jnp.bfloat16)
        dv_low = from_heads(value_grad).astype(jnp.bfloat16)
        grad_query = jnp.einsum("td,te->de", normed_low, dq_low, preferred_element_type=jnp.float32)
        grad_key = jnp.einsum("td,te->de", normed_low, dk_low, preferred_element_type=jnp.float32)
        grad_value = jnp.einsum("td,te->de", normed_low, dv_low, preferred_element_type=jnp.float32)
        d_normed = (
            jnp.einsum("te,de->td", dq_low, w_query, preferred_element_type=jnp.float32)
            + jnp.einsum("te,de->td", dk_low, w_key, preferred_element_type=jnp.float32)
            + jnp.einsum("te,de->td", dv_low, w_value, preferred_element_type=jnp.float32)
        )
        d_resid_norm, grad_gain_attn = jax.vjp(rms_scale, residual, gain_one)[1](d_normed)
        d_residual = d_mixed + d_resid_norm
        d_resid_low = d_residual.astype(jnp.bfloat16)
        grad_roi_proj = jnp.einsum(
            "tp,td->pd", pooled_low, d_resid_low, preferred_element_type=jnp.float32
        )
        d_pooled = jnp.einsum("td,pd->tp", d_resid_low, roi_proj, preferred_element_type=jnp.float32)
        d_pooled = d_pooled.astype(jnp.bfloat16)
        result_low = result_rows.astype(jnp.bfloat16)
        mixer_table = jnp.concatenate([grad_ffn_out, below(grad_ffn_in, 4), grad_output], axis=0)
        mixer_table = mixer_table.astype(jnp.bfloat16)
        chart = grad_bias_table.reshape(HEADS, 3, NB).transpose(2, 0, 1).reshape(NB, 3 * HEADS)
        embed_table = jnp.concatenate(
            [
                grad_query,
                grad_key,
                grad_value,
                grad_roi_proj,
                jnp.pad(jnp.stack([grad_gain_attn, grad_gain_ffn]), ((0, 14), (0, 0))),
                jnp.pad(chart, ((0, 80), (0, model_width - 3 * HEADS))),
            ],
            axis=0,
        ).astype(jnp.bfloat16)
    d_pooled_all = gathered(d_pooled).reshape(seq_all, -1)
    d_features, low_zero_up, low_end, low_start, box_token = run_unpool(
        ids, ordering, box_rows, d_pooled_all, pre_up_zero, 256
    )
    if heads_first:
        mixer_halves = halved(mixer_halves, 3, box_token)
        embed_halves = halved(embed_halves, 1, box_token)
        ordering = (embed_halves[2], mixer_halves[2])
    d_dec_one, d_dec_two, d_dec_three, low_one_up, low_two_up, up_token = run_up_back(
        ids,
        ordering,
        from_side(low_end, 1),
        low_zero_up,
        from_side(low_start, -1),
        pre_up_one,
        pre_up_two,
        lined_back(up_first),
        lined_back(up_second),
        up_third,
    )
    d_dec_three_all = windowed(d_dec_three)
    grad_up_first = run_grad_up_first(ids, (up_token,), dec_one, low_zero_up)
    light_early, early_token = run_grad_up(ids, (), grad_up_first, dec_two, low_one_up, u_three, low_two_up)
    if heads_first:
        mixer_share = halved(mixer_halves, 4, up_token)
        embed_halves = halved(embed_halves, 2, up_token)
        ordering = embed_halves[2:]
    low_three_up, low_four, low_three, d_pool_three, bottom_token = run_bottom_back(
        cut,
        ids,
        (*ordering, early_token),
        d_dec_three_all,
        pre_up_three,
        pre_four,
        pre_three,
        up_fourth,
        down_fifth,
        down_fourth,
    )
    dp_count = lax.axis_size(PAGES)
    if heads_first:
        embed_halves = halved(embed_halves, 3, bottom_token)
        early_parts = lax.all_to_all(
            light_early.reshape(32, -1, 256), (*PAGES, "tile"), 0, 0, tiled=True
        )
        early_share, early_done = run_total(ids, early_parts)
        ordering = (embed_halves[2], early_done)
    bottom_parts = (low_three_up, e_four, low_four, p_four, low_three, p_three_all)
    if cut:
        heavy = run_grad_bottom_all(ids, *bottom_parts)
        heavy_token = ()
    else:
        heavy, *heavy_token = run_grad_bottom(tile_count, dp_count, ids, ordering, *bottom_parts)
    low_two, low_one, low_zero = run_down_back(
        ids,
        heavy_token,
        d_pool_three,
        d_dec_two,
        pre_two,
        d_dec_one,
        pre_one,
        d_features,
        pre_zero,
        down_third,
        lined_back(down_second),
    )
    light_late = run_grad_down(ids, p_two, low_two, p_one, low_one, page_own, low_zero)
    both_axes = (*PAGES, "tile")
    device_total = dp_count * tile_count

    def summed_share(table):
        parts = table.reshape(device_total, -1, table.shape[1])
        parts = lax.all_to_all(parts, both_axes, 0, 0, tiled=True)
        return jnp.sum(parts.astype(jnp.float32), axis=0).astype(jnp.bfloat16)

    def spread_out(share):
        copies = jnp.broadcast_to(share[None], (device_total, *share.shape))
        return lax.all_to_all(copies, both_axes, 0, 0, tiled=True)

    late = spread_out(summed_share(light_late)).reshape(light_late.shape).astype(jnp.float32)
    wide = ffn_in.shape[1]
    if heads_first:
        embed_share = halved(embed_halves, 4)
        parts = lax.all_to_all(heavy, PAGES, 0, 0, tiled=True)
        share = run_gather(ids, parts, embed_share, early_share)
        mixer_all = lax.all_gather(mixer_share, both_axes, axis=0)
        whole = lax.all_gather(share, both_axes, axis=0)
        sum_ffn_out, sum_ffn_in, sum_output = run_unpack(
            mixer_all, False, [(2048, 512, 64), (512, 2048, 64), (512, 512, 16)]
        )
        *heavy_sums, sum_query, sum_key, sum_value, rest, early = run_unpack(
            whole, True, [(512, 512, 16)] * 4
        )
        rest = rest.reshape(NB, 16, model_width)
        sum_roi = rest[:, :4].reshape(-1, model_width)
        sum_bias = rest[:, 4, : 3 * HEADS].reshape(NB, HEADS, 3)
        sum_gain_attn, sum_gain_ffn = rest[0, 5], rest[0, 6]
    else:
        early = spread_out(summed_share(light_early)).reshape(light_early.shape)
        early = early.astype(jnp.float32)
        heavy_sums = [lax.psum(member, both_axes).astype(jnp.float32) for member in heavy]
        mixer_all = lax.psum(mixer_table, both_axes).astype(jnp.float32)
        embed_all = lax.psum(embed_table, both_axes).astype(jnp.float32)
        sum_ffn_out = mixer_all[:wide]
        sum_ffn_in = beside(mixer_all[wide : 2 * wide], wide // model_width)
        sum_output = mixer_all[2 * wide :]
        sum_query, sum_key, sum_value = (
            embed_all[n * model_width : (n + 1) * model_width] for n in range(3)
        )
        last = 3 * model_width + roi_proj.shape[0]
        sum_roi = embed_all[3 * model_width : last]
        sum_bias = embed_all[last + 16 : last + 16 + NB, : 3 * HEADS].reshape(NB, HEADS, 3)
        sum_gain_attn, sum_gain_ffn = embed_all[last], embed_all[last + 1]
    sum_bias = sum_bias.transpose(1, 2, 0).reshape(bias_table.shape)

    def unlined(table, kind):
        return table.reshape(3, kind.shape[2], 3, kind.shape[3]).transpose(0, 2, 1, 3)

    second_rest = below(early[1344:1440], 2)
    sum_up_second = jnp.concatenate([early[1152:1344], second_rest], axis=1)
    sum_down_second = jnp.concatenate([late[384:480, :96], late[384:480, 128:224]], axis=0)
    sum_first = late[480:512, :72].reshape(32, 3, 3, 8)[..., :3].transpose(1, 2, 0, 3)
    summed = [
        sum_first,
        unlined(sum_down_second, down_second),
        unlined(late[:384, :192], down_third),
        heavy_sums[2].reshape(down_fourth.shape),
        heavy_sums[1].reshape(down_fifth.shape),
        heavy_sums[0].reshape(up_fourth.shape),
        early[:1152].reshape(up_third.shape),
        unlined(sum_up_second, up_second),
        unlined(early[1440:1536, :192], up_first),
        sum_roi,
        sum_gain_attn,
        sum_query,
        sum_key,
        sum_value,
        sum_output,
        sum_bias,
        sum_gain_ffn,
        sum_ffn_in,
        sum_ffn_out,
    ]
    return (
        result_low[None],
        d_residual[None],
        summed[0],
        summed[1],
        summed[2],
        summed[3],
        summed[4],
        summed[5],
        summed[6],
        summed[7],
        summed[8],
        summed[9],
        summed[10],
        summed[11],
        summed[12],
        summed[13],
        summed[14],
        summed[15],
        summed[16],
        summed[17],
        summed[18],
    )


def solution(mesh):
    tiles = mesh.shape["tile"]
    split = Mesh(mesh.devices.reshape(mesh.shape["dp"] // 2, 2, tiles), (*PAGES, "tile"))
    return jax.shard_map(
        on_device,
        mesh=split,
        in_specs=(
            P(PAGES, "tile", None),
            P(PAGES, None, "tile", None),
            P(None, PAGES, "tile"),
            P(PAGES, "tile"),
            P(),
            P(),
            P(),
            P(),
            P(),
            P(),
            P(),
            P(),
            P(),
            P(),
            P(),
            P(),
            P(),
            P(),
            P(),
            P(),
            P(),
            P(),
            P(),
            P(PAGES, "tile", None),
        ),
        out_specs=(
            P(PAGES, "tile", None),
            P(PAGES, "tile", None),
            P(),
            P(),
            P(),
            P(),
            P(),
            P(),
            P(),
            P(),
            P(),
            P(),
            P(),
            P(),
            P(),
            P(),
            P(),
            P(),
            P(),
            P(),
            P(),
        ),
        check_vma=False,
    )
```

time: 1700 us -> 458 us (0.27); the launches traced: 1680 us -> 452 us
  blocking collectives: 478 us -> 34.8 us
  local copies, waits for them, and re-layouts: 408 us -> 33.4 us
  waiting for transfers between devices: 387 us -> 131 us
  matrix products: 202 us -> 0 us
  Pallas kernels: 0 us -> 170 us
  other arithmetic: 72.9 us -> 1 us
  starting transfers between devices: 108 us -> 65.7 us
    unnamed x1 -> x0, blocking collectives: 407 us -> none
    unnamed x6 -> x2, waiting for transfers between devices: 228 us -> 0.03 us
    concatenate x2, local copies, waits for them, and re-layouts: 218 us -> 0.16 us  [the longest x1 0.09 us: on_device(): jnp.concatenate([late[384:480, :96], late[384:480, 128:224]], axis=0)]
    dot_general x267 -> x0, matrix products: 202 us -> none  [the longest x81 45.7 us: conv_apply(): jnp.einsum('oc,chw->ohw', weight[row_off, col_off], window, preferred_ele...]
    pallas_call x0 -> x33, Pallas kernels: none -> 170 us  [the longest x31 144 us: call(): pl.pallas_call(ordered, cost_estimate=price(micros), out_shape=[pltpu.HBM...]
    reduce_scatter x2 -> x0, waiting for transfers between devices: 93.2 us -> none  [the longest x1 69 us: on_device(): lax.psum_scatter(back_out[2], 'tile', scatter_dimension=1, tiled=True)]
    ppermute x34 -> x12, starting transfers between devices: 103 us -> 17.6 us  [the longest x10 12.4 us: swapped(): return lax.ppermute(block, axis, hops)]
    all_gather x3 -> x0, blocking collectives: 70.9 us -> none  [the longest x1 30.8 us: on_device(): lax.all_gather(d_pooled.astype(jnp.bfloat16), 'tile', axis=0, tiled=True)]
  transfers between devices with their start and end apart: 40 -> 25, of which waited for: 20 -> 17; matrix products, arithmetic and copies ran while one was open for 8% -> 3% of each run, Pallas kernels for 0% -> 19%
where the time goes in v1:
time: 458 us; the launch traced here: 452 us
  Pallas kernels  170 us (37%)
  waiting for transfers between devices  131 us (29%)
  starting transfers between devices  65.7 us (14%)
  blocking collectives  34.8 us (8%)
  local copies, waits for them, and re-layouts  33.4 us (7%)
  between operations  15.3 us (3%)
    pallas_call x31, Pallas kernels, call(): pl.pallas_call(ordered, cost_estimate=price(micros), out_shape=[pltpu.HBM...  144 us
    ppermute x10, waiting for transfers between devices, swapped(): return lax.ppermute(block, axis, hops)  39.3 us
    pallas_call x2, Pallas kernels, run_unpack(): pl.pallas_call(functools.partial(unpack_body, split), cost_estimate=price...  26.2 us
    all_gather x1, waiting for transfers between devices, on_device(): whole = lax.all_gather(share, both_axes, axis=0)  24.4 us
    all_to_all x4, starting transfers between devices, gathered(): return lax.all_to_all(copies, 'tile', 0, 0, tiled=True)  22.3 us
    all_to_all x4, waiting for transfers between devices, gathered(): return lax.all_to_all(copies, 'tile', 0, 0, tiled=True)  21.6 us
    all_to_all x1, blocking collectives, spread_out(): return lax.all_to_all(copies, both_axes, 0, 0, tiled=True)  19.5 us
    unnamed x118, local copies, waits for them, and re-layouts  15.5 us
  transfers between devices with their start and end apart: 25, of which 17 were waited for; matrix products, arithmetic and copies ran while one was open for 3% of the time, Pallas kernels for 19%

profile of v1, /device:TPU:0, one launch (start us, length us, event | category | flops | bytes accessed | tf_op | source)
XLA Modules:
  0.0 451.8 jit_solution(16732974023100471437)
XLA Ops:
  9.8 7.3 %all-to-all-start = ((bf16[8,24,1088]{2,1,0:T(8,128)(2,1)}), bf16[8,24,1088]{2,1,0:T(8,128)(2,1)S(1)}, u32[]{:S(2)}, u32[]{:S(2)}) async-start(bf16[8,24,1088]{2,1,0:T(8,128)(2,1)} %broadcast_in_dim.17), calls=%async_computation | async-start | bytes 884736 | tf_op jit(solution)/shard_map/all_to_all | solution.py:1623
  21.1 8.7 %all-to-all-done.refs_1_ = bf16[8,24,1088]{2,1,0:T(8,128)(2,1)S(1)} async-done(((bf16[8,24,1088]{2,1,0:T(8,128)(2,1)}), bf16[8,24,1088]{2,1,0:T(8,128)(2,1)S(1)}, u32[]{:S(2)}, u32[]{:S(2)}) %all-to-all-start) | async-done | bytes 417824 | tf_op jit(solution)/shard_map/all_to_all | solution.py:1623
  29.9 11.3 %shard_map.391 = (bf16[32,8192]{1,0:T(8,128)(2,1)}, bf16[64,4096]{1,0:T(8,128)(2,1)}, bf16[32,2560]{1,0:T(8,128)(2,1)}, bf16[128,1280]{1,0:T(8,128)(2,1)}, bf16[...) custom-call(s32[6]{0:T(128)S(1)} %stack.9.refs_0_, ...), custom_call_target="tpu_custom_call" | custom-call | flops 5000000000 | bytes 20000000 | tf_op jit(solution)/shard_map/pallas_call | solution.py:216
  48.3 6.7 %all-to-all-done.1.refs_1_.refs_6_ = bf16[8,128,128]{2,1,0:T(8,128)(2,1)S(1)} async-done(((bf16[8,128,128]{2,1,0:T(8,128)(2,1)}), bf16[8,128,128]{2,1,0:T(8,128)(2,1)S(1)}, u32[]{:S(2)}, u32[]{:S(2)}) %all-to-all-start.1) | async-done | bytes 262176 | tf_op jit(solution)/shard_map/all_to_all | solution.py:1623
  55.0 10.0 %shard_map.392 = (bf16[256,1024]{1,0:T(8,128)(2,1)}, bf16[512,256]{1,0:T(8,128)(2,1)}, bf16[256,256]{1,0:T(8,128)(2,1)}, bf16[512,256]{1,0:T(8,128)(2,1)}, bf16[...) custom-call(s32[6]{0:T(128)S(1)} %stack.9.refs_0_, bf16[8,128,128]{2,1,0:T(8,128)(2,1)S(1)} %all-to-all-done.1.refs_1_.refs_6_, ...), custom_call_target="tpu_custom_call" | custom-call | flops 5500000256 | bytes 22000000 | tf_op jit(solution)/shard_map/pallas_call | solution.py:216
  65.0 9.3 %shard_map.393 = (bf16[128,1280]{1,0:T(8,128)(2,1)}, bf16[64,4608]{1,0:T(8,128)(2,1)}, bf16[32,8192]{1,0:T(8,128)(2,1)}, bf16[256,768]{1,0:T(8,128)(2,1)}, bf16[...) custom-call(s32[6]{0:T(128)S(1)} %stack.9.refs_0_, ...), custom_call_target="tpu_custom_call" | custom-call | flops 4499999744 | bytes 18000000 | tf_op jit(solution)/shard_map/pallas_call | solution.py:216
  74.4 7.7 %shard_map.394 = bf16[1024,128]{1,0:T(8,128)(2,1)} custom-call(s32[6]{0:T(128)S(1)} %stack.9.refs_0_, s32[1024,8]{1,0:T(8,128)S(1)} %pad_bitcast_fusion.refs_1_.refs_3_, bf16[512,512]{1,0:T(8,128)(2,1)S(1)} %get-tuple-element.232.refs_2_), custom_call_target="tpu_custom_call" | custom-call | flops 4000000000 | bytes 16000000 | tf_op jit(solution)/shard_map/pallas_call | solution.py:216
  85.8 8.5 %all-to-all-done.2.refs_1_ = bf16[8,128,128]{2,1,0:T(8,128)(2,1)S(1)} async-done(((bf16[8,128,128]{2,1,0:T(8,128)(2,1)}), bf16[8,128,128]{2,1,0:T(8,128)(2,1)S(1)}, u32[]{:S(2)}, u32[]{:S(2)}) %all-to-all-start.2) | async-done | bytes 262176 | tf_op jit(solution)/shard_map/all_to_all | solution.py:1696
  101.2 9.9 %all-to-all-done.3.refs_4_.refs_2_ = bf16[8,192,128]{2,1,0:T(8,128)(2,1)S(1)} async-done(((bf16[8,192,128]{2,1,0:T(8,128)(2,1)}), bf16[8,192,128]{2,1,0:T(8,128)(2,1)S(1)}, u32[]{:S(2)}, u32[]{:S(2)}) %all-to-all-start.3) | async-done | bytes 393248 | tf_op jit(solution)/shard_map/all_to_all | solution.py:1707
  111.1 10.3 %shard_map.396 = (bf16[4,1024,256]{2,1,0:T(8,128)(2,1)}, bf16[8,64,128]{2,1,0:T(8,128)(2,1)}, f32[64,1024]{1,0:T(8,128)}) custom-call(s32[6]{0:T(128)S(1)} %stack.9.refs_0_, f32[8,96]{1,0:T(8,128)S(1)} %convert_element_type.28.refs_1_, s32[8,1024]{1,0:T(8,128)S(1)} %pad.23.clone.refs_2_.refs_1_, s32[1024,8]{1,0:T(8,128)S(1)} %pad_bitcast_fusion.refs_1_.refs_3_, ...), custom_call_target="tpu_custom_call" | custom-call | flops 4499999744 | bytes 18000000 | tf_op jit(solution)/shard_map/pallas_call | solution.py:216
  125.1 7.3 %all-to-all-done.4.refs_1_ = bf16[8,64,128]{2,1,0:T(8,128)(2,1)S(1)} async-done(((bf16[8,64,128]{2,1,0:T(8,128)(2,1)}), bf16[8,64,128]{2,1,0:T(8,128)(2,1)S(1)}, u32[]{:S(2)}, u32[]{:S(2)}) %all-to-all-start.4) | async-done | bytes 131104 | tf_op jit(solution)/shard_map/all_to_all | solution.py:1711
  132.4 5.9 %shard_map.397 = (bf16[128,512]{1,0:T(8,128)(2,1)}, bf16[128,2048]{1,0:T(8,128)(2,1)S(1)}, bf16[128,2048]{1,0:T(8,128)(2,1)S(1)}, bf16[128,512]{1,0:T(8,128)(2,1...) custom-call(s32[6]{0:T(128)S(1)} %stack.9.refs_0_, ...), custom_call_target="tpu_custom_call" | custom-call | flops 2500000000 | bytes 10000000 | tf_op jit(solution)/shard_map/pallas_call | solution.py:216
  156.0 8.0 %shard_map.400 = (bf16[8,192,128]{2,1,0:T(8,128)(2,1)}, f32[32,128]{1,0:T(8,128)S(1)}) custom-call(s32[6]{0:T(128)S(1)} %stack.9.refs_0_, s32[8,1024]{1,0:T(8,128)S(1)} %copy-done.7, bf16[8,192,128]{2,1,0:T(8,128)(2,1)S(1)} %copy-done.3, bf16[4,1024,256]{2,1,0:T(8,128)(2,1)} %get-tuple-element.237.refs_3_, f32[64,1024]{1,0:T(8,128)} %get-tuple-element.238.refs_4_, ...), custom_call_target="tpu_custom_call" | custom-call | flops 3000000000 | bytes 12000000 | tf_op jit(solution)/shard_map/pallas_call | solution.py:216
  169.1 9.8 %all-to-all-done.6.refs_1_ = bf16[8,192,128]{2,1,0:T(8,128)(2,1)S(1)} async-done(((bf16[8,192,128]{2,1,0:T(8,128)(2,1)}), bf16[8,192,128]{2,1,0:T(8,128)(2,1)S(1)}, u32[]{:S(2)}, u32[]{:S(2)}) %all-to-all-start.6) | async-done | bytes 393248 | tf_op jit(solution)/shard_map/all_to_all | solution.py:1723
  188.2 6.7 %collective-permute-done.2.refs_2_ = bf16[1152,512]{1,0:T(8,128)(2,1)S(1)} collective-permute-done((bf16[1152,512]{1,0:T(8,128)(2,1)}, bf16[1152,512]{1,0:T(8,128)(2,1)S(1)}, u32[]{:S(2)}, u32[]{:S(2)}) %collective-permute-start.2) | collective-permute-done | bytes 1179680 | tf_op jit(solution)/shard_map/ppermute | solution.py:1659
  208.1 5.5 %collective-permute-done.3.refs_2_ = bf16[576,512]{1,0:T(8,128)(2,1)S(1)} collective-permute-done((bf16[576,512]{1,0:T(8,128)(2,1)}, bf16[576,512]{1,0:T(8,128)(2,1)S(1)}, u32[]{:S(2)}, u32[]{:S(2)}) %collective-permute-start.3) | collective-permute-done | bytes 589856 | tf_op jit(solution)/shard_map/ppermute | solution.py:1659
  217.2 7.9 %shard_map.406 = (f32[32,8192]{1,0:T(8,128)}, bf16[32,8192]{1,0:T(8,128)(2,1)S(1)}, bf16[32,5632]{1,0:T(8,128)(2,1)S(1)}, bf16[32,5632]{1,0:T(8,128)(2,1)S(1)}, f32[8,128]{1,0:T(8,128)}) custom-call(s32[6]{0:T(128)S(1)} %stack.9.refs_0_, s32[1024,8]{1,0:T(8,128)S(1)} %copy-done.1, bf16[1024,128]{1,0:T(8,128)(2,1)S(1)} %bitcast.70, ...), custom_call_target="tpu_custom_call" | custom-call | flops 4000000000 | bytes 16000000 | tf_op jit(solution)/shard_map/pallas_call | solution.py:216
  241.6 10.4 %shard_map.409 = (f32[64,4608]{1,0:T(8,128)}, f32[128,1024]{1,0:T(8,128)}, bf16[256,128]{1,0:T(8,128)(2,1)S(1)}, bf16[64,2048]{1,0:T(8,128)(2,1)}, bf16[128,512]{1,0:T(8,128)(2,1)}, /*index=5*/f32[8,128]{1,0:T(8,128)}) custom-call(s32[6]{0:T(128)S(1)} %stack.9.refs_0_, bf16[32,5632]{1,0:T(8,128)(2,1)S(1)} %collective-permute-done.4.refs_1_, ...), custom_call_target="tpu_custom_call" | custom-call | flops 4499999744 | bytes 18000000 | tf_op jit(solution)/shard_map/pallas_call | solution.py:216
  254.2 6.3 %all-to-all-start.8 = ((bf16[8,256,128]{2,1,0:T(8,128)(2,1)}), bf16[8,256,128]{2,1,0:T(8,128)(2,1)S(1)}, u32[]{:S(2)}, u32[]{:S(2)}) async-start(bf16[8,256,128]{2,1,0:T(8,128)(2,1)} %broadcast_in_dim.22), calls=%async_computation.8 | async-start | bytes 1048576 | tf_op jit(solution)/shard_map/all_to_all | solution.py:1623
  265.2 5.8 %shard_map.412 = (bf16[1536,256]{1,0:T(8,128)(2,1)}, f32[8,128]{1,0:T(8,128)}) custom-call(s32[6]{0:T(128)S(1)} %stack.9.refs_0_, f32[3,32,192]{2,1,0:T(8,128)S(1)} %shard_map.411.refs_1_, bf16[128,1024]{1,0:T(8,128)(2,1)} %get-tuple-element.290.refs_2_, bf16[64,2048]{1,0:T(8,128)(2,1)} %get-tuple-element.291.refs_3_, ...), custom_call_target="tpu_custom_call" | custom-call | flops 2000000000 | bytes 8000000 | tf_op jit(solution)/shard_map/pallas_call | solution.py:216
  271.0 6.2 %all-to-all-done.8.refs_1_ = bf16[8,256,128]{2,1,0:T(8,128)(2,1)S(1)} async-done(((bf16[8,256,128]{2,1,0:T(8,128)(2,1)}), bf16[8,256,128]{2,1,0:T(8,128)(2,1)S(1)}, u32[]{:S(2)}, u32[]{:S(2)}) %all-to-all-start.8) | async-done | bytes 524320 | tf_op jit(solution)/shard_map/all_to_all | solution.py:1623
  282.7 16.6 %collective-permute-done.8.refs_2_ = bf16[256,512]{1,0:T(8,128)(2,1)S(1)} collective-permute-done((bf16[256,512]{1,0:T(8,128)(2,1)S(1)}, bf16[256,512]{1,0:T(8,128)(2,1)S(1)}, u32[]{:S(2)}, u32[]{:S(2)}) %collective-permute-start.8) | collective-permute-done | bytes 262176 | tf_op jit(solution)/shard_map/ppermute | solution.py:1659
  300.1 11.3 %shard_map.413 = (bf16[256,1024]{1,0:T(8,128)(2,1)S(1)}, bf16[512,256]{1,0:T(8,128)(2,1)S(1)}, bf16[256,1024]{1,0:T(8,128)(2,1)S(1)}, f32[128,384]{1,0:T(8,128)}, f32[8,128]{1,0:T(8,128)}) custom-call(s32[6]{0:T(128)S(1)} %stack.9.refs_0_, bf16[8,256,128]{2,1,0:T(8,128)(2,1)S(1)} %all-to-all-done.8.refs_1_, bf16[256,1024]{1,0:T(8,128)(2,1)} %get-tuple-element.282.refs_2_, ...), custom_call_target="tpu_custom_call" | custom-call | flops 5000000000 | bytes 20000000 | tf_op jit(solution)/shard_map/pallas_call | solution.py:216
  311.5 5.6 %collective-permute-done.9.refs_2_ = bf16[128,512]{1,0:T(8,128)(2,1)S(1)} collective-permute-done((bf16[128,512]{1,0:T(8,128)(2,1)S(1)}, bf16[128,512]{1,0:T(8,128)(2,1)S(1)}, u32[]{:S(2)}, u32[]{:S(2)}) %collective-permute-start.9) | collective-permute-done | bytes 131104 | tf_op jit(solution)/shard_map/ppermute | solution.py:1659
  318.6 7.2 %shard_map.416 = (bf16[4,176,512]{2,1,0:T(8,128)(2,1)}, f32[8,128]{1,0:T(8,128)}) custom-call(s32[6]{0:T(128)S(1)} %stack.9.refs_0_, bf16[256,1024]{1,0:T(8,128)(2,1)S(1)} %get-tuple-element.299.refs_1_, bf16[512,256]{1,0:T(8,128)(2,1)} %get-tuple-element.300.refs_2_, bf16[512,256]{1,0:T(8,128)(2,1)S(1)} %get-tuple-element.301.refs_3_, ...), custom_call_target="tpu_custom_call" | custom-call | flops 3000000000 | bytes 12000000 | tf_op jit(solution)/shard_map/pallas_call | solution.py:216
  334.5 5.9 %all-to-all-done.12.refs_1_ = bf16[4,176,512]{2,1,0:T(8,128)(2,1)S(1)} async-done(((bf16[4,176,512]{2,1,0:T(8,128)(2,1)}), bf16[4,176,512]{2,1,0:T(8,128)(2,1)S(1)}, u32[]{:S(2)}, u32[]{:S(2)}) %all-to-all-start.12) | async-done | bytes 720928 | tf_op jit(solution)/shard_map/all_to_all | solution.py:2014
  342.1 5.8 %shard_map.417 = (bf16[128,512]{1,0:T(8,128)(2,1)S(1)}, bf16[64,2048]{1,0:T(8,128)(2,1)S(1)}, bf16[32,8192]{1,0:T(8,128)(2,1)S(1)}) custom-call(s32[6]{0:T(128)S(1)} %stack.9.refs_0_, f32[128,384]{1,0:T(8,128)} %get-tuple-element.295.refs_1_, f32[128,1024]{1,0:T(8,128)} %get-tuple-element.296.refs_2_, bf16[128,1280]{1,0:T(8,128)(2,1)} %get-tuple-element.229.refs_2_.refs_3_, ...), custom_call_target="tpu_custom_call" | custom-call | flops 2000000000 | bytes 8000000 | tf_op jit(solution)/shard_map/pallas_call | solution.py:216
  351.5 15.3 %all_to_all.65 = bf16[32,16,256]{2,1,0:T(8,128)(2,1)S(1)} all-to-all(bf16[32,16,256]{2,1,0:T(8,128)(2,1)S(1)} %bitcast.71), channel_id=1, replica_groups=mesh['x'=2,'core'=2,'tile'=8] {'x','core','tile'}, dimensions={0} | all-to-all | bytes 524288 | tf_op jit(solution)/shard_map/all_to_all | solution.py:2003
  366.9 19.5 %all_to_all.66 = bf16[32,16,256]{2,1,0:T(8,128)(2,1)S(1)} all-to-all(bf16[32,16,256]{2,1,0:T(8,128)(2,1)S(1)} %broadcast_in_dim.46), channel_id=1, replica_groups=mesh['x'=2,'core'=2,'tile'=8] {'x','core','tile'}, dimensions={0} | all-to-all | bytes 524288 | tf_op jit(solution)/shard_map/all_to_all | solution.py:2008
  389.1 12.7 %shard_map.423 = (f32[2048,512]{1,0:T(8,128)}, f32[512,2048]{1,0:T(8,128)}, f32[512,512]{1,0:T(8,128)}) custom-call(bf16[32,144,512]{2,1,0:T(8,128)(2,1)} %bitcast.97), custom_call_target="tpu_custom_call" | custom-call | flops 4000000000 | bytes 16000000 | tf_op jit(solution)/shard_map/pallas_call | solution.py:1077
  401.8 24.4 %all-gather.5.cloned.1.call-done = bf16[8704,512]{1,0:T(8,128)(2,1)} async-done(((bf16[272,512]{1,0:T(8,128)(2,1)}), bf16[8704,512]{1,0:T(8,128)(2,1)}) %all-gather.5.cloned.1.call-update) | async-done | bytes 8912912 | tf_op jit(solution)/shard_map/all_gather | solution.py:2017
  426.3 13.5 %shard_map.421 = (f32[9,256,512]{2,1,0:T(8,128)}, f32[9,512,256]{2,1,0:T(8,128)}, f32[9,256,128]{2,1,0:T(8,128)}, f32[512,512]{1,0:T(8,128)}, f32[512,512]{1,0:T...) custom-call(bf16[32,272,512]{2,1,0:T(8,128)(2,1)} %bitcast.96), custom_call_target="tpu_custom_call" | custom-call | flops 4000000000 | bytes 16000000 | tf_op jit(solution)/shard_map/pallas_call | solution.py:1077
  (239 shorter events, 129.4 us)
Async XLA Ops:
  9.8 20.0 %all-to-all-start = ((bf16[8,24,1088]{2,1,0:T(8,128)(2,1)}), bf16[8,24,1088]{2,1,0:T(8,128)(2,1)S(1)}, u32[]{:S(2)}, u32[]{:S(2)}) async-start(bf16[8,24,1088]{2,1,0:T(8,128)(2,1)} %broadcast_in_dim.17), calls=%async_computation | async-start | bytes 884736 | tf_op jit(solution)/shard_map/all_to_all | solution.py:1623
  41.9 13.1 %all-to-all-start.1 = ((bf16[8,128,128]{2,1,0:T(8,128)(2,1)}), bf16[8,128,128]{2,1,0:T(8,128)(2,1)S(1)}, u32[]{:S(2)}, u32[]{:S(2)}) async-start(bf16[8,128,128]{2,1,0:T(8,128)(2,1)} %broadcast_in_dim.18), calls=%async_computation.1 | async-start | bytes 524288 | tf_op jit(solution)/shard_map/all_to_all | solution.py:1623
  48.3 62.8 %copy-start = (s32[1024,8]{1,0:T(8,128)}, s32[1024,8]{1,0:T(8,128)S(1)}, u32[]{:S(2)}) copy-start(s32[1024,8]{1,0:T(8,128)S(1)} %pad_bitcast_fusion.refs_1_.refs_3_) | copy-start | bytes 98308
  82.1 12.1 %all-to-all-start.2 = ((bf16[8,128,128]{2,1,0:T(8,128)(2,1)}), bf16[8,128,128]{2,1,0:T(8,128)(2,1)S(1)}, u32[]{:S(2)}, u32[]{:S(2)}) async-start(bf16[8,128,128]{2,1,0:T(8,128)(2,1)} %bitcast.13), calls=%async_computation.2 | async-start | bytes 524288 | tf_op jit(solution)/shard_map/all_to_all | solution.py:1696
  96.3 25.1 %copy-start.37 = (bf16[128,512]{1,0:T(8,128)(2,1)}, bf16[128,512]{1,0:T(8,128)(2,1)S(1)}, u32[]{:S(2)}) copy-start(bf16[128,512]{1,0:T(8,128)(2,1)S(1)} %get-tuple-element.253.refs_1_) | copy-start | bytes 393220
  96.3 36.1 %copy-start.33 = (f32[128,512]{1,0:T(8,128)}, f32[128,512]{1,0:T(8,128)S(1)}, u32[]{:S(2)}) copy-start(f32[128,512]{1,0:T(8,128)S(1)} %get-tuple-element.235.refs_2_) | copy-start | bytes 786436
  96.3 14.8 %all-to-all-start.3 = ((bf16[8,192,128]{2,1,0:T(8,128)(2,1)}), bf16[8,192,128]{2,1,0:T(8,128)(2,1)S(1)}, u32[]{:S(2)}, u32[]{:S(2)}) async-start(bf16[8,192,128]{2,1,0:T(8,128)(2,1)} %get-tuple-element.233), calls=%async_computation.3 | async-start | bytes 786432 | tf_op jit(solution)/shard_map/all_to_all | solution.py:1707
  101.1 23.9 %copy-start.52 = (bf16[512]{0:T(512)(128)(2,1)S(1)}, bf16[512]{0:T(512)(128)(2,1)}, u32[]{:S(2)}) copy-start(bf16[512]{0:T(512)(128)(2,1)} %param.64) | copy-start | bytes 3076
  101.1 31.3 %copy-start.14 = (bf16[512,512]{1,0:T(8,128)(2,1)S(1)}, bf16[512,512]{1,0:T(8,128)(2,1)}, u32[]{:S(2)}) copy-start(bf16[512,512]{1,0:T(8,128)(2,1)} %refs_4_.3) | copy-start | bytes 1572868
  101.2 31.2 %copy-start.26 = (bf16[1,128,512]{2,1,0:T(8,128)(2,1)S(1)}, bf16[1,128,512]{2,1,0:T(8,128)(2,1)}, u32[]{:S(2)}) copy-start(bf16[1,128,512]{2,1,0:T(8,128)(2,1)} %param.67) | copy-start | bytes 393220
  121.4 11.0 %all-to-all-start.4 = ((bf16[8,64,128]{2,1,0:T(8,128)(2,1)}), bf16[8,64,128]{2,1,0:T(8,128)(2,1)S(1)}, u32[]{:S(2)}, u32[]{:S(2)}) async-start(bf16[8,64,128]{2,1,0:T(8,128)(2,1)} %get-tuple-element.234), calls=%async_computation.4 | async-start | bytes 262144 | tf_op jit(solution)/shard_map/all_to_all | solution.py:1711
  142.0 4.9 %collective-permute-start = (bf16[2304,512]{1,0:T(8,128)(2,1)}, bf16[2304,512]{1,0:T(8,128)(2,1)}, u32[]{:S(2)}, u32[]{:S(2)}) collective-permute-start(bf16[2304,512]{1,0:T(8,128)(2,1)} %get-tuple-element.245), channel_id=1, source_target_pairs={{0,8},{8,0},{1,9},{9,1},{2,10},{10,2},{3,11},{11,3},{4,12},{12,4},... | collective-permute-start | bytes 7077896 | tf_op jit(solution)/shard_map/ppermute | solution.py:1659
  142.1 12.2 %all-to-all-start.5 = ((bf16[8,64,128]{2,1,0:T(8,128)(2,1)}), bf16[8,64,128]{2,1,0:T(8,128)(2,1)}, u32[]{:S(2)}, u32[]{:S(2)}) async-start(bf16[8,64,128]{2,1,0:T(8,128)(2,1)} %get-tuple-element.239), calls=%async_computation.5 | async-start | bytes 262144 | tf_op jit(solution)/shard_map/all_to_all | solution.py:1715
  164.0 14.8 %all-to-all-start.6 = ((bf16[8,192,128]{2,1,0:T(8,128)(2,1)}), bf16[8,192,128]{2,1,0:T(8,128)(2,1)S(1)}, u32[]{:S(2)}, u32[]{:S(2)}) async-start(bf16[8,192,128]{2,1,0:T(8,128)(2,1)} %get-tuple-element.247), calls=%async_computation.6 | async-start | bytes 786432 | tf_op jit(solution)/shard_map/all_to_all | solution.py:1723
  167.5 27.4 %collective-permute-start.2 = (bf16[1152,512]{1,0:T(8,128)(2,1)}, bf16[1152,512]{1,0:T(8,128)(2,1)S(1)}, u32[]{:S(2)}, u32[]{:S(2)}) collective-permute-start(bf16[1152,512]{1,0:T(8,128)(2,1)} %copy-done.8), channel_id=1, source_target_pairs={{0,16},{16,0},{1,17},{17,1},{2,18},{18,2},{3,19},{19,3},{4,20},{20... | collective-permute-start | bytes 3538952 | tf_op jit(solution)/shard_map/ppermute | solution.py:1659
  188.2 16.1 %collective-permute-start.1 = (bf16[1024,512]{1,0:T(8,128)(2,1)}, bf16[1024,512]{1,0:T(8,128)(2,1)}, u32[]{:S(2)}, u32[]{:S(2)}) collective-permute-start(bf16[1024,512]{1,0:T(8,128)(2,1)} %get-tuple-element.261), channel_id=1, source_target_pairs={{0,8},{8,0},{1,9},{9,1},{2,10},{10,2},{3,11},{11,3},{4,12},{12,4},... | collective-permute-start | bytes 3145736 | tf_op jit(solution)/shard_map/ppermute | solution.py:1659
  197.3 16.2 %collective-permute-start.3 = (bf16[576,512]{1,0:T(8,128)(2,1)}, bf16[576,512]{1,0:T(8,128)(2,1)S(1)}, u32[]{:S(2)}, u32[]{:S(2)}) collective-permute-start(bf16[576,512]{1,0:T(8,128)(2,1)} %get-tuple-element.267), channel_id=1, source_target_pairs={{0,1},{1,0},{2,3},{3,2},{4,5},{5,4},{6,7},{7,6},{8,9},{9,8},{10,11... | collective-permute-start | bytes 1769480 | tf_op jit(solution)/shard_map/ppermute | solution.py:1659
  199.7 17.5 %all-to-all-start.7 = ((bf16[8,128,128]{2,1,0:T(8,128)(2,1)}), bf16[8,128,128]{2,1,0:T(8,128)(2,1)S(1)}, u32[]{:S(2)}, u32[]{:S(2)}) async-start(bf16[8,128,128]{2,1,0:T(8,128)(2,1)} %broadcast_in_dim.21), calls=%async_computation.7 | async-start | bytes 524288 | tf_op jit(solution)/shard_map/all_to_all | solution.py:1623
  204.2 184.9 %all-gather.7.cloned.1.call-start = ((), (), s32[]{:S(2)}) async-start(), calls=%async_computation.14 | async-start | bytes 4866048 | tf_op jit(solution)/shard_map/all_gather | solution.py:2016
  206.6 33.0 %collective-permute-start.6 = (bf16[512,512]{1,0:T(8,128)(2,1)}, bf16[512,512]{1,0:T(8,128)(2,1)S(1)}, u32[]{:S(2)}, u32[]{:S(2)}) collective-permute-start(bf16[512,512]{1,0:T(8,128)(2,1)} %get-tuple-element.275), channel_id=1, source_target_pairs={{0,16},{16,0},{1,17},{17,1},{2,18},{18,2},{3,19},{19,3},{4,20},{20... | collective-permute-start | bytes 1572872 | tf_op jit(solution)/shard_map/ppermute | solution.py:1659
  215.0 19.0 %collective-permute-start.7 = (bf16[288,512]{1,0:T(8,128)(2,1)}, bf16[288,512]{1,0:T(8,128)(2,1)}, u32[]{:S(2)}, u32[]{:S(2)}) collective-permute-start(bf16[288,512]{1,0:T(8,128)(2,1)} %get-tuple-element.279), channel_id=1, source_target_pairs={{0,4},{1,5},{2,6},{3,7},{4,0},{5,1},{6,2},{7,3},{8,12},{9,13},{10,... | collective-permute-start | bytes 884744 | tf_op jit(solution)/shard_map/ppermute | solution.py:1659
  225.9 15.7 %collective-permute-start.4 = (bf16[32,5632]{1,0:T(8,128)(2,1)S(1)}, bf16[32,5632]{1,0:T(8,128)(2,1)S(1)}, u32[]{:S(2)}, u32[]{:S(2)}) collective-permute-start(bf16[32,5632]{1,0:T(8,128)(2,1)S(1)} %get-tuple-element.269), channel_id=1, source_target_pairs={{0,1},{1,2},{2,3},{3,4},{4,5},{5,6},{6,7},{8,9},{9,10},{10,11},{11... | collective-permute-start | bytes 1081352 | tf_op jit(solution)/shard_map/ppermute | solution.py:1636
  229.5 12.1 %collective-permute-start.5 = (bf16[32,5632]{1,0:T(8,128)(2,1)S(1)}, bf16[32,5632]{1,0:T(8,128)(2,1)S(1)}, u32[]{:S(2)}, u32[]{:S(2)}) collective-permute-start(bf16[32,5632]{1,0:T(8,128)(2,1)S(1)} %get-tuple-element.271), channel_id=1, source_target_pairs={{1,0},{2,1},{3,2},{4,3},{5,4},{6,5},{7,6},{9,8},{10,9},{11,10},{12... | collective-permute-start | bytes 1081352 | tf_op jit(solution)/shard_map/ppermute | solution.py:1636
  236.0 16.0 %collective-permute-start.11 = (bf16[144,512]{1,0:T(8,128)(2,1)S(1)}, bf16[144,512]{1,0:T(8,128)(2,1)S(1)}, u32[]{:S(2)}, u32[]{:S(2)}) collective-permute-start(bf16[144,512]{1,0:T(8,128)(2,1)S(1)} %get-tuple-element.329), channel_id=1, source_target_pairs={{0,2},{1,3},{2,0},{3,1},{4,6},{5,7},{6,4},{7,5},{8,10},{9,11},{10,... | collective-permute-start | bytes 442376 | tf_op jit(solution)/shard_map/ppermute | solution.py:1659
  254.2 23.0 %all-to-all-start.8 = ((bf16[8,256,128]{2,1,0:T(8,128)(2,1)}), bf16[8,256,128]{2,1,0:T(8,128)(2,1)S(1)}, u32[]{:S(2)}, u32[]{:S(2)}) async-start(bf16[8,256,128]{2,1,0:T(8,128)(2,1)} %broadcast_in_dim.22), calls=%async_computation.8 | async-start | bytes 1048576 | tf_op jit(solution)/shard_map/all_to_all | solution.py:1623
  265.2 34.0 %copy-start.32 = (bf16[256,512]{1,0:T(8,128)(2,1)S(1)}, bf16[256,512]{1,0:T(8,128)(2,1)}, u32[]{:S(2)}) copy-start(bf16[256,512]{1,0:T(8,128)(2,1)} %copy-done.31) | copy-start | bytes 786436
  277.2 40.7 %all-to-all-start.9 = ((bf16[32,48,256]{2,1,0:T(8,128)(2,1)}), bf16[32,48,256]{2,1,0:T(8,128)(2,1)S(1)}, u32[]{:S(2)}, u32[]{:S(2)}) async-start(bf16[32,48,256]{2,1,0:T(8,128)(2,1)} %bitcast.29), calls=%async_computation.9 | async-start | bytes 1572864 | tf_op jit(solution)/shard_map/all_to_all | solution.py:1973
  280.8 18.5 %collective-permute-start.8 = (bf16[256,512]{1,0:T(8,128)(2,1)S(1)}, bf16[256,512]{1,0:T(8,128)(2,1)S(1)}, u32[]{:S(2)}, u32[]{:S(2)}) collective-permute-start(bf16[256,512]{1,0:T(8,128)(2,1)S(1)} %copy-done.24), channel_id=1, source_target_pairs={{0,1},{1,0},{2,3},{3,2},{4,5},{5,4},{6,7},{7,6},{8,9},{9,8},{10,11... | collective-permute-start | bytes 786440 | tf_op jit(solution)/shard_map/ppermute | solution.py:1659
  300.1 17.0 %collective-permute-start.9 = (bf16[128,512]{1,0:T(8,128)(2,1)S(1)}, bf16[128,512]{1,0:T(8,128)(2,1)S(1)}, u32[]{:S(2)}, u32[]{:S(2)}) collective-permute-start(bf16[128,512]{1,0:T(8,128)(2,1)S(1)} %get-tuple-element.305), channel_id=1, source_target_pairs={{0,4},{1,5},{2,6},{3,7},{4,0},{5,1},{6,2},{7,3},{8,12},{9,13},{10,... | collective-permute-start | bytes 393224 | tf_op jit(solution)/shard_map/ppermute | solution.py:1659
  325.8 14.6 %all-to-all-start.12 = ((bf16[4,176,512]{2,1,0:T(8,128)(2,1)}), bf16[4,176,512]{2,1,0:T(8,128)(2,1)S(1)}, u32[]{:S(2)}, u32[]{:S(2)}) async-start(bf16[4,176,512]{2,1,0:T(8,128)(2,1)} %get-tuple-element.316), calls=%async_computation.12 | async-start | bytes 1441792 | tf_op jit(solution)/shard_map/all_to_all | solution.py:2014
  329.4 96.8 %all-gather.5.cloned.1.call-start = ((), (), s32[]{:S(2)}) async-start(), calls=%async_computation.13 | async-start | bytes 9191424 | tf_op jit(solution)/shard_map/all_gather | solution.py:2017
  329.5 4.4 collective-permute-start.10
  (46 other events, 495.4 us)
Sparse Core Ops, SparseCore 0:
  253.4 75.2 all-gather.6
  341.8 84.3 all-gather.4

commit v2 on v1

--- a/solution.py
+++ b/solution.py
@@ -917,21 +917,21 @@
     return call(1, total_body, outs, [], ids, (parts,))
 
 
-def gather_body(ids, heavy, embed, early, share):
+def gather_body(ids, heavy, mixer, embed, early, share):
     rows, width = heavy.shape[1:]
     total = heavy[0].astype(f32)
     for n in range(1, heavy.shape[0]):
         total = total + heavy[n].astype(f32)
     share[0:rows, :] = total.astype(bf16)
-    share[rows : rows + 64, :] = embed[...]
+    share[rows : rows + 144, :] = mixer[...]
+    share[rows + 144 : rows + 208, :] = embed[...]
     pad = jnp.zeros((8, width), f32)
-    share[rows + 64 :, :] = jnp.concatenate([early[...].astype(f32), pad], axis=0).astype(bf16)
-
-
-def run_gather(ids, heavy, embed, early):
-    rows, width = heavy.shape[1:]
-    outs = [((rows + 96, width), bf16)]
-    return call(1, gather_body, outs, [], ids, (heavy, embed, early))[0]
+    share[rows + 208 :, :] = jnp.concatenate([early[...].astype(f32), pad], axis=0).astype(bf16)
+
+
+def run_gather(ids, *arrays):
+    rows, width = arrays[0].shape[1:]
+    return call(1, gather_body, [((rows + 240, width), bf16)], [], ids, arrays)[0]
 
 
 def run_finish(ids, kept, got, after):
@@ -998,7 +998,7 @@
     )
 
 
-def unpack_body(split, whole, *refs):
+def unpack_body(whole, *refs):
     stage, marks = refs[-2:]
     plain = list(refs[:-2])
     step = pl.program_id(0)
@@ -1018,67 +1018,63 @@
 
     fetch(step).wait()
     held = stage.at[step % 4]
-    first = 0
-    if split:
-        up, fifth, fourth, *plain, early = plain
-        for tap in range(9):
-            block = held[16 * tap : 16 * tap + 16, :].astype(f32)
-            up[tap] = block[0:8, :]
-            fifth[tap, 0:8, :] = block[8:16, 0:256]
-            fifth[tap, 8:16, :] = block[8:16, 256:512]
-        sides = held[144:176, :].astype(f32)
-        for tap in range(9):
-            rows = slice(8 * (tap // 4), 8 * (tap // 4) + 8)
-            fourth[tap] = sides[rows, 128 * (tap % 4) : 128 * (tap % 4) + 128]
-        first = 176
+    up, fifth, fourth, *plain, early = plain
+    for tap in range(9):
+        block = held[16 * tap : 16 * tap + 16, :].astype(f32)
+        up[tap] = block[0:8, :]
+        fifth[tap, 0:8, :] = block[8:16, 0:256]
+        fifth[tap, 8:16, :] = block[8:16, 256:512]
+    sides = held[144:176, :].astype(f32)
+    for tap in range(9):
+        rows = slice(8 * (tap // 4), 8 * (tap // 4) + 8)
+        fourth[tap] = sides[rows, 128 * (tap % 4) : 128 * (tap % 4) + 128]
+    first = 176
     for out in plain:
         rows = out.shape[0]
         out[...] = held[first : first + rows, :].astype(f32)
         first = first + rows
-    if split:
-        block = held[first : first + 32, :].astype(f32)
-        early[0:24, :] = block[0:24, 0:256]
-        early[24:48, :] = block[0:24, 256:512]
-
-
-def run_unpack(whole, split, rows):
+    block = held[first : first + 32, :].astype(f32)
+    early[0:24, :] = block[0:24, 0:256]
+    early[24:48, :] = block[0:24, 256:512]
+
+
+def run_unpack(whole):
     tiles = whole.shape[0] // 4
 
     def by_page(n):
         return (0, n % tiles * 4 + n // tiles, 0)
 
-    def chunk_of(n):
+    def by_chunk(n):
         tile, page = n % tiles, n // tiles
-        return page % 2 * 16 + page // 2 * 8 + tile % 2 * 4 + tile // 4 * 2 + tile // 2 % 2
-
-    def by_chunk(n):
-        return (chunk_of(n), 0)
+        return (page % 2 * 16 + page // 2 * 8 + tile % 2 * 4 + tile // 4 * 2 + tile // 2 % 2, 0)
+
+    def plain(n):
+        return (n, 0)
 
     def by_column(n):
-        return (chunk_of(n) % 8, chunk_of(n) // 8)
+        return (n % 8, n // 8)
+
+    def out(shape, block, spot):
+        return jax.ShapeDtypeStruct(shape, f32), pl.BlockSpec(block, spot)
 
     outs = [
-        (
-            jax.ShapeDtypeStruct((total, width), f32),
-            pl.BlockSpec((size, 512), by_column if width > 512 else by_chunk),
-        )
-        for total, width, size in rows
+        out((9, 256, 512), (9, 8, 512), by_page),
+        out((9, 512, 256), (9, 16, 256), by_page),
+        out((9, 256, 128), (9, 8, 128), by_page),
+        out((2048, 512), (64, 512), plain),
+        out((512, 2048), (64, 512), by_column),
+        out((512, 512), (16, 512), plain),
+        out((512, 512), (16, 512), by_chunk),
+        out((512, 512), (16, 512), by_chunk),
+        out((512, 512), (16, 512), by_chunk),
+        out((512, 512), (16, 512), by_chunk),
+        out((1536, 256), (48, 256), plain),
     ]
-    if split:
-        outs = (
-            [
-                (jax.ShapeDtypeStruct((9, 256, 512), f32), pl.BlockSpec((9, 8, 512), by_page)),
-                (jax.ShapeDtypeStruct((9, 512, 256), f32), pl.BlockSpec((9, 16, 256), by_page)),
-                (jax.ShapeDtypeStruct((9, 256, 128), f32), pl.BlockSpec((9, 8, 128), by_page)),
-            ]
-            + outs
-            + [(jax.ShapeDtypeStruct((1536, 256), f32), pl.BlockSpec((48, 256), lambda n: (n, 0)))]
-        )
     return pl.pallas_call(
-        functools.partial(unpack_body, split),
-        cost_estimate=price(8),
+        unpack_body,
+        cost_estimate=price(14),
         grid=(whole.shape[0],),
-        out_shape=[out for out, _ in outs],
+        out_shape=[shape for shape, _ in outs],
         in_specs=[pl.BlockSpec(memory_space=pltpu.HBM)],
         out_specs=[spec for _, spec in outs],
         scratch_shapes=[
@@ -1478,30 +1474,22 @@
             other[...] = second[...] if bit == 0 else first[...]
 
 
-def mixer_grads_body(ids, found, act, d_pre, ffn_low, d_low, upstream, mine, other, token, table):
+def mixer_grads_body(ids, found, act, d_pre, ffn_low, d_low, upstream, table, token):
     width = ffn_low.shape[1]
     grad_out = mm_tn(act[...], upstream[...]).astype(bf16)
     grad_in = mm_tn(ffn_low[...], d_pre[...]).astype(bf16)
     attn = jnp.concatenate([found[h] for h in range(HEADS)], axis=0)
     grad_attn = mm(attn, d_low[...]).astype(bf16)
     for c in range(32):
-        spot, row = 144 * (c % 16), 64 * (c % 8)
-        table[c // 16, spot : spot + 64, :] = grad_out[64 * c : 64 * c + 64, :]
+        spot, row = 144 * c, 64 * (c % 8)
+        table[spot : spot + 64, :] = grad_out[64 * c : 64 * c + 64, :]
         column = width * (c // 8)
-        table[c // 16, spot + 64 : spot + 128, :] = grad_in[row : row + 64, column : column + width]
-        table[c // 16, spot + 128 : spot + 144, :] = grad_attn[16 * c : 16 * c + 16, :]
-    put_halves(ids, table.at[0], table.at[1], mine, other)
-
-
-def run_mixer_grads(ids, bit, *arrays):
-    return call(
-        4,
-        mixer_grads_body,
-        [((2304, 512), bf16)] * 2 + [TOKEN],
-        [((2, 2304, 512), bf16)],
-        ids.at[5].set(bit),
-        arrays,
-    )
+        table[spot + 64 : spot + 128, :] = grad_in[row : row + 64, column : column + width]
+        table[spot + 128 : spot + 144, :] = grad_attn[16 * c : 16 * c + 16, :]
+
+
+def run_mixer_grads(ids, *arrays):
+    return call(4, mixer_grads_body, [((4608, 512), bf16), TOKEN], [], ids, arrays)
 
 
 def embed_back_body(ids, d_shared, residual, d_mixed, gain, wq, wk, wv, roi, d_resid, d_low, d_pooled, d_gain, d_rows, token):
@@ -1713,12 +1701,14 @@
             ids, found, residual, cotangent[0], w_output, gain_row_two, ffn_in, ffn_out
         )
         d_found = lax.all_to_all(d_found, "tile", 0, 0, tiled=True)
-        mixer_halves = run_mixer_grads(
-            ids, bit_of(*HOPS[0]), found, act_low, d_pre, ffn_low, d_mixed_low, cotangent[0]
-        )
-        mixer_halves = halved(mixer_halves, 0)
+        mixer_table, mixer_token = run_mixer_grads(
+            ids, found, act_low, d_pre, ffn_low, d_mixed_low, cotangent[0]
+        )
+        mixer_share = lax.psum_scatter(
+            mixer_table, (*PAGES, "tile"), scatter_dimension=0, tiled=True
+        )
         d_shared, d_table = run_attend_back(
-            tall, ids, mixer_halves[2:], meta_all, shared, prob, found_full, d_found
+            tall, ids, (mixer_token,), meta_all, shared, prob, found_full, d_found
         )
         d_shared = lax.all_to_all(d_shared, "tile", 0, 0, tiled=True)
         d_residual, d_resid_low, d_pooled, grad_gain_attn, d_rows, embed_token = run_embed_back(
@@ -1736,10 +1726,8 @@
             grad_gain_ffn,
             d_table,
         )
-        mixer_halves = halved(mixer_halves, 1, embed_token)
-        mixer_halves = halved(mixer_halves, 2)
         embed_halves = halved(embed_halves, 0)
-        ordering = (embed_halves[2], mixer_halves[2])
+        ordering = embed_halves[2:]
     else:
         ordering = ()
         pooled_low = jnp.sum(pieces.astype(jnp.float32), axis=0).astype(jnp.bfloat16)
@@ -1933,9 +1921,8 @@
         ids, ordering, box_rows, d_pooled_all, pre_up_zero, 256
     )
     if heads_first:
-        mixer_halves = halved(mixer_halves, 3, box_token)
         embed_halves = halved(embed_halves, 1, box_token)
-        ordering = (embed_halves[2], mixer_halves[2])
+        ordering = embed_halves[2:]
     d_dec_one, d_dec_two, d_dec_three, low_one_up, low_two_up, up_token = run_up_back(
         ids,
         ordering,
@@ -1950,10 +1937,14 @@
     )
     d_dec_three_all = windowed(d_dec_three)
     grad_up_first = run_grad_up_first(ids, (up_token,), dec_one, low_zero_up)
-    light_early, early_token = run_grad_up(ids, (), grad_up_first, dec_two, low_one_up, u_three, low_two_up)
     if heads_first:
-        mixer_share = halved(mixer_halves, 4, up_token)
         embed_halves = halved(embed_halves, 2, up_token)
+        ordering = embed_halves[2:]
+    light_early, early_token = run_grad_up(
+        ids, ordering, grad_up_first, dec_two, low_one_up, u_three, low_two_up
+    )
+    if heads_first:
+        embed_halves = halved(embed_halves, 3, up_token)
         ordering = embed_halves[2:]
     low_three_up, low_four, low_three, d_pool_three, bottom_token = run_bottom_back(
         cut,
@@ -1969,12 +1960,12 @@
     )
     dp_count = lax.axis_size(PAGES)
     if heads_first:
-        embed_halves = halved(embed_halves, 3, bottom_token)
+        embed_share = halved(embed_halves, 4, bottom_token)
         early_parts = lax.all_to_all(
             light_early.reshape(32, -1, 256), (*PAGES, "tile"), 0, 0, tiled=True
         )
-        early_share, early_done = run_total(ids, early_parts)
-        ordering = (embed_halves[2], early_done)
+        early_share, _ = run_total(ids, early_parts)
+        ordering = ()
     bottom_parts = (low_three_up, e_four, low_four, p_four, low_three, p_three_all)
     if cut:
         heavy = run_grad_bottom_all(ids, *bottom_parts)
@@ -2010,16 +2001,11 @@
     late = spread_out(summed_share(light_late)).reshape(light_late.shape).astype(jnp.float32)
     wide = ffn_in.shape[1]
     if heads_first:
-        embed_share = halved(embed_halves, 4)
         parts = lax.all_to_all(heavy, PAGES, 0, 0, tiled=True)
-        share = run_gather(ids, parts, embed_share, early_share)
-        mixer_all = lax.all_gather(mixer_share, both_axes, axis=0)
+        share = run_gather(ids, parts, mixer_share, embed_share, early_share)
         whole = lax.all_gather(share, both_axes, axis=0)
-        sum_ffn_out, sum_ffn_in, sum_output = run_unpack(
-            mixer_all, False, [(2048, 512, 64), (512, 2048, 64), (512, 512, 16)]
-        )
-        *heavy_sums, sum_query, sum_key, sum_value, rest, early = run_unpack(
-            whole, True, [(512, 512, 16)] * 4
+        *heavy_sums, sum_ffn_out, sum_ffn_in, sum_output, sum_query, sum_key, sum_value, rest, early = (
+            run_unpack(whole)
         )
         rest = rest.reshape(NB, 16, model_width)
         sum_roi = rest[:, :4].reshape(-1, model_width)

time: 458 us -> 478 us (1.044)
  waiting for transfers between devices: 131 us -> 174 us
  Pallas kernels: 170 us -> 150 us
    all_gather x1, waiting for transfers between devices: 24.4 us -> 59.5 us  [on_device(): whole = lax.all_gather(share, both_axes, axis=0)]
    ppermute x2, waiting for transfers between devices: 0.6 us -> 17.1 us  [from_side(): return lax.ppermute(block, 'tile', hops)]
    pallas_call x2 -> x1, Pallas kernels: 26.2 us -> 15.2 us  [run_unpack(): pl.pallas_call(unpack_body, cost_estimate=price(14), grid=(whole.shape[0]...]
    pallas_call x31 -> x26, Pallas kernels: 144 us -> 135 us  [call(): pl.pallas_call(ordered, cost_estimate=price(micros), out_shape=[pltpu.HBM...]
    ppermute x10 -> x5, starting transfers between devices: 12.4 us -> 6.32 us  [swapped(): return lax.ppermute(block, axis, hops)]
    unnamed x118 -> x86, local copies, waits for them, and re-layouts: 15.5 us -> 19 us
    ppermute x10 -> x5, waiting for transfers between devices: 39.3 us -> 36.3 us  [swapped(): return lax.ppermute(block, axis, hops)]
  transfers between devices with their start and end apart: 25 -> 20, of which waited for: 17 -> 13; matrix products, arithmetic and copies ran while one was open for 3% -> 3% of each run, Pallas kernels for 19% -> 16%
where the time goes in v2:
time: 478 us; the launch traced here: 472 us
  waiting for transfers between devices  174 us (36%)
  Pallas kernels  150 us (31%)
  starting transfers between devices  62.2 us (13%)
  blocking collectives  35.3 us (7%)
  local copies, waits for them, and re-layouts  34.6 us (7%)
  between operations  15.1 us (3%)
    pallas_call x26, Pallas kernels, call(): pl.pallas_call(ordered, cost_estimate=price(micros), out_shape=[pltpu.HBM...  135 us
    all_gather x1, waiting for transfers between devices, on_device(): whole = lax.all_gather(share, both_axes, axis=0)  59.5 us
    ppermute x5, waiting for transfers between devices, swapped(): return lax.ppermute(block, axis, hops)  36.3 us
    all_to_all x4, starting transfers between devices, gathered(): return lax.all_to_all(copies, 'tile', 0, 0, tiled=True)  21.6 us
    all_to_all x4, waiting for transfers between devices, gathered(): return lax.all_to_all(copies, 'tile', 0, 0, tiled=True)  21.1 us
    unnamed x86, local copies, waits for them, and re-layouts  19 us
    all_to_all x1, blocking collectives, summed_share(): parts = lax.all_to_all(parts, both_axes, 0, 0, tiled=True)  18.3 us
    ppermute x2, waiting for transfers between devices, from_side(): return lax.ppermute(block, 'tile', hops)  17.1 us
  transfers between devices with their start and end apart: 20, of which 13 were waited for; matrix products, arithmetic and copies ran while one was open for 3% of the time, Pallas kernels for 16%

profile of v2, /device:TPU:0, one launch (start us, length us, event | category | flops | bytes accessed | tf_op | source)
XLA Modules:
  0.0 472.3 jit_solution(3934753843632272918)
XLA Ops:
  9.8 7.3 %all-to-all-start = ((bf16[8,24,1088]{2,1,0:T(8,128)(2,1)}), bf16[8,24,1088]{2,1,0:T(8,128)(2,1)S(1)}, u32[]{:S(2)}, u32[]{:S(2)}) async-start(bf16[8,24,1088]{2,1,0:T(8,128)(2,1)} %broadcast_in_dim.17), calls=%async_computation | async-start | bytes 884736 | tf_op jit(solution)/shard_map/all_to_all | solution.py:1611
  21.1 8.7 %all-to-all-done.refs_1_ = bf16[8,24,1088]{2,1,0:T(8,128)(2,1)S(1)} async-done(((bf16[8,24,1088]{2,1,0:T(8,128)(2,1)}), bf16[8,24,1088]{2,1,0:T(8,128)(2,1)S(1)}, u32[]{:S(2)}, u32[]{:S(2)}) %all-to-all-start) | async-done | bytes 417824 | tf_op jit(solution)/shard_map/all_to_all | solution.py:1611
  29.8 11.3 %shard_map.391 = (bf16[32,8192]{1,0:T(8,128)(2,1)}, bf16[64,4096]{1,0:T(8,128)(2,1)}, bf16[32,2560]{1,0:T(8,128)(2,1)}, bf16[128,1280]{1,0:T(8,128)(2,1)}, bf16[...) custom-call(s32[6]{0:T(128)S(1)} %stack.9.refs_0_, ...), custom_call_target="tpu_custom_call" | custom-call | flops 5000000000 | bytes 20000000 | tf_op jit(solution)/shard_map/pallas_call | solution.py:216
  48.0 6.7 %all-to-all-done.1.refs_1_.refs_6_ = bf16[8,128,128]{2,1,0:T(8,128)(2,1)S(1)} async-done(((bf16[8,128,128]{2,1,0:T(8,128)(2,1)}), bf16[8,128,128]{2,1,0:T(8,128)(2,1)S(1)}, u32[]{:S(2)}, u32[]{:S(2)}) %all-to-all-start.1) | async-done | bytes 262176 | tf_op jit(solution)/shard_map/all_to_all | solution.py:1611
  54.7 10.0 %shard_map.392 = (bf16[256,1024]{1,0:T(8,128)(2,1)}, bf16[512,256]{1,0:T(8,128)(2,1)}, bf16[256,256]{1,0:T(8,128)(2,1)}, bf16[512,256]{1,0:T(8,128)(2,1)}, bf16[...) custom-call(s32[6]{0:T(128)S(1)} %stack.9.refs_0_, bf16[8,128,128]{2,1,0:T(8,128)(2,1)S(1)} %all-to-all-done.1.refs_1_.refs_6_, ...), custom_call_target="tpu_custom_call" | custom-call | flops 5500000256 | bytes 22000000 | tf_op jit(solution)/shard_map/pallas_call | solution.py:216
  64.7 9.3 %shard_map.393 = (bf16[128,1280]{1,0:T(8,128)(2,1)}, bf16[64,4608]{1,0:T(8,128)(2,1)}, bf16[32,8192]{1,0:T(8,128)(2,1)}, bf16[256,768]{1,0:T(8,128)(2,1)}, bf16[...) custom-call(s32[6]{0:T(128)S(1)} %stack.9.refs_0_, ...), custom_call_target="tpu_custom_call" | custom-call | flops 4499999744 | bytes 18000000 | tf_op jit(solution)/shard_map/pallas_call | solution.py:216
  74.1 8.1 %shard_map.394 = bf16[1024,128]{1,0:T(8,128)(2,1)} custom-call(s32[6]{0:T(128)S(1)} %stack.9.refs_0_, s32[1024,8]{1,0:T(8,128)S(1)} %pad_bitcast_fusion.refs_1_.refs_3_, bf16[512,512]{1,0:T(8,128)(2,1)S(1)} %get-tuple-element.179.refs_2_), custom_call_target="tpu_custom_call" | custom-call | flops 4000000000 | bytes 16000000 | tf_op jit(solution)/shard_map/pallas_call | solution.py:216
  85.8 8.5 %all-to-all-done.2.refs_1_ = bf16[8,128,128]{2,1,0:T(8,128)(2,1)S(1)} async-done(((bf16[8,128,128]{2,1,0:T(8,128)(2,1)}), bf16[8,128,128]{2,1,0:T(8,128)(2,1)S(1)}, u32[]{:S(2)}, u32[]{:S(2)}) %all-to-all-start.2) | async-done | bytes 262176 | tf_op jit(solution)/shard_map/all_to_all | solution.py:1684
  102.2 9.9 %all-to-all-done.3.refs_4_.refs_2_ = bf16[8,192,128]{2,1,0:T(8,128)(2,1)S(1)} async-done(((bf16[8,192,128]{2,1,0:T(8,128)(2,1)}), bf16[8,192,128]{2,1,0:T(8,128)(2,1)S(1)}, u32[]{:S(2)}, u32[]{:S(2)}) %all-to-all-start.3) | async-done | bytes 393248 | tf_op jit(solution)/shard_map/all_to_all | solution.py:1695
  112.1 10.3 %shard_map.396 = (bf16[4,1024,256]{2,1,0:T(8,128)(2,1)}, bf16[8,64,128]{2,1,0:T(8,128)(2,1)}, f32[64,1024]{1,0:T(8,128)}) custom-call(s32[6]{0:T(128)S(1)} %stack.9.refs_0_, f32[8,96]{1,0:T(8,128)S(1)} %convert_element_type.28.refs_1_, s32[8,1024]{1,0:T(8,128)S(1)} %pad.18.clone.refs_2_.refs_1_, s32[1024,8]{1,0:T(8,128)S(1)} %pad_bitcast_fusion.refs_1_.refs_3_, ...), custom_call_target="tpu_custom_call" | custom-call | flops 4499999744 | bytes 18000000 | tf_op jit(solution)/shard_map/pallas_call | solution.py:216
  126.1 7.3 %all-to-all-done.4.refs_1_ = bf16[8,64,128]{2,1,0:T(8,128)(2,1)S(1)} async-done(((bf16[8,64,128]{2,1,0:T(8,128)(2,1)}), bf16[8,64,128]{2,1,0:T(8,128)(2,1)S(1)}, u32[]{:S(2)}, u32[]{:S(2)}) %all-to-all-start.4) | async-done | bytes 131104 | tf_op jit(solution)/shard_map/all_to_all | solution.py:1699
  133.4 5.9 %shard_map.397 = (bf16[128,512]{1,0:T(8,128)(2,1)}, bf16[128,2048]{1,0:T(8,128)(2,1)S(1)}, bf16[128,2048]{1,0:T(8,128)(2,1)S(1)}, bf16[128,512]{1,0:T(8,128)(2,1...) custom-call(s32[6]{0:T(128)S(1)} %stack.9.refs_0_, ...), custom_call_target="tpu_custom_call" | custom-call | flops 2500000000 | bytes 10000000 | tf_op jit(solution)/shard_map/pallas_call | solution.py:216
  153.9 7.6 %shard_map.399 = (bf16[8,192,128]{2,1,0:T(8,128)(2,1)}, f32[32,128]{1,0:T(8,128)S(1)}) custom-call(s32[6]{0:T(128)S(1)} %stack.9.refs_0_, s32[8,1024]{1,0:T(8,128)S(1)} %pad.18.clone.refs_2_.refs_1_, bf16[8,192,128]{2,1,0:T(8,128)(2,1)S(1)} %all-to-all-done.3.refs_4_.refs_2_, bf16[4,1024,256]{2,1,0:T(8,128)(2,1)} %get-tuple-element.184.refs_3_, ...), custom_call_target="tpu_custom_call" | custom-call | flops 3000000000 | bytes 12000000 | tf_op jit(solution)/shard_map/pallas_call | solution.py:216
  161.5 5.9 %all-to-all-start.6 = ((bf16[8,192,128]{2,1,0:T(8,128)(2,1)}), bf16[8,192,128]{2,1,0:T(8,128)(2,1)S(1)}, u32[]{:S(2)}, u32[]{:S(2)}) async-start(bf16[8,192,128]{2,1,0:T(8,128)(2,1)} %get-tuple-element.192), calls=%async_computation.6 | async-start | bytes 786432 | tf_op jit(solution)/shard_map/all_to_all | solution.py:1713
  167.4 9.4 %all-to-all-done.6.refs_1_ = bf16[8,192,128]{2,1,0:T(8,128)(2,1)S(1)} async-done(((bf16[8,192,128]{2,1,0:T(8,128)(2,1)}), bf16[8,192,128]{2,1,0:T(8,128)(2,1)S(1)}, u32[]{:S(2)}, u32[]{:S(2)}) %all-to-all-start.6) | async-done | bytes 393248 | tf_op jit(solution)/shard_map/all_to_all | solution.py:1713
  190.6 5.7 %all-to-all-done.7 = bf16[8,128,128]{2,1,0:T(8,128)(2,1)S(1)} async-done(((bf16[8,128,128]{2,1,0:T(8,128)(2,1)}), bf16[8,128,128]{2,1,0:T(8,128)(2,1)S(1)}, u32[]{:S(2)}, u32[]{:S(2)}) %all-to-all-start.7) | async-done | bytes 262176 | tf_op jit(solution)/shard_map/all_to_all | solution.py:1611
  196.3 8.7 %shard_map.403 = (f32[32,8192]{1,0:T(8,128)}, bf16[32,8192]{1,0:T(8,128)(2,1)S(1)}, bf16[32,5632]{1,0:T(8,128)(2,1)}, bf16[32,5632]{1,0:T(8,128)(2,1)S(1)}, f32[8,128]{1,0:T(8,128)}) custom-call(s32[6]{0:T(128)S(1)} %stack.9.refs_0_, s32[1024,8]{1,0:T(8,128)S(1)} %pad_bitcast_fusion.refs_1_.refs_3_, bf16[1024,128]{1,0:T(8,128)(2,1)S(1)} %bitcast.69, ...), custom_call_target="tpu_custom_call" | custom-call | flops 4000000000 | bytes 16000000 | tf_op jit(solution)/shard_map/pallas_call | solution.py:216
  211.8 17.1 %collective-permute-done.1.refs_1_ = bf16[32,5632]{1,0:T(8,128)(2,1)S(1)} collective-permute-done((bf16[32,5632]{1,0:T(8,128)(2,1)}, bf16[32,5632]{1,0:T(8,128)(2,1)S(1)}, u32[]{:S(2)}, u32[]{:S(2)}) %collective-permute-start.1) | collective-permute-done | bytes 360480 | tf_op jit(solution)/shard_map/ppermute | solution.py:1624
  230.0 10.4 %shard_map.405 = (f32[64,4608]{1,0:T(8,128)}, f32[128,1024]{1,0:T(8,128)}, bf16[256,128]{1,0:T(8,128)(2,1)S(1)}, bf16[64,2048]{1,0:T(8,128)(2,1)}, bf16[128,512]{1,0:T(8,128)(2,1)}, /*index=5*/f32[8,128]{1,0:T(8,128)}) custom-call(s32[6]{0:T(128)S(1)} %stack.9.refs_0_, bf16[32,5632]{1,0:T(8,128)(2,1)S(1)} %collective-permute-done.1.refs_1_, ...), custom_call_target="tpu_custom_call" | custom-call | flops 4499999744 | bytes 18000000 | tf_op jit(solution)/shard_map/pallas_call | solution.py:216
  241.2 6.7 %all-to-all-start.8 = ((bf16[8,256,128]{2,1,0:T(8,128)(2,1)}), bf16[8,256,128]{2,1,0:T(8,128)(2,1)S(1)}, u32[]{:S(2)}, u32[]{:S(2)}) async-start(bf16[8,256,128]{2,1,0:T(8,128)(2,1)} %broadcast_in_dim.22), calls=%async_computation.8 | async-start | bytes 1048576 | tf_op jit(solution)/shard_map/all_to_all | solution.py:1611
  254.8 6.6 %collective-permute-done.4.refs_2_ = bf16[256,512]{1,0:T(8,128)(2,1)S(1)} collective-permute-done((bf16[256,512]{1,0:T(8,128)(2,1)S(1)}, bf16[256,512]{1,0:T(8,128)(2,1)S(1)}, u32[]{:S(2)}, u32[]{:S(2)}) %collective-permute-start.4) | collective-permute-done | bytes 262176 | tf_op jit(solution)/shard_map/ppermute | solution.py:1647
  262.0 5.8 %shard_map.409 = (bf16[1536,256]{1,0:T(8,128)(2,1)}, f32[8,128]{1,0:T(8,128)}) custom-call(s32[6]{0:T(128)S(1)} %stack.9.refs_0_, f32[3,32,192]{2,1,0:T(8,128)S(1)} %shard_map.408.refs_1_, bf16[128,1024]{1,0:T(8,128)(2,1)} %get-tuple-element.228.refs_2_, bf16[64,2048]{1,0:T(8,128)(2,1)} %get-tuple-element.229.refs_3_, ...), custom_call_target="tpu_custom_call" | custom-call | flops 2000000000 | bytes 8000000 | tf_op jit(solution)/shard_map/pallas_call | solution.py:216
  267.8 5.5 %all-to-all-start.12 = ((bf16[32,48,256]{2,1,0:T(8,128)(2,1)}), bf16[32,48,256]{2,1,0:T(8,128)(2,1)S(1)}, u32[]{:S(2)}, u32[]{:S(2)}) async-start(bf16[32,48,256]{2,1,0:T(8,128)(2,1)} %bitcast.36), calls=%async_computation.13 | async-start | bytes 1572864 | tf_op jit(solution)/shard_map/all_to_all | solution.py:1964
  276.1 25.3 %collective-permute-done.5.refs_2_ = bf16[128,512]{1,0:T(8,128)(2,1)S(1)} collective-permute-done((bf16[128,512]{1,0:T(8,128)(2,1)S(1)}, bf16[128,512]{1,0:T(8,128)(2,1)S(1)}, u32[]{:S(2)}, u32[]{:S(2)}) %collective-permute-start.5) | collective-permute-done | bytes 131104 | tf_op jit(solution)/shard_map/ppermute | solution.py:1647
  302.4 11.3 %shard_map.410 = (bf16[256,1024]{1,0:T(8,128)(2,1)S(1)}, bf16[512,256]{1,0:T(8,128)(2,1)S(1)}, bf16[256,1024]{1,0:T(8,128)(2,1)S(1)}, f32[128,384]{1,0:T(8,128)}, f32[8,128]{1,0:T(8,128)}) custom-call(s32[6]{0:T(128)S(1)} %stack.9.refs_0_, bf16[8,256,128]{2,1,0:T(8,128)(2,1)S(1)} %all-to-all-done.8.refs_1_, bf16[256,1024]{1,0:T(8,128)(2,1)} %get-tuple-element.218.refs_2_, ...), custom_call_target="tpu_custom_call" | custom-call | flops 5000000000 | bytes 20000000 | tf_op jit(solution)/shard_map/pallas_call | solution.py:216
  313.7 7.2 %shard_map.411 = (bf16[4,176,512]{2,1,0:T(8,128)(2,1)}, f32[8,128]{1,0:T(8,128)}) custom-call(s32[6]{0:T(128)S(1)} %stack.9.refs_0_, bf16[256,1024]{1,0:T(8,128)(2,1)S(1)} %get-tuple-element.238.refs_1_, bf16[512,256]{1,0:T(8,128)(2,1)} %get-tuple-element.239.refs_2_, bf16[512,256]{1,0:T(8,128)(2,1)S(1)} %get-tuple-element.240.refs_3_, ...), custom_call_target="tpu_custom_call" | custom-call | flops 3000000000 | bytes 12000000 | tf_op jit(solution)/shard_map/pallas_call | solution.py:216
  330.4 4.9 %all-to-all-done.11.refs_1_ = bf16[4,176,512]{2,1,0:T(8,128)(2,1)S(1)} async-done(((bf16[4,176,512]{2,1,0:T(8,128)(2,1)}), bf16[4,176,512]{2,1,0:T(8,128)(2,1)S(1)}, u32[]{:S(2)}, u32[]{:S(2)}) %all-to-all-start.11) | async-done | bytes 720928 | tf_op jit(solution)/shard_map/all_to_all | solution.py:2004
  338.1 5.8 %shard_map.412 = (bf16[128,512]{1,0:T(8,128)(2,1)S(1)}, bf16[64,2048]{1,0:T(8,128)(2,1)S(1)}, bf16[32,8192]{1,0:T(8,128)(2,1)S(1)}) custom-call(s32[6]{0:T(128)S(1)} %stack.9.refs_0_, f32[128,384]{1,0:T(8,128)} %get-tuple-element.234.refs_1_, f32[128,1024]{1,0:T(8,128)} %get-tuple-element.235.refs_2_, bf16[128,1280]{1,0:T(8,128)(2,1)} %get-tuple-element.176.refs_2_.refs_3_, ...), custom_call_target="tpu_custom_call" | custom-call | flops 2000000000 | bytes 8000000 | tf_op jit(solution)/shard_map/pallas_call | solution.py:216
  347.4 18.3 %all_to_all.65 = bf16[32,16,256]{2,1,0:T(8,128)(2,1)S(1)} all-to-all(bf16[32,16,256]{2,1,0:T(8,128)(2,1)S(1)} %bitcast.70), channel_id=1, replica_groups=mesh['x'=2,'core'=2,'tile'=8] {'x','core','tile'}, dimensions={0} | all-to-all | bytes 524288 | tf_op jit(solution)/shard_map/all_to_all | solution.py:1994
  365.8 16.9 %all_to_all.66 = bf16[32,16,256]{2,1,0:T(8,128)(2,1)S(1)} all-to-all(bf16[32,16,256]{2,1,0:T(8,128)(2,1)S(1)} %broadcast_in_dim.46), channel_id=1, replica_groups=mesh['x'=2,'core'=2,'tile'=8] {'x','core','tile'}, dimensions={0} | all-to-all | bytes 524288 | tf_op jit(solution)/shard_map/all_to_all | solution.py:1999
  385.5 59.5 %all-gather.3.cloned.1.call-done = bf16[13312,512]{1,0:T(8,128)(2,1)} async-done(((bf16[416,512]{1,0:T(8,128)(2,1)}), bf16[13312,512]{1,0:T(8,128)(2,1)}) %all-gather.3.cloned.1.call-update) | async-done | bytes 13631504 | tf_op jit(solution)/shard_map/all_gather | solution.py:2006
  445.0 15.2 %shard_map.417 = (f32[9,256,512]{2,1,0:T(8,128)}, f32[9,512,256]{2,1,0:T(8,128)}, f32[9,256,128]{2,1,0:T(8,128)}, f32[2048,512]{1,0:T(8,128)}, f32[512,2048]{1,0...) custom-call(bf16[32,416,512]{2,1,0:T(8,128)(2,1)} %bitcast.95), custom_call_target="tpu_custom_call" | custom-call | flops 7000000000 | bytes 28000000 | tf_op jit(solution)/shard_map/pallas_call | solution.py:1073
  (191 shorter events, 100.2 us)
Async XLA Ops:
  9.8 20.0 %all-to-all-start = ((bf16[8,24,1088]{2,1,0:T(8,128)(2,1)}), bf16[8,24,1088]{2,1,0:T(8,128)(2,1)S(1)}, u32[]{:S(2)}, u32[]{:S(2)}) async-start(bf16[8,24,1088]{2,1,0:T(8,128)(2,1)} %broadcast_in_dim.17), calls=%async_computation | async-start | bytes 884736 | tf_op jit(solution)/shard_map/all_to_all | solution.py:1611
  41.9 12.9 %all-to-all-start.1 = ((bf16[8,128,128]{2,1,0:T(8,128)(2,1)}), bf16[8,128,128]{2,1,0:T(8,128)(2,1)S(1)}, u32[]{:S(2)}, u32[]{:S(2)}) async-start(bf16[8,128,128]{2,1,0:T(8,128)(2,1)} %broadcast_in_dim.18), calls=%async_computation.1 | async-start | bytes 524288 | tf_op jit(solution)/shard_map/all_to_all | solution.py:1611
  48.0 16.7 %copy-start.1 = (bf16[3,3,128,256]{3,2,1,0:T(8,128)(2,1)S(1)}, bf16[3,3,128,256]{3,2,1,0:T(8,128)(2,1)}, u32[]{:S(2)}) copy-start(bf16[3,3,128,256]{3,2,1,0:T(8,128)(2,1)} %refs_8_.4) | copy-start | bytes 1769476
  74.0 20.3 %copy-start.5 = (bf16[512,512]{1,0:T(8,128)(2,1)S(1)}, bf16[512,512]{1,0:T(8,128)(2,1)}, u32[]{:S(2)}) copy-start(bf16[512,512]{1,0:T(8,128)(2,1)} %refs_5_.6) | copy-start | bytes 1572868
  74.0 20.3 %copy-start.6 = (bf16[512,512]{1,0:T(8,128)(2,1)S(1)}, bf16[512,512]{1,0:T(8,128)(2,1)}, u32[]{:S(2)}) copy-start(bf16[512,512]{1,0:T(8,128)(2,1)} %refs_6_.6) | copy-start | bytes 1572868
  74.0 20.3 %copy-start.13 = (bf16[1,128,512]{2,1,0:T(8,128)(2,1)S(1)}, bf16[1,128,512]{2,1,0:T(8,128)(2,1)}, u32[]{:S(2)}) copy-start(bf16[1,128,512]{2,1,0:T(8,128)(2,1)} %param.34) | copy-start | bytes 393220
  74.0 20.3 %copy-start.15 = (bf16[128,512]{1,0:T(8,128)(2,1)S(1)}, bf16[128,512]{1,0:T(8,128)(2,1)}, u32[]{:S(2)}) copy-start(bf16[128,512]{1,0:T(8,128)(2,1)} %refs_8_.3) | copy-start | bytes 393220
  82.1 12.1 %all-to-all-start.2 = ((bf16[8,128,128]{2,1,0:T(8,128)(2,1)}), bf16[8,128,128]{2,1,0:T(8,128)(2,1)S(1)}, u32[]{:S(2)}, u32[]{:S(2)}) async-start(bf16[8,128,128]{2,1,0:T(8,128)(2,1)} %bitcast.13), calls=%async_computation.2 | async-start | bytes 524288 | tf_op jit(solution)/shard_map/all_to_all | solution.py:1684
  97.3 14.8 %all-to-all-start.3 = ((bf16[8,192,128]{2,1,0:T(8,128)(2,1)}), bf16[8,192,128]{2,1,0:T(8,128)(2,1)S(1)}, u32[]{:S(2)}, u32[]{:S(2)}) async-start(bf16[8,192,128]{2,1,0:T(8,128)(2,1)} %get-tuple-element.180), calls=%async_computation.3 | async-start | bytes 786432 | tf_op jit(solution)/shard_map/all_to_all | solution.py:1695
  102.2 23.9 %copy-start.36 = (bf16[512]{0:T(512)(128)(2,1)S(1)}, bf16[512]{0:T(512)(128)(2,1)}, u32[]{:S(2)}) copy-start(bf16[512]{0:T(512)(128)(2,1)} %param.54) | copy-start | bytes 3076
  102.2 31.2 %copy-start.4 = (bf16[512,512]{1,0:T(8,128)(2,1)S(1)}, bf16[512,512]{1,0:T(8,128)(2,1)}, u32[]{:S(2)}) copy-start(bf16[512,512]{1,0:T(8,128)(2,1)} %refs_4_.3) | copy-start | bytes 1572868
  102.2 31.2 %copy-start.14 = (bf16[1,128,512]{2,1,0:T(8,128)(2,1)S(1)}, bf16[1,128,512]{2,1,0:T(8,128)(2,1)}, u32[]{:S(2)}) copy-start(bf16[1,128,512]{2,1,0:T(8,128)(2,1)} %param.57) | copy-start | bytes 393220
  122.4 11.0 %all-to-all-start.4 = ((bf16[8,64,128]{2,1,0:T(8,128)(2,1)}), bf16[8,64,128]{2,1,0:T(8,128)(2,1)S(1)}, u32[]{:S(2)}, u32[]{:S(2)}) async-start(bf16[8,64,128]{2,1,0:T(8,128)(2,1)} %get-tuple-element.181), calls=%async_computation.4 | async-start | bytes 262144 | tf_op jit(solution)/shard_map/all_to_all | solution.py:1699
  142.2 11.7 %all-to-all-start.5 = ((bf16[8,64,128]{2,1,0:T(8,128)(2,1)}), bf16[8,64,128]{2,1,0:T(8,128)(2,1)S(1)}, u32[]{:S(2)}, u32[]{:S(2)}) async-start(bf16[8,64,128]{2,1,0:T(8,128)(2,1)} %get-tuple-element.186), calls=%async_computation.5 | async-start | bytes 262144 | tf_op jit(solution)/shard_map/all_to_all | solution.py:1703
  145.6 189.7 %reduce-scatter.2.cloned.1.call-start = ((), (), s32[]{:S(2)}) async-start(), calls=%async_computation.14 | async-start | bytes 4866048 | tf_op jit(solution)/shard_map/reduce_scatter | solution.py:1707
  153.9 22.9 %copy-start.7 = (bf16[512,512]{1,0:T(8,128)(2,1)S(1)}, bf16[512,512]{1,0:T(8,128)(2,1)}, u32[]{:S(2)}) copy-start(bf16[512,512]{1,0:T(8,128)(2,1)} %refs_6_.6) | copy-start | bytes 1572868
  161.5 15.3 %all-to-all-start.6 = ((bf16[8,192,128]{2,1,0:T(8,128)(2,1)}), bf16[8,192,128]{2,1,0:T(8,128)(2,1)S(1)}, u32[]{:S(2)}, u32[]{:S(2)}) async-start(bf16[8,192,128]{2,1,0:T(8,128)(2,1)} %get-tuple-element.192), calls=%async_computation.6 | async-start | bytes 786432 | tf_op jit(solution)/shard_map/all_to_all | solution.py:1713
  182.3 4.5 collective-permute-start
  183.0 13.3 %all-to-all-start.7 = ((bf16[8,128,128]{2,1,0:T(8,128)(2,1)}), bf16[8,128,128]{2,1,0:T(8,128)(2,1)S(1)}, u32[]{:S(2)}, u32[]{:S(2)}) async-start(bf16[8,128,128]{2,1,0:T(8,128)(2,1)} %broadcast_in_dim.21), calls=%async_computation.7 | async-start | bytes 524288 | tf_op jit(solution)/shard_map/all_to_all | solution.py:1611
  189.2 21.8 %collective-permute-start.3 = (bf16[512,512]{1,0:T(8,128)(2,1)}, bf16[512,512]{1,0:T(8,128)(2,1)S(1)}, u32[]{:S(2)}, u32[]{:S(2)}) collective-permute-start(bf16[512,512]{1,0:T(8,128)(2,1)} %get-tuple-element.214), channel_id=1, source_target_pairs={{0,16},{16,0},{1,17},{17,1},{2,18},{18,2},{3,19},{19,3},{4,20},{20... | collective-permute-start | bytes 1572872 | tf_op jit(solution)/shard_map/ppermute | solution.py:1647
  205.8 23.1 %copy-start.2 = (bf16[3,3,128,256]{3,2,1,0:T(8,128)(2,1)S(1)}, bf16[3,3,128,256]{3,2,1,0:T(8,128)(2,1)}, u32[]{:S(2)}) copy-start(bf16[3,3,128,256]{3,2,1,0:T(8,128)(2,1)} %refs_8_.4) | copy-start | bytes 1769476
  205.8 23.1 %collective-permute-start.1 = (bf16[32,5632]{1,0:T(8,128)(2,1)}, bf16[32,5632]{1,0:T(8,128)(2,1)S(1)}, u32[]{:S(2)}, u32[]{:S(2)}) collective-permute-start(bf16[32,5632]{1,0:T(8,128)(2,1)} %get-tuple-element.208), channel_id=1, source_target_pairs={{0,1},{1,2},{2,3},{3,4},{4,5},{5,6},{6,7},{8,9},{9,10},{10,11},{11... | collective-permute-start | bytes 1081352 | tf_op jit(solution)/shard_map/ppermute | solution.py:1624
  209.3 19.6 %collective-permute-start.2 = (bf16[32,5632]{1,0:T(8,128)(2,1)S(1)}, bf16[32,5632]{1,0:T(8,128)(2,1)S(1)}, u32[]{:S(2)}, u32[]{:S(2)}) collective-permute-start(bf16[32,5632]{1,0:T(8,128)(2,1)S(1)} %get-tuple-element.210), channel_id=1, source_target_pairs={{1,0},{2,1},{3,2},{4,3},{5,4},{6,5},{7,6},{9,8},{10,9},{11,10},{12... | collective-permute-start | bytes 1081352 | tf_op jit(solution)/shard_map/ppermute | solution.py:1624
  211.8 28.5 %copy-start.16 = (bf16[256,512]{1,0:T(8,128)(2,1)}, bf16[256,512]{1,0:T(8,128)(2,1)S(1)}, u32[]{:S(2)}) copy-start(bf16[256,512]{1,0:T(8,128)(2,1)S(1)} %get-tuple-element.221.refs_1_) | copy-start | bytes 786436
  230.0 20.0 %copy-start.24 = (bf16[32,8192]{1,0:T(8,128)(2,1)S(1)}, bf16[32,8192]{1,0:T(8,128)(2,1)}, u32[]{:S(2)}) copy-start(bf16[32,8192]{1,0:T(8,128)(2,1)} %copy-done.22) | copy-start | bytes 1572868
  241.2 26.6 %all-to-all-start.8 = ((bf16[8,256,128]{2,1,0:T(8,128)(2,1)}), bf16[8,256,128]{2,1,0:T(8,128)(2,1)S(1)}, u32[]{:S(2)}, u32[]{:S(2)}) async-start(bf16[8,256,128]{2,1,0:T(8,128)(2,1)} %broadcast_in_dim.22), calls=%async_computation.8 | async-start | bytes 1048576 | tf_op jit(solution)/shard_map/all_to_all | solution.py:1611
  247.9 13.5 %collective-permute-start.4 = (bf16[256,512]{1,0:T(8,128)(2,1)S(1)}, bf16[256,512]{1,0:T(8,128)(2,1)S(1)}, u32[]{:S(2)}, u32[]{:S(2)}) collective-permute-start(bf16[256,512]{1,0:T(8,128)(2,1)S(1)} %get-tuple-element.222), channel_id=1, source_target_pairs={{0,1},{1,0},{2,3},{3,2},{4,5},{5,4},{6,7},{7,6},{8,9},{9,8},{10,11... | collective-permute-start | bytes 786440 | tf_op jit(solution)/shard_map/ppermute | solution.py:1647
  267.8 53.1 %all-to-all-start.12 = ((bf16[32,48,256]{2,1,0:T(8,128)(2,1)}), bf16[32,48,256]{2,1,0:T(8,128)(2,1)S(1)}, u32[]{:S(2)}, u32[]{:S(2)}) async-start(bf16[32,48,256]{2,1,0:T(8,128)(2,1)} %bitcast.36), calls=%async_computation.13 | async-start | bytes 1572864 | tf_op jit(solution)/shard_map/all_to_all | solution.py:1964
  273.4 28.0 %collective-permute-start.5 = (bf16[128,512]{1,0:T(8,128)(2,1)S(1)}, bf16[128,512]{1,0:T(8,128)(2,1)S(1)}, u32[]{:S(2)}, u32[]{:S(2)}) collective-permute-start(bf16[128,512]{1,0:T(8,128)(2,1)S(1)} %get-tuple-element.225), channel_id=1, source_target_pairs={{0,4},{1,5},{2,6},{3,7},{4,0},{5,1},{6,2},{7,3},{8,12},{9,13},{10,... | collective-permute-start | bytes 393224 | tf_op jit(solution)/shard_map/ppermute | solution.py:1647
  320.9 14.4 %all-to-all-start.11 = ((bf16[4,176,512]{2,1,0:T(8,128)(2,1)}), bf16[4,176,512]{2,1,0:T(8,128)(2,1)S(1)}, u32[]{:S(2)}, u32[]{:S(2)}) async-start(bf16[4,176,512]{2,1,0:T(8,128)(2,1)} %get-tuple-element.249), calls=%async_computation.11 | async-start | bytes 1441792 | tf_op jit(solution)/shard_map/all_to_all | solution.py:2004
  324.4 120.6 %all-gather.3.cloned.1.call-start = ((), (), s32[]{:S(2)}) async-start(), calls=%async_computation.15 | async-start | bytes 14057472 | tf_op jit(solution)/shard_map/all_gather | solution.py:2006
  324.6 4.5 collective-permute-start.6
  (25 other events, 139.8 us)
Sparse Core Ops, SparseCore 0:
  154.0 129.9 reduce-scatter.1
  337.8 107.2 all-gather.2

commit v3 on v2

--- a/solution.py
+++ b/solution.py
@@ -441,7 +441,7 @@
             target[:, (2 * n + m) * 2 * width : (2 * n + m + 1) * 2 * width] = line
 
 
-def up_body(ids, dec_three, pre_two, pre_one, pre_zero, w_third, w_second, w_first, pre_up_two, pre_up_one, pre_up_zero, u_three, dec_two, dec_one, features, wide_two, stack_two, wide_one, stack_one):
+def up_body(ids, dec_three, pre_two, pre_one, pre_zero, w_third, w_second, w_first, pre_up_two, pre_up_one, pre_up_zero, u_three, dec_two, dec_one, features, edge_end, edge_start, wide_two, stack_two, wide_one, stack_one):
     tile, high, place = ids[0], ids[1], ids[2]
     block = dec_three[:, lanes_at(place * 128, 384)]
     wide = widened(block)
@@ -489,6 +489,9 @@
                 :, 512 * n : 512 * n + 512
             ]
 
+    edge_end[...] = pre_up_zero[:, 5 * 512 : 16 * 512]
+    edge_start[...] = pre_up_zero[:, 0 : 11 * 512]
+
 
 def run_up(ids, dec_three, pre_two, pre_one, pre_zero, w_third, w_second, w_first):
     return call(
@@ -502,6 +505,8 @@
             ((128, 8 * 128), bf16),
             ((64, 10 * 256), bf16),
             ((16 * 32, 512), bf16),
+            ((32, 11 * 512), bf16),
+            ((32, 11 * 512), bf16),
         ],
         [
             ((128, 20 * 256), bf16),
@@ -563,13 +568,14 @@
     )[0]
 
 
-def unpool_body(step, ids, boxes, d_pooled, pre_up, d_features, d_low, low_end, low_start, token, total):
+def unpool_body(step, ids, boxes, d_pooled, pre_before, pre_up, pre_behind, d_features, d_low, token, total):
     tile = ids[0]
+    lines = 38
     x_ids = lane_ids((1, 512))
-    y_ids = (x_ids >> 5) + tile * 16
+    y_ids = (lane_ids((1, lines * 32)) >> 5) + (tile * 16 - 11)
     group = lane_ids((1, 128)) >> 5
-    source = row_ids_of((128, 512))
-    target = lane_ids((1, 512)) & 31
+    source = row_ids_of((128, lines * 32))
+    target = lane_ids((1, lines * 32)) & 31
     copies = [
         jnp.where(source == target + 32 * n, 1.0, 0.0).astype(bf16) for n in range(4)
     ]
@@ -593,43 +599,36 @@
             found = term if found is None else found + term
         total[...] += found
 
-    for y in range(16):
-        own = slice(512 * y, 512 * y + 512)
+    for y in range(lines):
         line = total[32 * y : 32 * y + 32, :]
-        d_features[:, own] = line
-        low = (line * gelu_slope(pre_up[:, own])).astype(bf16)
-        d_low[:, own] = low
-        if y >= 5:
-            low_end[:, 512 * (y - 5) : 512 * (y - 4)] = low
         if y < 11:
-            low_start[:, own] = low
-
-
-def run_unpool(ids, after, boxes, d_pooled, pre_up, step):
+            pre = pre_before[:, 512 * y : 512 * y + 512]
+        elif y < 27:
+            own = slice(512 * (y - 11), 512 * (y - 10))
+            d_features[:, own] = line
+            pre = pre_up[:, own]
+        else:
+            pre = pre_behind[:, 512 * (y - 27) : 512 * (y - 26)]
+        d_low[:, 512 * y : 512 * y + 512] = (line * gelu_slope(pre)).astype(bf16)
+
+
+def run_unpool(ids, after, boxes, d_pooled, pre_before, pre_up, pre_behind, step):
     return call(
-        8,
+        14,
         functools.partial(unpool_body, step),
-        [
-            ((32, 8192), f32),
-            ((32, 8192), bf16),
-            ((32, 11 * 512), bf16),
-            ((32, 11 * 512), bf16),
-            TOKEN,
-        ],
-        [((512, 512), f32)],
+        [((32, 8192), f32), ((32, 38 * 512), bf16), TOKEN],
+        [((38 * 32, 512), f32)],
         ids,
-        (boxes, d_pooled, pre_up),
+        (boxes, d_pooled, pre_before, pre_up, pre_behind),
         after,
-        late=(2,),
+        late=(2, 3, 4),
         sent=(0,),
     )
 
 
-def up_back_body(ids, before, d_low, behind, pre_up_one, pre_up_two, wd_first, wd_second, w_third, d_dec_one, d_dec_two, d_dec_three, low_one, low_two, token, stack_zero, wide_low):
+def up_back_body(ids, d_low, pre_up_one, pre_up_two, wd_first, wd_second, w_third, d_dec_one, d_dec_two, d_dec_three, low_one, low_two, token, stack_zero, wide_low):
     tile, high = ids[0], ids[1]
-    reach = 11 * 512
-    for first, piece in ((0, before), (reach, d_low), (reach + 8192, behind)):
-        stack_zero[:, first : first + piece.shape[1]] = stack_cols(piece[...], 512)
+    stack_zero[...] = stack_cols(d_low[...], 512)
     halve = halving(512, 1.0)
     pre_up_one.ready()
 
@@ -687,7 +686,7 @@
     d_dec_three[...] = mm_fine(pairs, pair_halving(1.0)).astype(bf16)
 
 
-def run_up_back(ids, after, before, d_low, behind, pre_up_one, pre_up_two, wd_first, wd_second, w_third):
+def run_up_back(ids, after, d_low, pre_up_one, pre_up_two, wd_first, wd_second, w_third):
     return call(
         9,
         up_back_body,
@@ -701,9 +700,9 @@
         ],
         [((96, 38 * 512), bf16), ((64, 18 * 256), bf16)],
         ids,
-        (before, d_low, behind, pre_up_one, pre_up_two, wd_first, wd_second, w_third),
+        (d_low, pre_up_one, pre_up_two, wd_first, wd_second, w_third),
         after,
-        late=(3, 4),
+        late=(1, 2),
         sent=(0, 1, 3, 4),
     )
 
@@ -825,7 +824,7 @@
     spread_rows(dec_one[...], wide_one, 256)
     stack_one[...] = stack_cols(wide_one[...], 512)
     for i in range(3):
-        grad[i] = mm_nt(d_low[...], stack_one[:, (1 + i) * 512 : (17 + i) * 512])
+        grad[i] = mm_nt(d_low[:, 11 * 512 : 27 * 512], stack_one[:, (1 + i) * 512 : (17 + i) * 512])
 
 
 def run_grad_up_first(ids, after, dec_one, d_low):
@@ -1210,10 +1209,13 @@
         total = total + pieces[n].astype(f32)
     low = total.astype(bf16)
     pooled[...] = low
+    pooled.send()
     resid = emb[...].astype(f32) + mm(low, roi[...])
     residual[...] = resid
+    residual.send()
     normal = (resid * norm_parts(resid) * gain[...].astype(f32)).astype(bf16)
     normed[...] = normal
+    normed.send()
     for n, weight in enumerate((wq, wk, wv)):
         turned = mm(normal, weight[...]).T.astype(bf16)
         for h in range(HEADS):
@@ -1234,6 +1236,7 @@
         [],
         ids,
         (pieces, emb, *arrays),
+        sent=(0, 1, 2),
     )
 
 
@@ -1425,18 +1428,24 @@
     wide_gain = gain[...].astype(f32)
     low = (mixed * norm_parts(mixed) * wide_gain).astype(bf16)
     ffn_low[...] = low
+    ffn_low.send()
     pre = mm(low, w_in[...])
     hidden = gelu_of(pre).astype(bf16)
     act[...] = hidden
+    act.send()
     result[...] = (mixed + mm(hidden, w_down[...])).astype(bf16)
+    result.send()
     d_hidden = (mm_nt(upstream[...], w_down[...]) * gelu_slope(pre)).astype(bf16)
     d_pre[...] = d_hidden
+    d_pre.send()
     d_norm, gain_sum = norm_back(mixed, wide_gain, mm_nt(d_hidden, w_in[...]))
     d_gain[...] = gain_sum
     d_sum = upstream[...].astype(f32) + d_norm
     d_mixed[...] = d_sum
+    d_mixed.send()
     narrow = d_sum.astype(bf16)
     d_low[...] = narrow
+    d_low.send()
     back = mm_nt(w_out[...], narrow).astype(bf16)
     for h in range(HEADS):
         d_found[h] = back[HD * h : HD * h + HD, :]
@@ -1462,6 +1471,7 @@
         ids,
         (found, residual, upstream, w_out, gain, w_in, w_down),
         late=(5, 6),
+        sent=(0, 1, 2, 3, 4, 5),
     )
 
 
@@ -1489,7 +1499,16 @@
 
 
 def run_mixer_grads(ids, *arrays):
-    return call(4, mixer_grads_body, [((4608, 512), bf16), TOKEN], [], ids, arrays)
+    return call(
+        4,
+        mixer_grads_body,
+        [((4608, 512), bf16), TOKEN],
+        [],
+        ids,
+        arrays,
+        late=(1, 5, 3, 2, 4),
+        sent=(0,),
+    )
 
 
 def embed_back_body(ids, d_shared, residual, d_mixed, gain, wq, wk, wv, roi, d_resid, d_low, d_pooled, d_gain, d_rows, token):
@@ -1503,6 +1522,7 @@
     d_gain[...] = gain_sum
     total = d_mixed[...] + d_norm
     d_resid[...] = total
+    d_resid.send()
     low = total.astype(bf16)
     d_low[...] = low
     d_pooled[...] = mm_nt(low, roi[...]).astype(bf16)
@@ -1525,6 +1545,8 @@
         [],
         ids,
         (d_shared, residual, *arrays),
+        late=(1, 2),
+        sent=(0,),
     )
 
 
@@ -1677,9 +1699,20 @@
     pre_three, pre_four, p_four, e_four, pre_up_three, dec_three = run_bottom(
         cut, ids, p_three_all, down_fourth, down_fifth, up_fourth
     )
-    pre_up_two, pre_up_one, pre_up_zero, u_three, dec_two, dec_one, features = run_up(
+    (
+        pre_up_two,
+        pre_up_one,
+        pre_up_zero,
+        u_three,
+        dec_two,
+        dec_one,
+        features,
+        edge_end,
+        edge_start,
+    ) = run_up(
         ids, dec_three, pre_two, pre_one, pre_zero, up_third, lined(up_second), lined(up_first)
     )
+    pre_up_edges = (from_side(edge_end, 1), from_side(edge_start, -1))
     pooled_own = run_pool(ids, box_rows, features, 256)
     pieces = lax.all_to_all(
         pooled_own.reshape(tile_count, tok_rows, -1), "tile", 0, 0, tiled=True
@@ -1917,18 +1950,23 @@
             axis=0,
         ).astype(jnp.bfloat16)
     d_pooled_all = gathered(d_pooled).reshape(seq_all, -1)
-    d_features, low_zero_up, low_end, low_start, box_token = run_unpool(
-        ids, ordering, box_rows, d_pooled_all, pre_up_zero, 256
+    d_features, low_zero_up, box_token = run_unpool(
+        ids,
+        ordering,
+        box_rows,
+        d_pooled_all,
+        pre_up_edges[0],
+        pre_up_zero,
+        pre_up_edges[1],
+        256,
     )
     if heads_first:
         embed_halves = halved(embed_halves, 1, box_token)
-        ordering = embed_halves[2:]
+        ordering = ()
     d_dec_one, d_dec_two, d_dec_three, low_one_up, low_two_up, up_token = run_up_back(
         ids,
         ordering,
-        from_side(low_end, 1),
         low_zero_up,
-        from_side(low_start, -1),
         pre_up_one,
         pre_up_two,
         lined_back(up_first),
@@ -1943,13 +1981,10 @@
     light_early, early_token = run_grad_up(
         ids, ordering, grad_up_first, dec_two, low_one_up, u_three, low_two_up
     )
-    if heads_first:
-        embed_halves = halved(embed_halves, 3, up_token)
-        ordering = embed_halves[2:]
     low_three_up, low_four, low_three, d_pool_three, bottom_token = run_bottom_back(
         cut,
         ids,
-        (*ordering, early_token),
+        (early_token,),
         d_dec_three_all,
         pre_up_three,
         pre_four,
@@ -1960,7 +1995,7 @@
     )
     dp_count = lax.axis_size(PAGES)
     if heads_first:
-        embed_share = halved(embed_halves, 4, bottom_token)
+        embed_share = halved(halved(embed_halves, 3, bottom_token), 4)
         early_parts = lax.all_to_all(
             light_early.reshape(32, -1, 256), (*PAGES, "tile"), 0, 0, tiled=True
         )

time: 478 us -> 448 us (0.937)
  waiting for transfers between devices: 174 us -> 147 us
  local copies, waits for them, and re-layouts: 34.6 us -> 23 us
  Pallas kernels: 150 us -> 159 us
    ppermute x5, waiting for transfers between devices: 36.3 us -> 15.4 us  [swapped(): return lax.ppermute(block, axis, hops)]
    unnamed x86 -> x68, local copies, waits for them, and re-layouts: 19 us -> 8.58 us
    pallas_call x26, Pallas kernels: 135 us -> 144 us  [call(): pl.pallas_call(ordered, cost_estimate=price(micros), out_shape=[pltpu.HBM...]
    all_to_all x1, waiting for transfers between devices: 4.94 us -> 0.01 us  [on_device(): parts = lax.all_to_all(heavy, PAGES, 0, 0, tiled=True)]
  transfers between devices with their start and end apart: 20 -> 20, of which waited for: 13 -> 13; matrix products, arithmetic and copies ran while one was open for 3% -> 2% of each run, Pallas kernels for 16% -> 19%
where the time goes in v3:
time: 448 us; the launch traced here: 442 us
  Pallas kernels  159 us (35%)
  waiting for transfers between devices  147 us (33%)
  starting transfers between devices  61.7 us (14%)
  blocking collectives  35.6 us (8%)
  local copies, waits for them, and re-layouts  23 us (5%)
  between operations  15.2 us (3%)
    pallas_call x26, Pallas kernels, call(): pl.pallas_call(ordered, cost_estimate=price(micros), out_shape=[pltpu.HBM...  144 us
    all_gather x1, waiting for transfers between devices, on_device(): whole = lax.all_gather(share, both_axes, axis=0)  59.5 us
    all_to_all x4, starting transfers between devices, gathered(): return lax.all_to_all(copies, 'tile', 0, 0, tiled=True)  22.1 us
    all_to_all x1, blocking collectives, summed_share(): parts = lax.all_to_all(parts, both_axes, 0, 0, tiled=True)  18.5 us
    all_to_all x4, waiting for transfers between devices, gathered(): return lax.all_to_all(copies, 'tile', 0, 0, tiled=True)  18.1 us
    all_to_all x1, blocking collectives, spread_out(): return lax.all_to_all(copies, both_axes, 0, 0, tiled=True)  17 us
    ppermute x5, waiting for transfers between devices, swapped(): return lax.ppermute(block, axis, hops)  15.4 us
    pallas_call x1, Pallas kernels, run_unpack(): pl.pallas_call(unpack_body, cost_estimate=price(14), grid=(whole.shape[0]...  15.2 us
  transfers between devices with their start and end apart: 20, of which 13 were waited for; matrix products, arithmetic and copies ran while one was open for 2% of the time, Pallas kernels for 19%

profile of v3, /device:TPU:0, one launch (start us, length us, event | category | flops | bytes accessed | tf_op | source)
XLA Modules:
  0.0 442.5 jit_solution(16716402383598612348)
XLA Ops:
  9.8 7.3 %all-to-all-start = ((bf16[8,24,1088]{2,1,0:T(8,128)(2,1)}), bf16[8,24,1088]{2,1,0:T(8,128)(2,1)S(1)}, u32[]{:S(2)}, u32[]{:S(2)}) async-start(bf16[8,24,1088]{2,1,0:T(8,128)(2,1)} %broadcast_in_dim.17), calls=%async_computation | async-start | bytes 884736 | tf_op jit(solution)/shard_map/all_to_all | solution.py:1633
  20.2 9.6 %all-to-all-done.refs_1_ = bf16[8,24,1088]{2,1,0:T(8,128)(2,1)S(1)} async-done(((bf16[8,24,1088]{2,1,0:T(8,128)(2,1)}), bf16[8,24,1088]{2,1,0:T(8,128)(2,1)S(1)}, u32[]{:S(2)}, u32[]{:S(2)}) %all-to-all-start) | async-done | bytes 417824 | tf_op jit(solution)/shard_map/all_to_all | solution.py:1633
  29.9 11.3 %shard_map.391 = (bf16[32,8192]{1,0:T(8,128)(2,1)}, bf16[64,4096]{1,0:T(8,128)(2,1)}, bf16[32,2560]{1,0:T(8,128)(2,1)}, bf16[128,1280]{1,0:T(8,128)(2,1)}, bf16[...) custom-call(s32[6]{0:T(128)S(1)} %stack.9.refs_0_, ...), custom_call_target="tpu_custom_call" | custom-call | flops 5000000000 | bytes 20000000 | tf_op jit(solution)/shard_map/pallas_call | solution.py:216
  46.2 8.5 %all-to-all-done.1.refs_1_.refs_6_ = bf16[8,128,128]{2,1,0:T(8,128)(2,1)S(1)} async-done(((bf16[8,128,128]{2,1,0:T(8,128)(2,1)}), bf16[8,128,128]{2,1,0:T(8,128)(2,1)S(1)}, u32[]{:S(2)}, u32[]{:S(2)}) %all-to-all-start.1) | async-done | bytes 262176 | tf_op jit(solution)/shard_map/all_to_all | solution.py:1633
  54.7 10.0 %shard_map.392 = (bf16[256,1024]{1,0:T(8,128)(2,1)}, bf16[512,256]{1,0:T(8,128)(2,1)}, bf16[256,256]{1,0:T(8,128)(2,1)}, bf16[512,256]{1,0:T(8,128)(2,1)}, bf16[...) custom-call(s32[6]{0:T(128)S(1)} %stack.9.refs_0_, bf16[8,128,128]{2,1,0:T(8,128)(2,1)S(1)} %all-to-all-done.1.refs_1_.refs_6_, ...), custom_call_target="tpu_custom_call" | custom-call | flops 5500000256 | bytes 22000000 | tf_op jit(solution)/shard_map/pallas_call | solution.py:216
  64.7 10.2 %shard_map.393 = (bf16[128,1280]{1,0:T(8,128)(2,1)}, bf16[64,4608]{1,0:T(8,128)(2,1)}, bf16[32,8192]{1,0:T(8,128)(2,1)}, bf16[256,768]{1,0:T(8,128)(2,1)}, bf16[...) custom-call(s32[6]{0:T(128)S(1)} %stack.9.refs_0_, ...), custom_call_target="tpu_custom_call" | custom-call | flops 4499999744 | bytes 18000000 | tf_op jit(solution)/shard_map/pallas_call | solution.py:216
  74.9 7.8 %shard_map.394 = bf16[1024,128]{1,0:T(8,128)(2,1)} custom-call(s32[6]{0:T(128)S(1)} %stack.9.refs_0_, s32[1024,8]{1,0:T(8,128)S(1)} %pad_bitcast_fusion.refs_1_.refs_3_, bf16[512,512]{1,0:T(8,128)(2,1)S(1)} %get-tuple-element.177.refs_2_), custom_call_target="tpu_custom_call" | custom-call | flops 4000000000 | bytes 16000000 | tf_op jit(solution)/shard_map/pallas_call | solution.py:216
  86.3 8.5 %all-to-all-done.2.refs_1_ = bf16[8,128,128]{2,1,0:T(8,128)(2,1)S(1)} async-done(((bf16[8,128,128]{2,1,0:T(8,128)(2,1)}), bf16[8,128,128]{2,1,0:T(8,128)(2,1)S(1)}, u32[]{:S(2)}, u32[]{:S(2)}) %all-to-all-start.2) | async-done | bytes 262176 | tf_op jit(solution)/shard_map/all_to_all | solution.py:1717
  102.3 11.0 %all-to-all-done.3.refs_4_.refs_2_ = bf16[8,192,128]{2,1,0:T(8,128)(2,1)S(1)} async-done(((bf16[8,192,128]{2,1,0:T(8,128)(2,1)}), bf16[8,192,128]{2,1,0:T(8,128)(2,1)S(1)}, u32[]{:S(2)}, u32[]{:S(2)}) %all-to-all-start.3) | async-done | bytes 393248 | tf_op jit(solution)/shard_map/all_to_all | solution.py:1728
  113.3 10.3 %shard_map.396 = (bf16[4,1024,256]{2,1,0:T(8,128)(2,1)}, bf16[8,64,128]{2,1,0:T(8,128)(2,1)}, f32[64,1024]{1,0:T(8,128)}) custom-call(s32[6]{0:T(128)S(1)} %stack.9.refs_0_, f32[8,96]{1,0:T(8,128)S(1)} %convert_element_type.28.refs_1_, s32[8,1024]{1,0:T(8,128)S(1)} %pad.18.clone.refs_2_.refs_1_, s32[1024,8]{1,0:T(8,128)S(1)} %pad_bitcast_fusion.refs_1_.refs_3_, ...), custom_call_target="tpu_custom_call" | custom-call | flops 4499999744 | bytes 18000000 | tf_op jit(solution)/shard_map/pallas_call | solution.py:216
  127.2 7.3 %all-to-all-done.4.refs_1_ = bf16[8,64,128]{2,1,0:T(8,128)(2,1)S(1)} async-done(((bf16[8,64,128]{2,1,0:T(8,128)(2,1)}), bf16[8,64,128]{2,1,0:T(8,128)(2,1)S(1)}, u32[]{:S(2)}, u32[]{:S(2)}) %all-to-all-start.4) | async-done | bytes 131104 | tf_op jit(solution)/shard_map/all_to_all | solution.py:1732
  134.6 6.8 %shard_map.397 = (bf16[128,512]{1,0:T(8,128)(2,1)}, bf16[128,2048]{1,0:T(8,128)(2,1)}, bf16[128,2048]{1,0:T(8,128)(2,1)}, bf16[128,512]{1,0:T(8,128)(2,1)}, f32[...) custom-call(s32[6]{0:T(128)S(1)} %stack.9.refs_0_, ...), custom_call_target="tpu_custom_call" | custom-call | flops 2500000000 | bytes 10000000 | tf_op jit(solution)/shard_map/pallas_call | solution.py:216
  145.2 5.9 %shard_map.398 = (bf16[4608,512]{1,0:T(8,128)(2,1)}, f32[8,128]{1,0:T(8,128)}) custom-call(s32[6]{0:T(128)S(1)} %stack.9.refs_0_, bf16[8,64,128]{2,1,0:T(8,128)(2,1)S(1)} %all-to-all-done.4.refs_1_, bf16[128,2048]{1,0:T(8,128)(2,1)} %get-tuple-element.185.refs_2_, bf16[128,2048]{1,0:T(8,128)(2,1)} %get-tuple-element.186.refs_3_, ...), custom_call_target="tpu_custom_call" | custom-call | flops 2000000000 | bytes 8000000 | tf_op jit(solution)/shard_map/pallas_call | solution.py:216
  152.1 7.6 %shard_map.399 = (bf16[8,192,128]{2,1,0:T(8,128)(2,1)}, f32[32,128]{1,0:T(8,128)S(1)}) custom-call(s32[6]{0:T(128)S(1)} %stack.9.refs_0_, s32[8,1024]{1,0:T(8,128)S(1)} %pad.18.clone.refs_2_.refs_1_, bf16[8,192,128]{2,1,0:T(8,128)(2,1)S(1)} %all-to-all-done.3.refs_4_.refs_2_, bf16[4,1024,256]{2,1,0:T(8,128)(2,1)} %get-tuple-element.182.refs_3_, ...), custom_call_target="tpu_custom_call" | custom-call | flops 3000000000 | bytes 12000000 | tf_op jit(solution)/shard_map/pallas_call | solution.py:216
  159.7 5.2 %all-to-all-start.6 = ((bf16[8,192,128]{2,1,0:T(8,128)(2,1)}), bf16[8,192,128]{2,1,0:T(8,128)(2,1)S(1)}, u32[]{:S(2)}, u32[]{:S(2)}) async-start(bf16[8,192,128]{2,1,0:T(8,128)(2,1)} %get-tuple-element.190), calls=%async_computation.6 | async-start | bytes 786432 | tf_op jit(solution)/shard_map/all_to_all | solution.py:1746
  164.9 9.4 %all-to-all-done.6.refs_1_ = bf16[8,192,128]{2,1,0:T(8,128)(2,1)S(1)} async-done(((bf16[8,192,128]{2,1,0:T(8,128)(2,1)}), bf16[8,192,128]{2,1,0:T(8,128)(2,1)S(1)}, u32[]{:S(2)}, u32[]{:S(2)}) %all-to-all-start.6) | async-done | bytes 393248 | tf_op jit(solution)/shard_map/all_to_all | solution.py:1746
  185.2 4.7 %collective-permute-start = (bf16[32,5632]{1,0:T(8,128)(2,1)}, bf16[32,5632]{1,0:T(8,128)(2,1)}, u32[]{:S(2)}, u32[]{:S(2)}) collective-permute-start(bf16[32,5632]{1,0:T(8,128)(2,1)} %get-tuple-element.195), channel_id=1, source_target_pairs={{0,1},{1,2},{2,3},{3,4},{4,5},{5,6},{6,7},{8,9},{9,10},{10,11},{11... | collective-permute-start | bytes 1081352 | tf_op jit(solution)/shard_map/ppermute | solution.py:1646
  197.1 12.5 %collective-permute-done.refs_3_ = bf16[32,5632]{1,0:T(8,128)(2,1)} collective-permute-done((bf16[32,5632]{1,0:T(8,128)(2,1)}, bf16[32,5632]{1,0:T(8,128)(2,1)}, u32[]{:S(2)}, u32[]{:S(2)}) %collective-permute-start) | collective-permute-done | bytes 360480 | tf_op jit(solution)/shard_map/ppermute | solution.py:1646
  209.6 11.6 %shard_map.403 = (f32[32,8192]{1,0:T(8,128)}, bf16[32,19456]{1,0:T(8,128)(2,1)S(1)}, f32[8,128]{1,0:T(8,128)}) custom-call(s32[6]{0:T(128)S(1)} %stack.9.refs_0_, s32[1024,8]{1,0:T(8,128)S(1)} %pad_bitcast_fusion.refs_1_.refs_3_, bf16[1024,128]{1,0:T(8,128)(2,1)S(1)} %bitcast.69, bf16[32,5632]{1,0:T(8,128)(2,1)} %collective-permute-done.refs_3_, ...), custom_call_target="tpu_custom_call" | custom-call | flops 7000000000 | bytes 28000000 | tf_op jit(solution)/shard_map/pallas_call | solution.py:216
  221.2 10.0 %shard_map.404 = (f32[64,4608]{1,0:T(8,128)}, f32[128,1024]{1,0:T(8,128)}, bf16[256,128]{1,0:T(8,128)(2,1)S(1)}, bf16[64,2048]{1,0:T(8,128)(2,1)}, bf16[128,512]{1,0:T(8,128)(2,1)}, /*index=5*/f32[8,128]{1,0:T(8,128)}) custom-call(s32[6]{0:T(128)S(1)} %stack.9.refs_0_, bf16[32,19456]{1,0:T(8,128)(2,1)S(1)} %get-tuple-element.208.refs_1_.refs_2_, ...), custom_call_target="tpu_custom_call" | custom-call | flops 4499999744 | bytes 18000000 | tf_op jit(solution)/shard_map/pallas_call | solution.py:216
  232.1 7.3 %all-to-all-start.8 = ((bf16[8,256,128]{2,1,0:T(8,128)(2,1)}), bf16[8,256,128]{2,1,0:T(8,128)(2,1)S(1)}, u32[]{:S(2)}, u32[]{:S(2)}) async-start(bf16[8,256,128]{2,1,0:T(8,128)(2,1)} %broadcast_in_dim.22), calls=%async_computation.8 | async-start | bytes 1048576 | tf_op jit(solution)/shard_map/all_to_all | solution.py:1633
  243.5 4.8 %shard_map.405.refs_1_ = f32[3,32,192]{2,1,0:T(8,128)S(1)} custom-call(s32[6]{0:T(128)S(1)} %stack.9.refs_0_, bf16[64,2560]{1,0:T(8,128)(2,1)} %get-tuple-element.215.refs_1_, bf16[32,19456]{1,0:T(8,128)(2,1)S(1)} %copy-done.18, f32[8,128]{1,0:T(8,128)} %get-tuple-element.216.refs_3_), custom_call_target="tpu_custom_call" | custom-call | flops 2000000000 | bytes 8000000 | tf_op jit(solution)/shard_map/pallas_call | solution.py:216
  251.0 5.8 %shard_map.408 = (bf16[1536,256]{1,0:T(8,128)(2,1)}, f32[8,128]{1,0:T(8,128)}) custom-call(s32[6]{0:T(128)S(1)} %stack.9.refs_0_, f32[3,32,192]{2,1,0:T(8,128)S(1)} %shard_map.405.refs_1_, bf16[128,1024]{1,0:T(8,128)(2,1)} %get-tuple-element.217.refs_2_, bf16[64,2048]{1,0:T(8,128)(2,1)} %get-tuple-element.218.refs_3_, ...), custom_call_target="tpu_custom_call" | custom-call | flops 2000000000 | bytes 8000000 | tf_op jit(solution)/shard_map/pallas_call | solution.py:216
  256.8 6.3 %all-to-all-start.12 = ((bf16[32,48,256]{2,1,0:T(8,128)(2,1)}), bf16[32,48,256]{2,1,0:T(8,128)(2,1)S(1)}, u32[]{:S(2)}, u32[]{:S(2)}) async-start(bf16[32,48,256]{2,1,0:T(8,128)(2,1)} %bitcast.36), calls=%async_computation.13 | async-start | bytes 1572864 | tf_op jit(solution)/shard_map/all_to_all | solution.py:1999
  263.1 11.3 %shard_map.409 = (bf16[256,1024]{1,0:T(8,128)(2,1)S(1)}, bf16[512,256]{1,0:T(8,128)(2,1)S(1)}, bf16[256,1024]{1,0:T(8,128)(2,1)S(1)}, f32[128,384]{1,0:T(8,128)}, f32[8,128]{1,0:T(8,128)}) custom-call(s32[6]{0:T(128)S(1)} %stack.9.refs_0_, bf16[8,256,128]{2,1,0:T(8,128)(2,1)S(1)} %all-to-all-done.8.refs_1_, bf16[256,1024]{1,0:T(8,128)(2,1)} %get-tuple-element.212.refs_2_, ...), custom_call_target="tpu_custom_call" | custom-call | flops 5000000000 | bytes 20000000 | tf_op jit(solution)/shard_map/pallas_call | solution.py:216
  274.4 7.2 %shard_map.410 = (bf16[4,176,512]{2,1,0:T(8,128)(2,1)}, f32[8,128]{1,0:T(8,128)}) custom-call(s32[6]{0:T(128)S(1)} %stack.9.refs_0_, bf16[256,1024]{1,0:T(8,128)(2,1)S(1)} %get-tuple-element.232.refs_1_, bf16[512,256]{1,0:T(8,128)(2,1)} %get-tuple-element.233.refs_2_, bf16[512,256]{1,0:T(8,128)(2,1)S(1)} %get-tuple-element.234.refs_3_, ...), custom_call_target="tpu_custom_call" | custom-call | flops 3000000000 | bytes 12000000 | tf_op jit(solution)/shard_map/pallas_call | solution.py:216
  289.8 9.1 %collective-permute-done.5.refs_2_ = bf16[128,512]{1,0:T(8,128)(2,1)S(1)} collective-permute-done((bf16[128,512]{1,0:T(8,128)(2,1)S(1)}, bf16[128,512]{1,0:T(8,128)(2,1)S(1)}, u32[]{:S(2)}, u32[]{:S(2)}) %collective-permute-start.5) | collective-permute-done | bytes 131104 | tf_op jit(solution)/shard_map/ppermute | solution.py:1669
  307.9 5.8 %shard_map.411 = (bf16[128,512]{1,0:T(8,128)(2,1)S(1)}, bf16[64,2048]{1,0:T(8,128)(2,1)S(1)}, bf16[32,8192]{1,0:T(8,128)(2,1)S(1)}) custom-call(s32[6]{0:T(128)S(1)} %stack.9.refs_0_, f32[128,384]{1,0:T(8,128)} %get-tuple-element.228.refs_1_, f32[128,1024]{1,0:T(8,128)} %get-tuple-element.229.refs_2_, bf16[128,1280]{1,0:T(8,128)(2,1)} %get-tuple-element.174.refs_2_.refs_3_, ...), custom_call_target="tpu_custom_call" | custom-call | flops 2000000000 | bytes 8000000 | tf_op jit(solution)/shard_map/pallas_call | solution.py:216
  317.2 18.5 %all_to_all.65 = bf16[32,16,256]{2,1,0:T(8,128)(2,1)S(1)} all-to-all(bf16[32,16,256]{2,1,0:T(8,128)(2,1)S(1)} %bitcast.70), channel_id=1, replica_groups=mesh['x'=2,'core'=2,'tile'=8] {'x','core','tile'}, dimensions={0} | all-to-all | bytes 524288 | tf_op jit(solution)/shard_map/all_to_all | solution.py:2029
  335.9 17.0 %all_to_all.66 = bf16[32,16,256]{2,1,0:T(8,128)(2,1)S(1)} all-to-all(bf16[32,16,256]{2,1,0:T(8,128)(2,1)S(1)} %broadcast_in_dim.46), channel_id=1, replica_groups=mesh['x'=2,'core'=2,'tile'=8] {'x','core','tile'}, dimensions={0} | all-to-all | bytes 524288 | tf_op jit(solution)/shard_map/all_to_all | solution.py:2034
  355.6 59.5 %all-gather.3.cloned.1.call-done = bf16[13312,512]{1,0:T(8,128)(2,1)} async-done(((bf16[416,512]{1,0:T(8,128)(2,1)}), bf16[13312,512]{1,0:T(8,128)(2,1)}) %all-gather.3.cloned.1.call-update) | async-done | bytes 13631504 | tf_op jit(solution)/shard_map/all_gather | solution.py:2041
  415.1 15.2 %shard_map.417 = (f32[9,256,512]{2,1,0:T(8,128)}, f32[9,512,256]{2,1,0:T(8,128)}, f32[9,256,128]{2,1,0:T(8,128)}, f32[2048,512]{1,0:T(8,128)}, f32[512,2048]{1,0...) custom-call(bf16[32,416,512]{2,1,0:T(8,128)(2,1)} %bitcast.97), custom_call_target="tpu_custom_call" | custom-call | flops 7000000000 | bytes 28000000 | tf_op jit(solution)/shard_map/pallas_call | solution.py:1072
  (173 shorter events, 84.0 us)
Async XLA Ops:
  9.8 20.0 %all-to-all-start = ((bf16[8,24,1088]{2,1,0:T(8,128)(2,1)}), bf16[8,24,1088]{2,1,0:T(8,128)(2,1)S(1)}, u32[]{:S(2)}, u32[]{:S(2)}) async-start(bf16[8,24,1088]{2,1,0:T(8,128)(2,1)} %broadcast_in_dim.17), calls=%async_computation | async-start | bytes 884736 | tf_op jit(solution)/shard_map/all_to_all | solution.py:1633
  41.9 12.8 %all-to-all-start.1 = ((bf16[8,128,128]{2,1,0:T(8,128)(2,1)}), bf16[8,128,128]{2,1,0:T(8,128)(2,1)S(1)}, u32[]{:S(2)}, u32[]{:S(2)}) async-start(bf16[8,128,128]{2,1,0:T(8,128)(2,1)} %broadcast_in_dim.18), calls=%async_computation.1 | async-start | bytes 524288 | tf_op jit(solution)/shard_map/all_to_all | solution.py:1633
  46.1 18.5 %copy-start = (bf16[3,3,128,256]{3,2,1,0:T(8,128)(2,1)S(1)}, bf16[3,3,128,256]{3,2,1,0:T(8,128)(2,1)}, u32[]{:S(2)}) copy-start(bf16[3,3,128,256]{3,2,1,0:T(8,128)(2,1)} %refs_6_.8) | copy-start | bytes 1769476
  74.9 20.0 %copy-start.4 = (bf16[512,512]{1,0:T(8,128)(2,1)S(1)}, bf16[512,512]{1,0:T(8,128)(2,1)}, u32[]{:S(2)}) copy-start(bf16[512,512]{1,0:T(8,128)(2,1)} %refs_5_.6) | copy-start | bytes 1572868
  74.9 20.0 %copy-start.5 = (bf16[512,512]{1,0:T(8,128)(2,1)S(1)}, bf16[512,512]{1,0:T(8,128)(2,1)}, u32[]{:S(2)}) copy-start(bf16[512,512]{1,0:T(8,128)(2,1)} %refs_6_.7) | copy-start | bytes 1572868
  74.9 20.0 %copy-start.12 = (bf16[1,128,512]{2,1,0:T(8,128)(2,1)S(1)}, bf16[1,128,512]{2,1,0:T(8,128)(2,1)}, u32[]{:S(2)}) copy-start(bf16[1,128,512]{2,1,0:T(8,128)(2,1)} %param.34) | copy-start | bytes 393220
  74.9 20.0 %copy-start.14 = (bf16[128,512]{1,0:T(8,128)(2,1)S(1)}, bf16[128,512]{1,0:T(8,128)(2,1)}, u32[]{:S(2)}) copy-start(bf16[128,512]{1,0:T(8,128)(2,1)} %refs_8_.2) | copy-start | bytes 393220
  82.7 12.1 %all-to-all-start.2 = ((bf16[8,128,128]{2,1,0:T(8,128)(2,1)}), bf16[8,128,128]{2,1,0:T(8,128)(2,1)S(1)}, u32[]{:S(2)}, u32[]{:S(2)}) async-start(bf16[8,128,128]{2,1,0:T(8,128)(2,1)} %bitcast.13), calls=%async_computation.2 | async-start | bytes 524288 | tf_op jit(solution)/shard_map/all_to_all | solution.py:1717
  98.4 14.8 %all-to-all-start.3 = ((bf16[8,192,128]{2,1,0:T(8,128)(2,1)}), bf16[8,192,128]{2,1,0:T(8,128)(2,1)S(1)}, u32[]{:S(2)}, u32[]{:S(2)}) async-start(bf16[8,192,128]{2,1,0:T(8,128)(2,1)} %get-tuple-element.178), calls=%async_computation.3 | async-start | bytes 786432 | tf_op jit(solution)/shard_map/all_to_all | solution.py:1728
  102.3 25.0 %copy-start.27 = (bf16[512]{0:T(512)(128)(2,1)S(1)}, bf16[512]{0:T(512)(128)(2,1)}, u32[]{:S(2)}) copy-start(bf16[512]{0:T(512)(128)(2,1)} %param.54) | copy-start | bytes 3076
  102.3 32.3 %copy-start.3 = (bf16[512,512]{1,0:T(8,128)(2,1)S(1)}, bf16[512,512]{1,0:T(8,128)(2,1)}, u32[]{:S(2)}) copy-start(bf16[512,512]{1,0:T(8,128)(2,1)} %refs_4_.3) | copy-start | bytes 1572868
  102.3 32.3 %copy-start.13 = (bf16[1,128,512]{2,1,0:T(8,128)(2,1)S(1)}, bf16[1,128,512]{2,1,0:T(8,128)(2,1)}, u32[]{:S(2)}) copy-start(bf16[1,128,512]{2,1,0:T(8,128)(2,1)} %param.57) | copy-start | bytes 393220
  102.3 32.3 %copy-start.15 = (f32[128,512]{1,0:T(8,128)S(1)}, f32[128,512]{1,0:T(8,128)}, u32[]{:S(2)}) copy-start(f32[128,512]{1,0:T(8,128)} %get-tuple-element.180.refs_2_) | copy-start | bytes 786436
  123.6 11.0 %all-to-all-start.4 = ((bf16[8,64,128]{2,1,0:T(8,128)(2,1)}), bf16[8,64,128]{2,1,0:T(8,128)(2,1)S(1)}, u32[]{:S(2)}, u32[]{:S(2)}) async-start(bf16[8,64,128]{2,1,0:T(8,128)(2,1)} %get-tuple-element.179), calls=%async_computation.4 | async-start | bytes 262144 | tf_op jit(solution)/shard_map/all_to_all | solution.py:1732
  141.4 10.7 %all-to-all-start.5 = ((bf16[8,64,128]{2,1,0:T(8,128)(2,1)}), bf16[8,64,128]{2,1,0:T(8,128)(2,1)S(1)}, u32[]{:S(2)}, u32[]{:S(2)}) async-start(bf16[8,64,128]{2,1,0:T(8,128)(2,1)} %get-tuple-element.184), calls=%async_computation.5 | async-start | bytes 262144 | tf_op jit(solution)/shard_map/all_to_all | solution.py:1736
  144.8 160.3 %reduce-scatter.2.cloned.1.call-start = ((), (), s32[]{:S(2)}) async-start(), calls=%async_computation.14 | async-start | bytes 4866048 | tf_op jit(solution)/shard_map/reduce_scatter | solution.py:1740
  152.1 22.2 %copy-start.6 = (bf16[512,512]{1,0:T(8,128)(2,1)S(1)}, bf16[512,512]{1,0:T(8,128)(2,1)}, u32[]{:S(2)}) copy-start(bf16[512,512]{1,0:T(8,128)(2,1)} %refs_6_.7) | copy-start | bytes 1572868
  159.7 18.7 %copy-start.16 = (bf16[128,512]{1,0:T(8,128)(2,1)S(1)}, bf16[128,512]{1,0:T(8,128)(2,1)}, u32[]{:S(2)}) copy-start(bf16[128,512]{1,0:T(8,128)(2,1)} %get-tuple-element.198.refs_1_) | copy-start | bytes 393220
  159.7 18.7 %copy-start.19 = (bf16[128,128]{1,0:T(8,128)(2,1)S(1)}, bf16[128,128]{1,0:T(8,128)(2,1)}, u32[]{:S(2)}) copy-start(bf16[128,128]{1,0:T(8,128)(2,1)} %get-tuple-element.200.refs_3_) | copy-start | bytes 98308
  159.7 14.6 %all-to-all-start.6 = ((bf16[8,192,128]{2,1,0:T(8,128)(2,1)}), bf16[8,192,128]{2,1,0:T(8,128)(2,1)S(1)}, u32[]{:S(2)}, u32[]{:S(2)}) async-start(bf16[8,192,128]{2,1,0:T(8,128)(2,1)} %get-tuple-element.190), calls=%async_computation.6 | async-start | bytes 786432 | tf_op jit(solution)/shard_map/all_to_all | solution.py:1746
  180.8 12.3 %collective-permute-start.2 = (bf16[1024,512]{1,0:T(8,128)(2,1)}, bf16[1024,512]{1,0:T(8,128)(2,1)S(1)}, u32[]{:S(2)}, u32[]{:S(2)}) collective-permute-start(bf16[1024,512]{1,0:T(8,128)(2,1)} %get-tuple-element.206), channel_id=1, source_target_pairs={{0,8},{8,0},{1,9},{9,1},{2,10},{10,2},{3,11},{11,3},{4,12},{12,4},... | collective-permute-start | bytes 3145736 | tf_op jit(solution)/shard_map/ppermute | solution.py:1669
  181.5 28.1 %all-to-all-start.7 = ((bf16[8,128,128]{2,1,0:T(8,128)(2,1)}), bf16[8,128,128]{2,1,0:T(8,128)(2,1)S(1)}, u32[]{:S(2)}, u32[]{:S(2)}) async-start(bf16[8,128,128]{2,1,0:T(8,128)(2,1)} %broadcast_in_dim.21), calls=%async_computation.7 | async-start | bytes 524288 | tf_op jit(solution)/shard_map/all_to_all | solution.py:1633
  185.2 24.4 %collective-permute-start = (bf16[32,5632]{1,0:T(8,128)(2,1)}, bf16[32,5632]{1,0:T(8,128)(2,1)}, u32[]{:S(2)}, u32[]{:S(2)}) collective-permute-start(bf16[32,5632]{1,0:T(8,128)(2,1)} %get-tuple-element.195), channel_id=1, source_target_pairs={{0,1},{1,2},{2,3},{3,4},{4,5},{5,6},{6,7},{8,9},{9,10},{10,11},{11... | collective-permute-start | bytes 1081352 | tf_op jit(solution)/shard_map/ppermute | solution.py:1646
  189.8 19.7 %collective-permute-start.1 = (bf16[32,5632]{1,0:T(8,128)(2,1)}, bf16[32,5632]{1,0:T(8,128)(2,1)}, u32[]{:S(2)}, u32[]{:S(2)}) collective-permute-start(bf16[32,5632]{1,0:T(8,128)(2,1)} %get-tuple-element.197), channel_id=1, source_target_pairs={{1,0},{2,1},{3,2},{4,3},{5,4},{6,5},{7,6},{9,8},{10,9},{11,10},{12... | collective-permute-start | bytes 1081352 | tf_op jit(solution)/shard_map/ppermute | solution.py:1646
  195.6 43.8 %collective-permute-start.3 = (bf16[512,512]{1,0:T(8,128)(2,1)}, bf16[512,512]{1,0:T(8,128)(2,1)S(1)}, u32[]{:S(2)}, u32[]{:S(2)}) collective-permute-start(bf16[512,512]{1,0:T(8,128)(2,1)} %get-tuple-element.222), channel_id=1, source_target_pairs={{0,16},{16,0},{1,17},{17,1},{2,18},{18,2},{3,19},{19,3},{4,20},{20... | collective-permute-start | bytes 1572872 | tf_op jit(solution)/shard_map/ppermute | solution.py:1669
  232.1 24.7 %all-to-all-start.8 = ((bf16[8,256,128]{2,1,0:T(8,128)(2,1)}), bf16[8,256,128]{2,1,0:T(8,128)(2,1)S(1)}, u32[]{:S(2)}, u32[]{:S(2)}) async-start(bf16[8,256,128]{2,1,0:T(8,128)(2,1)} %broadcast_in_dim.22), calls=%async_computation.8 | async-start | bytes 1048576 | tf_op jit(solution)/shard_map/all_to_all | solution.py:1633
  240.1 10.3 %collective-permute-start.4 = (bf16[256,512]{1,0:T(8,128)(2,1)S(1)}, bf16[256,512]{1,0:T(8,128)(2,1)S(1)}, u32[]{:S(2)}, u32[]{:S(2)}) collective-permute-start(bf16[256,512]{1,0:T(8,128)(2,1)S(1)} %get-tuple-element.225), channel_id=1, source_target_pairs={{0,1},{1,0},{2,3},{3,2},{4,5},{5,4},{6,7},{7,6},{8,9},{9,8},{10,11... | collective-permute-start | bytes 786440 | tf_op jit(solution)/shard_map/ppermute | solution.py:1669
  256.8 29.0 %all-to-all-start.12 = ((bf16[32,48,256]{2,1,0:T(8,128)(2,1)}), bf16[32,48,256]{2,1,0:T(8,128)(2,1)S(1)}, u32[]{:S(2)}, u32[]{:S(2)}) async-start(bf16[32,48,256]{2,1,0:T(8,128)(2,1)} %bitcast.36), calls=%async_computation.13 | async-start | bytes 1572864 | tf_op jit(solution)/shard_map/all_to_all | solution.py:1999
  285.8 19.2 %all-to-all-start.11 = ((bf16[4,176,512]{2,1,0:T(8,128)(2,1)}), bf16[4,176,512]{2,1,0:T(8,128)(2,1)S(1)}, u32[]{:S(2)}, u32[]{:S(2)}) async-start(bf16[4,176,512]{2,1,0:T(8,128)(2,1)} %get-tuple-element.243), calls=%async_computation.11 | async-start | bytes 1441792 | tf_op jit(solution)/shard_map/all_to_all | solution.py:2039
  289.3 125.8 %all-gather.3.cloned.1.call-start = ((), (), s32[]{:S(2)}) async-start(), calls=%async_computation.15 | async-start | bytes 14057472 | tf_op jit(solution)/shard_map/all_gather | solution.py:2041
  289.6 9.2 %collective-permute-start.5 = (bf16[128,512]{1,0:T(8,128)(2,1)S(1)}, bf16[128,512]{1,0:T(8,128)(2,1)S(1)}, u32[]{:S(2)}, u32[]{:S(2)}) collective-permute-start(bf16[128,512]{1,0:T(8,128)(2,1)S(1)} %get-tuple-element.246), channel_id=1, source_target_pairs={{0,4},{1,5},{2,6},{3,7},{4,0},{5,1},{6,2},{7,3},{8,12},{9,13},{10,... | collective-permute-start | bytes 393224 | tf_op jit(solution)/shard_map/ppermute | solution.py:1669
  299.5 4.3 collective-permute-start.6
  (16 other events, 121.0 us)
Sparse Core Ops, SparseCore 0:
  151.7 118.9 reduce-scatter.1
  307.5 107.5 all-gather.2

commit v4 on v3

--- a/solution.py
+++ b/solution.py
@@ -21,7 +21,7 @@
 f32 = jnp.float32
 bf16 = jnp.bfloat16
 gelu_scale = math.sqrt(2.0 / math.pi)
-VMEM_CAP = 28 * 1024 * 1024
+VMEM_CAP = 40 * 1024 * 1024
 
 
 def gelu_of(x):
@@ -346,23 +346,31 @@
 
 
 def conv_taps(x, weight, width):
-    total = None
-    for i in range(3):
-        lined = row_shift(x, i - 1, width)
-        for j in range(3):
-            term = mm(weight[i, j], col_shift(lined, j - 1, width))
-            total = term if total is None else total + term
-    return total
+    lines = [row_shift(x, i - 1, width) for i in range(3)]
+    taps = [col_shift(line, j - 1, width) for line in lines for j in range(3)]
+    joined = jnp.concatenate([weight[i, j] for i in range(3) for j in range(3)], axis=1)
+    return mm(joined, jnp.concatenate(taps, axis=0))
 
 
 def conv_taps_back(x, weight, width):
-    total = None
-    for i in range(3):
-        lined = row_shift(x, i - 1, width)
-        for j in range(3):
-            term = mm_tn(weight[2 - i, 2 - j], col_shift(lined, j - 1, width))
-            total = term if total is None else total + term
-    return total
+    lines = [row_shift(x, 1 - i, width) for i in range(3)]
+    taps = [col_shift(line, 1 - j, width) for line in lines for j in range(3)]
+    joined = jnp.concatenate([weight[i, j] for i in range(3) for j in range(3)], axis=0)
+    return mm_tn(joined, jnp.concatenate(taps, axis=0))
+
+
+def conv_rows(x, weight, width, lanes):
+    moved = [col_shift(x, j - 1, width) for j in range(3)]
+    taps = [moved[j][:, i * width : i * width + lanes] for i in range(3) for j in range(3)]
+    joined = jnp.concatenate([weight[i, j] for i in range(3) for j in range(3)], axis=1)
+    return mm(joined, jnp.concatenate(taps, axis=0))
+
+
+def conv_rows_back(x, weight, width, lanes):
+    moved = [col_shift(x, j - 1, width) for j in range(3)]
+    taps = [moved[2 - j][:, (2 - i) * width : (2 - i) * width + lanes] for i in range(3) for j in range(3)]
+    joined = jnp.concatenate([weight[i, j] for i in range(3) for j in range(3)], axis=0)
+    return mm_tn(joined, jnp.concatenate(taps, axis=0))
 
 
 def laid_out(blocks):
@@ -447,12 +455,7 @@
     wide = widened(block)
     u_three[...] = wide[:, 384 : 384 + 768]
     u_three.send()
-    total = None
-    for j in range(3):
-        moved = col_shift(wide, j - 1, 128)
-        for i in range(3):
-            term = mm(w_third[i, j], moved[:, i * 128 : i * 128 + 1280])
-            total = term if total is None else total + term
+    total = conv_rows(wide, w_third, 128, 1280)
     pre_up_two[...] = total.astype(bf16)
     pre_up_two.send()
     dec = gelu_of(total) + gelu_of(pre_two[...])
@@ -674,12 +677,7 @@
     d_dec_two.send()
     low_two[...] = low[:, 128 : 5 * 128]
     low_two.send()
-    total = None
-    for j in range(3):
-        moved = col_shift(low, j - 1, 128)
-        for i in range(3):
-            term = mm_tn(w_third[2 - i, 2 - j], moved[:, i * 128 : i * 128 + 512])
-            total = term if total is None else total + term
+    total = conv_rows_back(low, w_third, 128, 512)
     pairs = jnp.concatenate(
         [total[:, :128] + total[:, 128:256], total[:, 256:384] + total[:, 384:]], axis=1
     )
@@ -1309,7 +1307,7 @@
             out_low[2 * block + n] = found[:, 128 * n : 128 * n + 128].astype(bf16)
 
 
-def run_attend(tall, ids, table, meta, meta_cols, shared):
+def run_attend(tall, ids, after, table, meta, meta_cols, shared):
     seq = meta.shape[1]
     count = shared.shape[0]
     return call(
@@ -1327,6 +1325,7 @@
         ],
         ids,
         (meta, meta_cols, shared),
+        after,
         sent=(0, 2),
         table=table,
     )
@@ -1727,7 +1726,7 @@
         )
         shared = lax.all_to_all(shared, "tile", 0, 0, tiled=True)
         prob, found_low, found_full = run_attend(
-            tall, ids, bias_table.astype(jnp.float32), meta_all, box_rows, shared
+            tall, ids, pre_up_edges, bias_table.astype(jnp.float32), meta_all, box_rows, shared
         )
         found = lax.all_to_all(found_low, "tile", 0, 0, tiled=True)
         result_low, act_low, d_pre, ffn_low, d_mixed, d_mixed_low, d_found, grad_gain_ffn = run_mixer(
@@ -1962,7 +1961,7 @@
     )
     if heads_first:
         embed_halves = halved(embed_halves, 1, box_token)
-        ordering = ()
+        ordering = embed_halves[2:]
     d_dec_one, d_dec_two, d_dec_three, low_one_up, low_two_up, up_token = run_up_back(
         ids,
         ordering,
@@ -1974,9 +1973,12 @@
         up_third,
     )
     d_dec_three_all = windowed(d_dec_three)
-    grad_up_first = run_grad_up_first(ids, (up_token,), dec_one, low_zero_up)
     if heads_first:
         embed_halves = halved(embed_halves, 2, up_token)
+        ordering = embed_halves[2:]
+    grad_up_first = run_grad_up_first(ids, (up_token, *ordering), dec_one, low_zero_up)
+    if heads_first:
+        embed_halves = halved(embed_halves, 3)
         ordering = embed_halves[2:]
     light_early, early_token = run_grad_up(
         ids, ordering, grad_up_first, dec_two, low_one_up, u_three, low_two_up
@@ -1995,7 +1997,7 @@
     )
     dp_count = lax.axis_size(PAGES)
     if heads_first:
-        embed_share = halved(halved(embed_halves, 3, bottom_token), 4)
+        embed_share = halved(embed_halves, 4, bottom_token)
         early_parts = lax.all_to_all(
             light_early.reshape(32, -1, 256), (*PAGES, "tile"), 0, 0, tiled=True
         )

time: 448 us -> 452 us (level)
  waiting for transfers between devices: 147 us -> 152 us
    all_to_all x1, waiting for transfers between devices: 11 us -> 0.01 us  [on_device(): shared = lax.all_to_all(shared, 'tile', 0, 0, tiled=True)]
    ppermute x5, waiting for transfers between devices: 15.4 us -> 21.9 us  [swapped(): return lax.ppermute(block, axis, hops)]
    all_to_all x1, waiting for transfers between devices: 0.01 us -> 5.2 us  [on_device(): parts = lax.all_to_all(heavy, PAGES, 0, 0, tiled=True)]
    all_to_all x4, waiting for transfers between devices: 18.1 us -> 23.3 us  [gathered(): return lax.all_to_all(copies, 'tile', 0, 0, tiled=True)]
    unnamed x68 -> x80, local copies, waits for them, and re-layouts: 8.58 us -> 11.9 us
  transfers between devices with their start and end apart: 20 -> 20, of which waited for: 13 -> 14; matrix products, arithmetic and copies ran while one was open for 2% -> 2% of each run, Pallas kernels for 19% -> 19%
where the time goes in v4:
time: 452 us; the launch traced here: 447 us
  Pallas kernels  158 us (35%)
  waiting for transfers between devices  152 us (34%)
  starting transfers between devices  60.5 us (13%)
  blocking collectives  35.1 us (8%)
  local copies, waits for them, and re-layouts  24.7 us (5%)
  between operations  15.2 us (3%)
    pallas_call x26, Pallas kernels, call(): pl.pallas_call(ordered, cost_estimate=price(micros), out_shape=[pltpu.HBM...  143 us
    all_gather x1, waiting for transfers between devices, on_device(): whole = lax.all_gather(share, both_axes, axis=0)  59.5 us
    all_to_all x4, waiting for transfers between devices, gathered(): return lax.all_to_all(copies, 'tile', 0, 0, tiled=True)  23.3 us
    ppermute x5, waiting for transfers between devices, swapped(): return lax.ppermute(block, axis, hops)  21.9 us
    all_to_all x4, starting transfers between devices, gathered(): return lax.all_to_all(copies, 'tile', 0, 0, tiled=True)  18.4 us
    all_to_all x1, blocking collectives, summed_share(): parts = lax.all_to_all(parts, both_axes, 0, 0, tiled=True)  18.1 us
    all_to_all x1, blocking collectives, spread_out(): return lax.all_to_all(copies, both_axes, 0, 0, tiled=True)  17 us
    pallas_call x1, Pallas kernels, run_unpack(): pl.pallas_call(unpack_body, cost_estimate=price(14), grid=(whole.shape[0]...  15.2 us
  transfers between devices with their start and end apart: 20, of which 14 were waited for; matrix products, arithmetic and copies ran while one was open for 2% of the time, Pallas kernels for 19%

profile of v4, /device:TPU:0, one launch (start us, length us, event | category | flops | bytes accessed | tf_op | source)
XLA Modules:
  0.0 446.6 jit_solution(11695870431141124587)
XLA Ops:
  9.8 7.3 %all-to-all-start = ((bf16[8,24,1088]{2,1,0:T(8,128)(2,1)}), bf16[8,24,1088]{2,1,0:T(8,128)(2,1)S(1)}, u32[]{:S(2)}, u32[]{:S(2)}) async-start(bf16[8,24,1088]{2,1,0:T(8,128)(2,1)} %broadcast_in_dim.17), calls=%async_computation | async-start | bytes 884736 | tf_op jit(solution)/shard_map/all_to_all | solution.py:1632
  20.2 9.6 %all-to-all-done.refs_1_ = bf16[8,24,1088]{2,1,0:T(8,128)(2,1)S(1)} async-done(((bf16[8,24,1088]{2,1,0:T(8,128)(2,1)}), bf16[8,24,1088]{2,1,0:T(8,128)(2,1)S(1)}, u32[]{:S(2)}, u32[]{:S(2)}) %all-to-all-start) | async-done | bytes 417824 | tf_op jit(solution)/shard_map/all_to_all | solution.py:1632
  29.9 11.3 %shard_map.391 = (bf16[32,8192]{1,0:T(8,128)(2,1)}, bf16[64,4096]{1,0:T(8,128)(2,1)}, bf16[32,2560]{1,0:T(8,128)(2,1)}, bf16[128,1280]{1,0:T(8,128)(2,1)}, bf16[...) custom-call(s32[6]{0:T(128)S(1)} %stack.9.refs_0_, ...), custom_call_target="tpu_custom_call" | custom-call | flops 5000000000 | bytes 20000000 | tf_op jit(solution)/shard_map/pallas_call | solution.py:216
  46.1 8.5 %all-to-all-done.1.refs_1_.refs_6_ = bf16[8,128,128]{2,1,0:T(8,128)(2,1)S(1)} async-done(((bf16[8,128,128]{2,1,0:T(8,128)(2,1)}), bf16[8,128,128]{2,1,0:T(8,128)(2,1)S(1)}, u32[]{:S(2)}, u32[]{:S(2)}) %all-to-all-start.1) | async-done | bytes 262176 | tf_op jit(solution)/shard_map/all_to_all | solution.py:1632
  54.6 9.5 %shard_map.392 = (bf16[256,1024]{1,0:T(8,128)(2,1)}, bf16[512,256]{1,0:T(8,128)(2,1)}, bf16[256,256]{1,0:T(8,128)(2,1)}, bf16[512,256]{1,0:T(8,128)(2,1)}, bf16[...) custom-call(s32[6]{0:T(128)S(1)} %stack.9.refs_0_, bf16[8,128,128]{2,1,0:T(8,128)(2,1)S(1)} %all-to-all-done.1.refs_1_.refs_6_, ...), custom_call_target="tpu_custom_call" | custom-call | flops 5500000256 | bytes 22000000 | tf_op jit(solution)/shard_map/pallas_call | solution.py:216
  64.2 8.4 %shard_map.393 = (bf16[128,1280]{1,0:T(8,128)(2,1)}, bf16[64,4608]{1,0:T(8,128)(2,1)}, bf16[32,8192]{1,0:T(8,128)(2,1)}, bf16[256,768]{1,0:T(8,128)(2,1)}, bf16[...) custom-call(s32[6]{0:T(128)S(1)} %stack.9.refs_0_, ...), custom_call_target="tpu_custom_call" | custom-call | flops 4499999744 | bytes 18000000 | tf_op jit(solution)/shard_map/pallas_call | solution.py:216
  72.6 7.8 %shard_map.394 = bf16[1024,128]{1,0:T(8,128)(2,1)} custom-call(s32[6]{0:T(128)S(1)} %stack.9.refs_0_, s32[1024,8]{1,0:T(8,128)S(1)} %pad_bitcast_fusion.refs_1_.refs_3_, bf16[512,512]{1,0:T(8,128)(2,1)S(1)} %get-tuple-element.179.refs_2_), custom_call_target="tpu_custom_call" | custom-call | flops 4000000000 | bytes 16000000 | tf_op jit(solution)/shard_map/pallas_call | solution.py:216
  84.1 8.5 %all-to-all-done.2.refs_1_ = bf16[8,128,128]{2,1,0:T(8,128)(2,1)S(1)} async-done(((bf16[8,128,128]{2,1,0:T(8,128)(2,1)}), bf16[8,128,128]{2,1,0:T(8,128)(2,1)S(1)}, u32[]{:S(2)}, u32[]{:S(2)}) %all-to-all-start.2) | async-done | bytes 262176 | tf_op jit(solution)/shard_map/all_to_all | solution.py:1716
  99.8 4.7 %collective-permute-start = (bf16[32,5632]{1,0:T(8,128)(2,1)S(1)}, bf16[32,5632]{1,0:T(8,128)(2,1)}, u32[]{:S(2)}, u32[]{:S(2)}) collective-permute-start(bf16[32,5632]{1,0:T(8,128)(2,1)S(1)} %get-tuple-element.181), channel_id=1, source_target_pairs={{0,1},{1,2},{2,3},{3,4},{4,5},{5,6},{6,7},{8,9},{9,10},{10,11},{11... | collective-permute-start | bytes 1081352 | tf_op jit(solution)/shard_map/ppermute | solution.py:1645
  107.1 13.6 %collective-permute-done.refs_5_.refs_3_ = bf16[32,5632]{1,0:T(8,128)(2,1)} collective-permute-done((bf16[32,5632]{1,0:T(8,128)(2,1)S(1)}, bf16[32,5632]{1,0:T(8,128)(2,1)}, u32[]{:S(2)}, u32[]{:S(2)}) %collective-permute-start) | collective-permute-done | bytes 360480 | tf_op jit(solution)/shard_map/ppermute | solution.py:1645
  120.7 10.3 %shard_map.396 = (bf16[4,1024,256]{2,1,0:T(8,128)(2,1)}, bf16[8,64,128]{2,1,0:T(8,128)(2,1)}, f32[64,1024]{1,0:T(8,128)}) custom-call(s32[6]{0:T(128)S(1)} %stack.9.refs_0_, f32[8,96]{1,0:T(8,128)S(1)} %convert_element_type.28.refs_1_, s32[8,1024]{1,0:T(8,128)S(1)} %pad.18.clone.refs_2_.refs_1_, s32[1024,8]{1,0:T(8,128)S(1)} %pad_bitcast_fusion.refs_1_.refs_3_, ...), custom_call_target="tpu_custom_call" | custom-call | flops 4499999744 | bytes 18000000 | tf_op jit(solution)/shard_map/pallas_call | solution.py:216
  130.9 6.7 %all-to-all-start.4 = ((bf16[8,64,128]{2,1,0:T(8,128)(2,1)}), bf16[8,64,128]{2,1,0:T(8,128)(2,1)S(1)}, u32[]{:S(2)}, u32[]{:S(2)}) async-start(bf16[8,64,128]{2,1,0:T(8,128)(2,1)} %get-tuple-element.183), calls=%async_computation.4 | async-start | bytes 262144 | tf_op jit(solution)/shard_map/all_to_all | solution.py:1731
  137.7 7.3 %all-to-all-done.4.refs_1_ = bf16[8,64,128]{2,1,0:T(8,128)(2,1)S(1)} async-done(((bf16[8,64,128]{2,1,0:T(8,128)(2,1)}), bf16[8,64,128]{2,1,0:T(8,128)(2,1)S(1)}, u32[]{:S(2)}, u32[]{:S(2)}) %all-to-all-start.4) | async-done | bytes 131104 | tf_op jit(solution)/shard_map/all_to_all | solution.py:1731
  145.0 6.8 %shard_map.397 = (bf16[128,512]{1,0:T(8,128)(2,1)}, bf16[128,2048]{1,0:T(8,128)(2,1)}, bf16[128,2048]{1,0:T(8,128)(2,1)}, bf16[128,512]{1,0:T(8,128)(2,1)}, f32[...) custom-call(s32[6]{0:T(128)S(1)} %stack.9.refs_0_, ...), custom_call_target="tpu_custom_call" | custom-call | flops 2500000000 | bytes 10000000 | tf_op jit(solution)/shard_map/pallas_call | solution.py:216
  155.7 5.9 %shard_map.398 = (bf16[4608,512]{1,0:T(8,128)(2,1)}, f32[8,128]{1,0:T(8,128)}) custom-call(s32[6]{0:T(128)S(1)} %stack.9.refs_0_, bf16[8,64,128]{2,1,0:T(8,128)(2,1)S(1)} %all-to-all-done.4.refs_1_, bf16[128,2048]{1,0:T(8,128)(2,1)} %get-tuple-element.189.refs_2_, bf16[128,2048]{1,0:T(8,128)(2,1)} %get-tuple-element.190.refs_3_, ...), custom_call_target="tpu_custom_call" | custom-call | flops 2000000000 | bytes 8000000 | tf_op jit(solution)/shard_map/pallas_call | solution.py:216
  162.5 7.6 %shard_map.399 = (bf16[8,192,128]{2,1,0:T(8,128)(2,1)}, f32[32,128]{1,0:T(8,128)S(1)}) custom-call(s32[6]{0:T(128)S(1)} %stack.9.refs_0_, s32[8,1024]{1,0:T(8,128)S(1)} %pad.18.clone.refs_2_.refs_1_, bf16[8,192,128]{2,1,0:T(8,128)(2,1)S(1)} %all-to-all-done.3.refs_4_.refs_2_, bf16[4,1024,256]{2,1,0:T(8,128)(2,1)} %get-tuple-element.186.refs_3_, ...), custom_call_target="tpu_custom_call" | custom-call | flops 3000000000 | bytes 12000000 | tf_op jit(solution)/shard_map/pallas_call | solution.py:216
  170.2 5.2 %all-to-all-start.6 = ((bf16[8,192,128]{2,1,0:T(8,128)(2,1)}), bf16[8,192,128]{2,1,0:T(8,128)(2,1)S(1)}, u32[]{:S(2)}, u32[]{:S(2)}) async-start(bf16[8,192,128]{2,1,0:T(8,128)(2,1)} %get-tuple-element.194), calls=%async_computation.6 | async-start | bytes 786432 | tf_op jit(solution)/shard_map/all_to_all | solution.py:1745
  175.4 9.3 %all-to-all-done.6.refs_1_ = bf16[8,192,128]{2,1,0:T(8,128)(2,1)S(1)} async-done(((bf16[8,192,128]{2,1,0:T(8,128)(2,1)}), bf16[8,192,128]{2,1,0:T(8,128)(2,1)S(1)}, u32[]{:S(2)}, u32[]{:S(2)}) %all-to-all-start.6) | async-done | bytes 393248 | tf_op jit(solution)/shard_map/all_to_all | solution.py:1745
  200.0 5.2 %all-to-all-done.7 = bf16[8,128,128]{2,1,0:T(8,128)(2,1)S(1)} async-done(((bf16[8,128,128]{2,1,0:T(8,128)(2,1)}), bf16[8,128,128]{2,1,0:T(8,128)(2,1)S(1)}, u32[]{:S(2)}, u32[]{:S(2)}) %all-to-all-start.7) | async-done | bytes 262176 | tf_op jit(solution)/shard_map/all_to_all | solution.py:1632
  205.2 11.5 %shard_map.403 = (f32[32,8192]{1,0:T(8,128)}, bf16[32,19456]{1,0:T(8,128)(2,1)S(1)}, f32[8,128]{1,0:T(8,128)}) custom-call(s32[6]{0:T(128)S(1)} %stack.9.refs_0_, s32[1024,8]{1,0:T(8,128)S(1)} %pad_bitcast_fusion.refs_1_.refs_3_, bf16[1024,128]{1,0:T(8,128)(2,1)S(1)} %bitcast.69, bf16[32,5632]{1,0:T(8,128)(2,1)} %collective-permute-done.refs_5_.refs_3_, ...), custom_call_target="tpu_custom_call" | custom-call | flops 7000000000 | bytes 28000000 | tf_op jit(solution)/shard_map/pallas_call | solution.py:216
  218.9 9.7 %shard_map.405 = (f32[64,4608]{1,0:T(8,128)}, f32[128,1024]{1,0:T(8,128)}, bf16[256,128]{1,0:T(8,128)(2,1)S(1)}, bf16[64,2048]{1,0:T(8,128)(2,1)}, bf16[128,512]{1,0:T(8,128)(2,1)}, /*index=5*/f32[8,128]{1,0:T(8,128)}) custom-call(s32[6]{0:T(128)S(1)} %stack.9.refs_0_, bf16[32,19456]{1,0:T(8,128)(2,1)S(1)} %get-tuple-element.210.refs_1_.refs_2_, ...), custom_call_target="tpu_custom_call" | custom-call | flops 4499999744 | bytes 18000000 | tf_op jit(solution)/shard_map/pallas_call | solution.py:216
  235.1 15.9 %collective-permute-done.4.refs_2_ = bf16[256,512]{1,0:T(8,128)(2,1)S(1)} collective-permute-done((bf16[256,512]{1,0:T(8,128)(2,1)S(1)}, bf16[256,512]{1,0:T(8,128)(2,1)S(1)}, u32[]{:S(2)}, u32[]{:S(2)}) %collective-permute-start.4) | collective-permute-done | bytes 262176 | tf_op jit(solution)/shard_map/ppermute | solution.py:1668
  256.4 4.8 %shard_map.407.refs_1_ = f32[3,32,192]{2,1,0:T(8,128)S(1)} custom-call(s32[6]{0:T(128)S(1)} %stack.9.refs_0_, bf16[64,2560]{1,0:T(8,128)(2,1)} %get-tuple-element.221.refs_1_, bf16[32,19456]{1,0:T(8,128)(2,1)S(1)} %copy-done.22, f32[8,128]{1,0:T(8,128)} %get-tuple-element.222.refs_3_, f32[8,128]{1,0:T(8,128)} %get-tuple-element.225.refs_4_), custom_call_target="tpu_custom_call" | custom-call | flops 2000000000 | bytes 8000000 | tf_op jit(solution)/shard_map/pallas_call | solution.py:216
  263.6 5.8 %shard_map.409 = (bf16[1536,256]{1,0:T(8,128)(2,1)}, f32[8,128]{1,0:T(8,128)}) custom-call(s32[6]{0:T(128)S(1)} %stack.9.refs_0_, f32[3,32,192]{2,1,0:T(8,128)S(1)} %shard_map.407.refs_1_, bf16[128,1024]{1,0:T(8,128)(2,1)} %get-tuple-element.226.refs_2_, bf16[64,2048]{1,0:T(8,128)(2,1)} %get-tuple-element.227.refs_3_, ...), custom_call_target="tpu_custom_call" | custom-call | flops 2000000000 | bytes 8000000 | tf_op jit(solution)/shard_map/pallas_call | solution.py:216
  272.9 12.7 %shard_map.410 = (bf16[256,1024]{1,0:T(8,128)(2,1)S(1)}, bf16[512,256]{1,0:T(8,128)(2,1)S(1)}, bf16[256,1024]{1,0:T(8,128)(2,1)S(1)}, f32[128,384]{1,0:T(8,128)}, f32[8,128]{1,0:T(8,128)}) custom-call(s32[6]{0:T(128)S(1)} %stack.9.refs_0_, bf16[8,256,128]{2,1,0:T(8,128)(2,1)S(1)} %all-to-all-done.8.refs_1_, bf16[256,1024]{1,0:T(8,128)(2,1)} %get-tuple-element.218.refs_2_, ...), custom_call_target="tpu_custom_call" | custom-call | flops 5000000000 | bytes 20000000 | tf_op jit(solution)/shard_map/pallas_call | solution.py:216
  285.5 7.4 %shard_map.411 = (bf16[4,176,512]{2,1,0:T(8,128)(2,1)}, f32[8,128]{1,0:T(8,128)}) custom-call(s32[6]{0:T(128)S(1)} %stack.9.refs_0_, bf16[256,1024]{1,0:T(8,128)(2,1)S(1)} %get-tuple-element.238.refs_1_, bf16[512,256]{1,0:T(8,128)(2,1)} %get-tuple-element.239.refs_2_, bf16[512,256]{1,0:T(8,128)(2,1)S(1)} %get-tuple-element.240.refs_3_, ...), custom_call_target="tpu_custom_call" | custom-call | flops 3000000000 | bytes 12000000 | tf_op jit(solution)/shard_map/pallas_call | solution.py:216
  304.5 5.2 %all-to-all-done.11.refs_1_ = bf16[4,176,512]{2,1,0:T(8,128)(2,1)S(1)} async-done(((bf16[4,176,512]{2,1,0:T(8,128)(2,1)}), bf16[4,176,512]{2,1,0:T(8,128)(2,1)S(1)}, u32[]{:S(2)}, u32[]{:S(2)}) %all-to-all-start.11) | async-done | bytes 720928 | tf_op jit(solution)/shard_map/all_to_all | solution.py:2041
  312.5 5.8 %shard_map.412 = (bf16[128,512]{1,0:T(8,128)(2,1)S(1)}, bf16[64,2048]{1,0:T(8,128)(2,1)S(1)}, bf16[32,8192]{1,0:T(8,128)(2,1)S(1)}) custom-call(s32[6]{0:T(128)S(1)} %stack.9.refs_0_, f32[128,384]{1,0:T(8,128)} %get-tuple-element.234.refs_1_, f32[128,1024]{1,0:T(8,128)} %get-tuple-element.235.refs_2_, bf16[128,1280]{1,0:T(8,128)(2,1)} %get-tuple-element.176.refs_2_.refs_3_, ...), custom_call_target="tpu_custom_call" | custom-call | flops 2000000000 | bytes 8000000 | tf_op jit(solution)/shard_map/pallas_call | solution.py:216
  321.8 18.1 %all_to_all.65 = bf16[32,16,256]{2,1,0:T(8,128)(2,1)S(1)} all-to-all(bf16[32,16,256]{2,1,0:T(8,128)(2,1)S(1)} %bitcast.70), channel_id=1, replica_groups=mesh['x'=2,'core'=2,'tile'=8] {'x','core','tile'}, dimensions={0} | all-to-all | bytes 524288 | tf_op jit(solution)/shard_map/all_to_all | solution.py:2031
  340.0 17.0 %all_to_all.66 = bf16[32,16,256]{2,1,0:T(8,128)(2,1)S(1)} all-to-all(bf16[32,16,256]{2,1,0:T(8,128)(2,1)S(1)} %broadcast_in_dim.46), channel_id=1, replica_groups=mesh['x'=2,'core'=2,'tile'=8] {'x','core','tile'}, dimensions={0} | all-to-all | bytes 524288 | tf_op jit(solution)/shard_map/all_to_all | solution.py:2036
  359.7 59.5 %all-gather.3.cloned.1.call-done = bf16[13312,512]{1,0:T(8,128)(2,1)} async-done(((bf16[416,512]{1,0:T(8,128)(2,1)}), bf16[13312,512]{1,0:T(8,128)(2,1)}) %all-gather.3.cloned.1.call-update) | async-done | bytes 13631504 | tf_op jit(solution)/shard_map/all_gather | solution.py:2043
  419.3 15.2 %shard_map.417 = (f32[9,256,512]{2,1,0:T(8,128)}, f32[9,512,256]{2,1,0:T(8,128)}, f32[9,256,128]{2,1,0:T(8,128)}, f32[2048,512]{1,0:T(8,128)}, f32[512,2048]{1,0...) custom-call(bf16[32,416,512]{2,1,0:T(8,128)(2,1)} %bitcast.97), custom_call_target="tpu_custom_call" | custom-call | flops 7000000000 | bytes 28000000 | tf_op jit(solution)/shard_map/pallas_call | solution.py:1070
  (185 shorter events, 89.3 us)
Async XLA Ops:
  9.8 20.0 %all-to-all-start = ((bf16[8,24,1088]{2,1,0:T(8,128)(2,1)}), bf16[8,24,1088]{2,1,0:T(8,128)(2,1)S(1)}, u32[]{:S(2)}, u32[]{:S(2)}) async-start(bf16[8,24,1088]{2,1,0:T(8,128)(2,1)} %broadcast_in_dim.17), calls=%async_computation | async-start | bytes 884736 | tf_op jit(solution)/shard_map/all_to_all | solution.py:1632
  41.9 12.8 %all-to-all-start.1 = ((bf16[8,128,128]{2,1,0:T(8,128)(2,1)}), bf16[8,128,128]{2,1,0:T(8,128)(2,1)S(1)}, u32[]{:S(2)}, u32[]{:S(2)}) async-start(bf16[8,128,128]{2,1,0:T(8,128)(2,1)} %broadcast_in_dim.18), calls=%async_computation.1 | async-start | bytes 524288 | tf_op jit(solution)/shard_map/all_to_all | solution.py:1632
  46.1 18.1 %copy-start.24 = (s32[5,8,128]{0,2,1:T(8,128)}, s32[5,8,128]{0,2,1:T(8,128)S(1)}, u32[]{:S(2)}) copy-start(s32[5,8,128]{0,2,1:T(8,128)S(1)} %copy.80) | copy-start | bytes 61444
  72.6 20.0 %copy-start.4 = (bf16[512,512]{1,0:T(8,128)(2,1)S(1)}, bf16[512,512]{1,0:T(8,128)(2,1)}, u32[]{:S(2)}) copy-start(bf16[512,512]{1,0:T(8,128)(2,1)} %refs_5_.6) | copy-start | bytes 1572868
  72.6 20.0 %copy-start.5 = (bf16[512,512]{1,0:T(8,128)(2,1)S(1)}, bf16[512,512]{1,0:T(8,128)(2,1)}, u32[]{:S(2)}) copy-start(bf16[512,512]{1,0:T(8,128)(2,1)} %refs_6_.7) | copy-start | bytes 1572868
  72.6 20.0 %copy-start.14 = (bf16[1,128,512]{2,1,0:T(8,128)(2,1)S(1)}, bf16[1,128,512]{2,1,0:T(8,128)(2,1)}, u32[]{:S(2)}) copy-start(bf16[1,128,512]{2,1,0:T(8,128)(2,1)} %param.34) | copy-start | bytes 393220
  72.6 20.0 %copy-start.16 = (bf16[128,512]{1,0:T(8,128)(2,1)S(1)}, bf16[128,512]{1,0:T(8,128)(2,1)}, u32[]{:S(2)}) copy-start(bf16[128,512]{1,0:T(8,128)(2,1)} %refs_8_.2) | copy-start | bytes 393220
  80.5 12.1 %all-to-all-start.2 = ((bf16[8,128,128]{2,1,0:T(8,128)(2,1)}), bf16[8,128,128]{2,1,0:T(8,128)(2,1)S(1)}, u32[]{:S(2)}, u32[]{:S(2)}) async-start(bf16[8,128,128]{2,1,0:T(8,128)(2,1)} %bitcast.13), calls=%async_computation.2 | async-start | bytes 524288 | tf_op jit(solution)/shard_map/all_to_all | solution.py:1716
  96.2 24.4 %all-to-all-start.3 = ((bf16[8,192,128]{2,1,0:T(8,128)(2,1)}), bf16[8,192,128]{2,1,0:T(8,128)(2,1)S(1)}, u32[]{:S(2)}, u32[]{:S(2)}) async-start(bf16[8,192,128]{2,1,0:T(8,128)(2,1)} %get-tuple-element.180), calls=%async_computation.3 | async-start | bytes 786432 | tf_op jit(solution)/shard_map/all_to_all | solution.py:1727
  99.8 20.8 %collective-permute-start = (bf16[32,5632]{1,0:T(8,128)(2,1)S(1)}, bf16[32,5632]{1,0:T(8,128)(2,1)}, u32[]{:S(2)}, u32[]{:S(2)}) collective-permute-start(bf16[32,5632]{1,0:T(8,128)(2,1)S(1)} %get-tuple-element.181), channel_id=1, source_target_pairs={{0,1},{1,2},{2,3},{3,4},{4,5},{5,6},{6,7},{8,9},{9,10},{10,11},{11... | collective-permute-start | bytes 1081352 | tf_op jit(solution)/shard_map/ppermute | solution.py:1645
  104.5 16.2 %collective-permute-start.1 = (bf16[32,5632]{1,0:T(8,128)(2,1)S(1)}, bf16[32,5632]{1,0:T(8,128)(2,1)}, u32[]{:S(2)}, u32[]{:S(2)}) collective-permute-start(bf16[32,5632]{1,0:T(8,128)(2,1)S(1)} %get-tuple-element.182), channel_id=1, source_target_pairs={{1,0},{2,1},{3,2},{4,3},{5,4},{6,5},{7,6},{9,8},{10,9},{11,10},{12... | collective-permute-start | bytes 1081352 | tf_op jit(solution)/shard_map/ppermute | solution.py:1645
  107.0 30.6 %copy-start.33 = (bf16[512]{0:T(512)(128)(2,1)S(1)}, bf16[512]{0:T(512)(128)(2,1)}, u32[]{:S(2)}) copy-start(bf16[512]{0:T(512)(128)(2,1)} %param.54) | copy-start | bytes 3076
  107.0 38.0 %copy-start.3 = (bf16[512,512]{1,0:T(8,128)(2,1)S(1)}, bf16[512,512]{1,0:T(8,128)(2,1)}, u32[]{:S(2)}) copy-start(bf16[512,512]{1,0:T(8,128)(2,1)} %refs_4_.3) | copy-start | bytes 1572868
  107.1 38.0 %copy-start.15 = (bf16[1,128,512]{2,1,0:T(8,128)(2,1)S(1)}, bf16[1,128,512]{2,1,0:T(8,128)(2,1)}, u32[]{:S(2)}) copy-start(bf16[1,128,512]{2,1,0:T(8,128)(2,1)} %param.57) | copy-start | bytes 393220
  120.7 24.4 %copy-start.19 = (f32[128,512]{1,0:T(8,128)S(1)}, f32[128,512]{1,0:T(8,128)}, u32[]{:S(2)}) copy-start(f32[128,512]{1,0:T(8,128)} %get-tuple-element.184.refs_2_) | copy-start | bytes 786436
  130.9 14.1 %all-to-all-start.4 = ((bf16[8,64,128]{2,1,0:T(8,128)(2,1)}), bf16[8,64,128]{2,1,0:T(8,128)(2,1)S(1)}, u32[]{:S(2)}, u32[]{:S(2)}) async-start(bf16[8,64,128]{2,1,0:T(8,128)(2,1)} %get-tuple-element.183), calls=%async_computation.4 | async-start | bytes 262144 | tf_op jit(solution)/shard_map/all_to_all | solution.py:1731
  151.9 10.7 %all-to-all-start.5 = ((bf16[8,64,128]{2,1,0:T(8,128)(2,1)}), bf16[8,64,128]{2,1,0:T(8,128)(2,1)S(1)}, u32[]{:S(2)}, u32[]{:S(2)}) async-start(bf16[8,64,128]{2,1,0:T(8,128)(2,1)} %get-tuple-element.188), calls=%async_computation.5 | async-start | bytes 262144 | tf_op jit(solution)/shard_map/all_to_all | solution.py:1735
  155.3 154.4 %reduce-scatter.2.cloned.1.call-start = ((), (), s32[]{:S(2)}) async-start(), calls=%async_computation.14 | async-start | bytes 4866048 | tf_op jit(solution)/shard_map/reduce_scatter | solution.py:1739
  162.5 22.1 %copy-start.6 = (bf16[512,512]{1,0:T(8,128)(2,1)S(1)}, bf16[512,512]{1,0:T(8,128)(2,1)}, u32[]{:S(2)}) copy-start(bf16[512,512]{1,0:T(8,128)(2,1)} %refs_6_.7) | copy-start | bytes 1572868
  170.1 18.6 %copy-start.20 = (bf16[128,512]{1,0:T(8,128)(2,1)S(1)}, bf16[128,512]{1,0:T(8,128)(2,1)}, u32[]{:S(2)}) copy-start(bf16[128,512]{1,0:T(8,128)(2,1)} %get-tuple-element.200.refs_1_) | copy-start | bytes 393220
  170.1 18.6 %copy-start.23 = (bf16[128,128]{1,0:T(8,128)(2,1)S(1)}, bf16[128,128]{1,0:T(8,128)(2,1)}, u32[]{:S(2)}) copy-start(bf16[128,128]{1,0:T(8,128)(2,1)} %get-tuple-element.202.refs_3_) | copy-start | bytes 98308
  170.2 14.5 %all-to-all-start.6 = ((bf16[8,192,128]{2,1,0:T(8,128)(2,1)}), bf16[8,192,128]{2,1,0:T(8,128)(2,1)S(1)}, u32[]{:S(2)}, u32[]{:S(2)}) async-start(bf16[8,192,128]{2,1,0:T(8,128)(2,1)} %get-tuple-element.194), calls=%async_computation.6 | async-start | bytes 786432 | tf_op jit(solution)/shard_map/all_to_all | solution.py:1745
  191.2 4.8 %collective-permute-start.2 = (bf16[1024,512]{1,0:T(8,128)(2,1)}, bf16[1024,512]{1,0:T(8,128)(2,1)S(1)}, u32[]{:S(2)}, u32[]{:S(2)}) collective-permute-start(bf16[1024,512]{1,0:T(8,128)(2,1)} %get-tuple-element.208), channel_id=1, source_target_pairs={{0,8},{8,0},{1,9},{9,1},{2,10},{10,2},{3,11},{11,3},{4,12},{12,4},... | collective-permute-start | bytes 3145736 | tf_op jit(solution)/shard_map/ppermute | solution.py:1668
  191.9 13.3 %all-to-all-start.7 = ((bf16[8,128,128]{2,1,0:T(8,128)(2,1)}), bf16[8,128,128]{2,1,0:T(8,128)(2,1)S(1)}, u32[]{:S(2)}, u32[]{:S(2)}) async-start(bf16[8,128,128]{2,1,0:T(8,128)(2,1)} %broadcast_in_dim.21), calls=%async_computation.7 | async-start | bytes 524288 | tf_op jit(solution)/shard_map/all_to_all | solution.py:1632
  198.5 18.2 %collective-permute-start.3 = (bf16[512,512]{1,0:T(8,128)(2,1)}, bf16[512,512]{1,0:T(8,128)(2,1)S(1)}, u32[]{:S(2)}, u32[]{:S(2)}) collective-permute-start(bf16[512,512]{1,0:T(8,128)(2,1)} %get-tuple-element.214), channel_id=1, source_target_pairs={{0,16},{16,0},{1,17},{17,1},{2,18},{18,2},{3,19},{19,3},{4,20},{20... | collective-permute-start | bytes 1572872 | tf_op jit(solution)/shard_map/ppermute | solution.py:1668
  229.5 39.9 %all-to-all-start.8 = ((bf16[8,256,128]{2,1,0:T(8,128)(2,1)}), bf16[8,256,128]{2,1,0:T(8,128)(2,1)S(1)}, u32[]{:S(2)}, u32[]{:S(2)}) async-start(bf16[8,256,128]{2,1,0:T(8,128)(2,1)} %broadcast_in_dim.22), calls=%async_computation.8 | async-start | bytes 1048576 | tf_op jit(solution)/shard_map/all_to_all | solution.py:1632
  233.1 18.0 %collective-permute-start.4 = (bf16[256,512]{1,0:T(8,128)(2,1)S(1)}, bf16[256,512]{1,0:T(8,128)(2,1)S(1)}, u32[]{:S(2)}, u32[]{:S(2)}) collective-permute-start(bf16[256,512]{1,0:T(8,128)(2,1)S(1)} %copy-done.12), channel_id=1, source_target_pairs={{0,1},{1,0},{2,3},{3,2},{4,5},{5,4},{6,7},{7,6},{8,9},{9,8},{10,11... | collective-permute-start | bytes 786440 | tf_op jit(solution)/shard_map/ppermute | solution.py:1668
  252.6 10.3 %collective-permute-start.5 = (bf16[128,512]{1,0:T(8,128)(2,1)S(1)}, bf16[128,512]{1,0:T(8,128)(2,1)S(1)}, u32[]{:S(2)}, u32[]{:S(2)}) collective-permute-start(bf16[128,512]{1,0:T(8,128)(2,1)S(1)} %get-tuple-element.231), channel_id=1, source_target_pairs={{0,4},{1,5},{2,6},{3,7},{4,0},{5,1},{6,2},{7,3},{8,12},{9,13},{10,... | collective-permute-start | bytes 393224 | tf_op jit(solution)/shard_map/ppermute | solution.py:1668
  269.3 25.9 %all-to-all-start.12 = ((bf16[32,48,256]{2,1,0:T(8,128)(2,1)}), bf16[32,48,256]{2,1,0:T(8,128)(2,1)S(1)}, u32[]{:S(2)}, u32[]{:S(2)}) async-start(bf16[32,48,256]{2,1,0:T(8,128)(2,1)} %bitcast.36), calls=%async_computation.13 | async-start | bytes 1572864 | tf_op jit(solution)/shard_map/all_to_all | solution.py:2001
  295.3 14.4 %all-to-all-start.11 = ((bf16[4,176,512]{2,1,0:T(8,128)(2,1)}), bf16[4,176,512]{2,1,0:T(8,128)(2,1)S(1)}, u32[]{:S(2)}, u32[]{:S(2)}) async-start(bf16[4,176,512]{2,1,0:T(8,128)(2,1)} %get-tuple-element.249), calls=%async_computation.11 | async-start | bytes 1441792 | tf_op jit(solution)/shard_map/all_to_all | solution.py:2041
  298.8 120.5 %all-gather.3.cloned.1.call-start = ((), (), s32[]{:S(2)}) async-start(), calls=%async_computation.15 | async-start | bytes 14057472 | tf_op jit(solution)/shard_map/all_gather | solution.py:2043
  298.8 4.4 collective-permute-start.6
  (22 other events, 170.1 us)
Sparse Core Ops, SparseCore 0:
  162.1 117.3 reduce-scatter.1
  312.1 107.0 all-gather.2

commit v5 on v4

--- a/solution.py
+++ b/solution.py
@@ -353,10 +353,13 @@
 
 
 def conv_taps_back(x, weight, width):
-    lines = [row_shift(x, 1 - i, width) for i in range(3)]
-    taps = [col_shift(line, 1 - j, width) for line in lines for j in range(3)]
-    joined = jnp.concatenate([weight[i, j] for i in range(3) for j in range(3)], axis=0)
-    return mm_tn(joined, jnp.concatenate(taps, axis=0))
+    total = None
+    for i in range(3):
+        lined = row_shift(x, i - 1, width)
+        for j in range(3):
+            term = mm_tn(weight[2 - i, 2 - j], col_shift(lined, j - 1, width))
+            total = term if total is None else total + term
+    return total
 
 
 def conv_rows(x, weight, width, lanes):
@@ -571,7 +574,7 @@
     )[0]
 
 
-def unpool_body(step, ids, boxes, d_pooled, pre_before, pre_up, pre_behind, d_features, d_low, token, total):
+def unpool_body(step, ids, boxes, d_pooled, pre_up, d_features, d_low, d_before, d_behind, token, total):
     tile = ids[0]
     lines = 38
     x_ids = lane_ids((1, 512))
@@ -605,33 +608,42 @@
     for y in range(lines):
         line = total[32 * y : 32 * y + 32, :]
         if y < 11:
-            pre = pre_before[:, 512 * y : 512 * y + 512]
+            d_before[:, 512 * y : 512 * y + 512] = line.astype(bf16)
         elif y < 27:
             own = slice(512 * (y - 11), 512 * (y - 10))
             d_features[:, own] = line
-            pre = pre_up[:, own]
+            d_low[:, own] = (line * gelu_slope(pre_up[:, own])).astype(bf16)
         else:
-            pre = pre_behind[:, 512 * (y - 27) : 512 * (y - 26)]
-        d_low[:, 512 * y : 512 * y + 512] = (line * gelu_slope(pre)).astype(bf16)
-
-
-def run_unpool(ids, after, boxes, d_pooled, pre_before, pre_up, pre_behind, step):
+            d_behind[:, 512 * (y - 27) : 512 * (y - 26)] = line.astype(bf16)
+
+
+def run_unpool(ids, after, boxes, d_pooled, pre_up, step):
     return call(
         14,
         functools.partial(unpool_body, step),
-        [((32, 8192), f32), ((32, 38 * 512), bf16), TOKEN],
+        [
+            ((32, 8192), f32),
+            ((32, 8192), bf16),
+            ((32, 11 * 512), bf16),
+            ((32, 11 * 512), bf16),
+            TOKEN,
+        ],
         [((38 * 32, 512), f32)],
         ids,
-        (boxes, d_pooled, pre_before, pre_up, pre_behind),
+        (boxes, d_pooled, pre_up),
         after,
-        late=(2, 3, 4),
+        late=(2,),
         sent=(0,),
     )
 
 
-def up_back_body(ids, d_low, pre_up_one, pre_up_two, wd_first, wd_second, w_third, d_dec_one, d_dec_two, d_dec_three, low_one, low_two, token, stack_zero, wide_low):
+def up_back_body(ids, d_before, d_low, d_behind, pre_before, pre_behind, pre_up_one, pre_up_two, wd_first, wd_second, w_third, d_dec_one, d_dec_two, d_dec_three, low_one, low_two, token, stack_zero, wide_low):
     tile, high = ids[0], ids[1]
-    stack_zero[...] = stack_cols(d_low[...], 512)
+    reach = 11 * 512
+    stack_zero[:, reach : reach + 8192] = stack_cols(d_low[...], 512)
+    for first, grad, pre in ((0, d_before, pre_before), (reach + 8192, d_behind, pre_behind)):
+        low = (grad[...].astype(f32) * gelu_slope(pre[...])).astype(bf16)
+        stack_zero[:, first : first + reach] = stack_cols(low, 512)
     halve = halving(512, 1.0)
     pre_up_one.ready()
 
@@ -684,7 +696,7 @@
     d_dec_three[...] = mm_fine(pairs, pair_halving(1.0)).astype(bf16)
 
 
-def run_up_back(ids, after, d_low, pre_up_one, pre_up_two, wd_first, wd_second, w_third):
+def run_up_back(ids, after, d_before, d_low, d_behind, pre_before, pre_behind, pre_up_one, pre_up_two, wd_first, wd_second, w_third):
     return call(
         9,
         up_back_body,
@@ -698,9 +710,20 @@
         ],
         [((96, 38 * 512), bf16), ((64, 18 * 256), bf16)],
         ids,
-        (d_low, pre_up_one, pre_up_two, wd_first, wd_second, w_third),
+        (
+            d_before,
+            d_low,
+            d_behind,
+            pre_before,
+            pre_behind,
+            pre_up_one,
+            pre_up_two,
+            wd_first,
+            wd_second,
+            w_third,
+        ),
         after,
-        late=(1, 2),
+        late=(3, 4, 5, 6),
         sent=(0, 1, 3, 4),
     )
 
@@ -822,7 +845,7 @@
     spread_rows(dec_one[...], wide_one, 256)
     stack_one[...] = stack_cols(wide_one[...], 512)
     for i in range(3):
-        grad[i] = mm_nt(d_low[:, 11 * 512 : 27 * 512], stack_one[:, (1 + i) * 512 : (17 + i) * 512])
+        grad[i] = mm_nt(d_low[...], stack_one[:, (1 + i) * 512 : (17 + i) * 512])
 
 
 def run_grad_up_first(ids, after, dec_one, d_low):
@@ -1726,7 +1749,7 @@
         )
         shared = lax.all_to_all(shared, "tile", 0, 0, tiled=True)
         prob, found_low, found_full = run_attend(
-            tall, ids, pre_up_edges, bias_table.astype(jnp.float32), meta_all, box_rows, shared
+            tall, ids, (), bias_table.astype(jnp.float32), meta_all, box_rows, shared
         )
         found = lax.all_to_all(found_low, "tile", 0, 0, tiled=True)
         result_low, act_low, d_pre, ffn_low, d_mixed, d_mixed_low, d_found, grad_gain_ffn = run_mixer(
@@ -1949,23 +1972,19 @@
             axis=0,
         ).astype(jnp.bfloat16)
     d_pooled_all = gathered(d_pooled).reshape(seq_all, -1)
-    d_features, low_zero_up, box_token = run_unpool(
-        ids,
-        ordering,
-        box_rows,
-        d_pooled_all,
-        pre_up_edges[0],
-        pre_up_zero,
-        pre_up_edges[1],
-        256,
+    d_features, low_zero_up, d_before, d_behind, box_token = run_unpool(
+        ids, ordering, box_rows, d_pooled_all, pre_up_zero, 256
     )
     if heads_first:
         embed_halves = halved(embed_halves, 1, box_token)
-        ordering = embed_halves[2:]
+        ordering = ()
     d_dec_one, d_dec_two, d_dec_three, low_one_up, low_two_up, up_token = run_up_back(
         ids,
         ordering,
+        d_before,
         low_zero_up,
+        d_behind,
+        *pre_up_edges,
         pre_up_one,
         pre_up_two,
         lined_back(up_first),
@@ -1973,12 +1992,9 @@
         up_third,
     )
     d_dec_three_all = windowed(d_dec_three)
+    grad_up_first = run_grad_up_first(ids, (up_token,), dec_one, low_zero_up)
     if heads_first:
         embed_halves = halved(embed_halves, 2, up_token)
-        ordering = embed_halves[2:]
-    grad_up_first = run_grad_up_first(ids, (up_token, *ordering), dec_one, low_zero_up)
-    if heads_first:
-        embed_halves = halved(embed_halves, 3)
         ordering = embed_halves[2:]
     light_early, early_token = run_grad_up(
         ids, ordering, grad_up_first, dec_two, low_one_up, u_three, low_two_up
@@ -1997,7 +2013,7 @@
     )
     dp_count = lax.axis_size(PAGES)
     if heads_first:
-        embed_share = halved(embed_halves, 4, bottom_token)
+        embed_share = halved(halved(embed_halves, 3, bottom_token), 4)
         early_parts = lax.all_to_all(
             light_early.reshape(32, -1, 256), (*PAGES, "tile"), 0, 0, tiled=True
         )

time: 452 us -> 444 us (0.982)
    all_to_all x1, waiting for transfers between devices: 0.01 us -> 11 us  [on_device(): shared = lax.all_to_all(shared, 'tile', 0, 0, tiled=True)]
    ppermute x2, waiting for transfers between devices: 13.6 us -> 3.67 us  [from_side(): return lax.ppermute(block, 'tile', hops)]
    all_to_all x4, waiting for transfers between devices: 23.3 us -> 17.2 us  [gathered(): return lax.all_to_all(copies, 'tile', 0, 0, tiled=True)]
    all_to_all x1, waiting for transfers between devices: 5.2 us -> 0.01 us  [on_device(): parts = lax.all_to_all(heavy, PAGES, 0, 0, tiled=True)]
    unnamed x80 -> x70, local copies, waits for them, and re-layouts: 11.9 us -> 8 us
  transfers between devices with their start and end apart: 20 -> 20, of which waited for: 14 -> 13; matrix products, arithmetic and copies ran while one was open for 2% -> 3% of each run, Pallas kernels for 19% -> 19%
where the time goes in v5:
time: 444 us; the launch traced here: 439 us
  Pallas kernels  157 us (35%)
  waiting for transfers between devices  148 us (33%)
  starting transfers between devices  59.1 us (13%)
  blocking collectives  35.4 us (8%)
  local copies, waits for them, and re-layouts  23.3 us (5%)
  between operations  15.2 us (3%)
    pallas_call x26, Pallas kernels, call(): pl.pallas_call(ordered, cost_estimate=price(micros), out_shape=[pltpu.HBM...  142 us
    all_gather x1, waiting for transfers between devices, on_device(): whole = lax.all_gather(share, both_axes, axis=0)  59.5 us
    ppermute x5, waiting for transfers between devices, swapped(): return lax.ppermute(block, axis, hops)  23.7 us
    all_to_all x4, starting transfers between devices, gathered(): return lax.all_to_all(copies, 'tile', 0, 0, tiled=True)  21 us
    all_to_all x1, blocking collectives, summed_share(): parts = lax.all_to_all(parts, both_axes, 0, 0, tiled=True)  18.4 us
    all_to_all x4, waiting for transfers between devices, gathered(): return lax.all_to_all(copies, 'tile', 0, 0, tiled=True)  17.2 us
    all_to_all x1, blocking collectives, spread_out(): return lax.all_to_all(copies, both_axes, 0, 0, tiled=True)  17 us
    pallas_call x1, Pallas kernels, run_unpack(): pl.pallas_call(unpack_body, cost_estimate=price(14), grid=(whole.shape[0]...  15.2 us
  transfers between devices with their start and end apart: 20, of which 13 were waited for; matrix products, arithmetic and copies ran while one was open for 3% of the time, Pallas kernels for 19%

profile of v5, /device:TPU:0, one launch (start us, length us, event | category | flops | bytes accessed | tf_op | source)
XLA Modules:
  0.0 439.1 jit_solution(14573615071349517066)
XLA Ops:
  9.8 7.3 %all-to-all-start = ((bf16[8,24,1088]{2,1,0:T(8,128)(2,1)}), bf16[8,24,1088]{2,1,0:T(8,128)(2,1)S(1)}, u32[]{:S(2)}, u32[]{:S(2)}) async-start(bf16[8,24,1088]{2,1,0:T(8,128)(2,1)} %broadcast_in_dim.17), calls=%async_computation | async-start | bytes 884736 | tf_op jit(solution)/shard_map/all_to_all | solution.py:1655
  21.1 8.7 %all-to-all-done.refs_1_ = bf16[8,24,1088]{2,1,0:T(8,128)(2,1)S(1)} async-done(((bf16[8,24,1088]{2,1,0:T(8,128)(2,1)}), bf16[8,24,1088]{2,1,0:T(8,128)(2,1)S(1)}, u32[]{:S(2)}, u32[]{:S(2)}) %all-to-all-start) | async-done | bytes 417824 | tf_op jit(solution)/shard_map/all_to_all | solution.py:1655
  29.8 11.3 %shard_map.391 = (bf16[32,8192]{1,0:T(8,128)(2,1)}, bf16[64,4096]{1,0:T(8,128)(2,1)}, bf16[32,2560]{1,0:T(8,128)(2,1)}, bf16[128,1280]{1,0:T(8,128)(2,1)}, bf16[...) custom-call(s32[6]{0:T(128)S(1)} %stack.9.refs_0_, ...), custom_call_target="tpu_custom_call" | custom-call | flops 5000000000 | bytes 20000000 | tf_op jit(solution)/shard_map/pallas_call | solution.py:216
  46.1 8.5 %all-to-all-done.1.refs_1_.refs_6_ = bf16[8,128,128]{2,1,0:T(8,128)(2,1)S(1)} async-done(((bf16[8,128,128]{2,1,0:T(8,128)(2,1)}), bf16[8,128,128]{2,1,0:T(8,128)(2,1)S(1)}, u32[]{:S(2)}, u32[]{:S(2)}) %all-to-all-start.1) | async-done | bytes 262176 | tf_op jit(solution)/shard_map/all_to_all | solution.py:1655
  54.6 9.5 %shard_map.392 = (bf16[256,1024]{1,0:T(8,128)(2,1)}, bf16[512,256]{1,0:T(8,128)(2,1)}, bf16[256,256]{1,0:T(8,128)(2,1)}, bf16[512,256]{1,0:T(8,128)(2,1)}, bf16[...) custom-call(s32[6]{0:T(128)S(1)} %stack.9.refs_0_, bf16[8,128,128]{2,1,0:T(8,128)(2,1)S(1)} %all-to-all-done.1.refs_1_.refs_6_, ...), custom_call_target="tpu_custom_call" | custom-call | flops 5500000256 | bytes 22000000 | tf_op jit(solution)/shard_map/pallas_call | solution.py:216
  64.2 8.4 %shard_map.393 = (bf16[128,1280]{1,0:T(8,128)(2,1)}, bf16[64,4608]{1,0:T(8,128)(2,1)}, bf16[32,8192]{1,0:T(8,128)(2,1)}, bf16[256,768]{1,0:T(8,128)(2,1)}, bf16[...) custom-call(s32[6]{0:T(128)S(1)} %stack.9.refs_0_, ...), custom_call_target="tpu_custom_call" | custom-call | flops 4499999744 | bytes 18000000 | tf_op jit(solution)/shard_map/pallas_call | solution.py:216
  73.3 7.8 %shard_map.394 = bf16[1024,128]{1,0:T(8,128)(2,1)} custom-call(s32[6]{0:T(128)S(1)} %stack.9.refs_0_, s32[1024,8]{1,0:T(8,128)S(1)} %pad_bitcast_fusion.refs_1_.refs_3_, bf16[512,512]{1,0:T(8,128)(2,1)S(1)} %get-tuple-element.179.refs_2_), custom_call_target="tpu_custom_call" | custom-call | flops 4000000000 | bytes 16000000 | tf_op jit(solution)/shard_map/pallas_call | solution.py:216
  84.7 8.5 %all-to-all-done.2.refs_1_ = bf16[8,128,128]{2,1,0:T(8,128)(2,1)S(1)} async-done(((bf16[8,128,128]{2,1,0:T(8,128)(2,1)}), bf16[8,128,128]{2,1,0:T(8,128)(2,1)S(1)}, u32[]{:S(2)}, u32[]{:S(2)}) %all-to-all-start.2) | async-done | bytes 262176 | tf_op jit(solution)/shard_map/all_to_all | solution.py:1739
  100.7 11.0 %all-to-all-done.3.refs_4_.refs_2_ = bf16[8,192,128]{2,1,0:T(8,128)(2,1)S(1)} async-done(((bf16[8,192,128]{2,1,0:T(8,128)(2,1)}), bf16[8,192,128]{2,1,0:T(8,128)(2,1)S(1)}, u32[]{:S(2)}, u32[]{:S(2)}) %all-to-all-start.3) | async-done | bytes 393248 | tf_op jit(solution)/shard_map/all_to_all | solution.py:1750
  111.7 10.3 %shard_map.396 = (bf16[4,1024,256]{2,1,0:T(8,128)(2,1)}, bf16[8,64,128]{2,1,0:T(8,128)(2,1)}, f32[64,1024]{1,0:T(8,128)}) custom-call(s32[6]{0:T(128)S(1)} %stack.9.refs_0_, f32[8,96]{1,0:T(8,128)S(1)} %convert_element_type.28.refs_1_, s32[8,1024]{1,0:T(8,128)S(1)} %pad.18.clone.refs_2_.refs_1_, s32[1024,8]{1,0:T(8,128)S(1)} %pad_bitcast_fusion.refs_1_.refs_3_, ...), custom_call_target="tpu_custom_call" | custom-call | flops 4499999744 | bytes 18000000 | tf_op jit(solution)/shard_map/pallas_call | solution.py:216
  125.6 7.3 %all-to-all-done.4.refs_1_ = bf16[8,64,128]{2,1,0:T(8,128)(2,1)S(1)} async-done(((bf16[8,64,128]{2,1,0:T(8,128)(2,1)}), bf16[8,64,128]{2,1,0:T(8,128)(2,1)S(1)}, u32[]{:S(2)}, u32[]{:S(2)}) %all-to-all-start.4) | async-done | bytes 131104 | tf_op jit(solution)/shard_map/all_to_all | solution.py:1754
  133.0 6.8 %shard_map.397 = (bf16[128,512]{1,0:T(8,128)(2,1)}, bf16[128,2048]{1,0:T(8,128)(2,1)}, bf16[128,2048]{1,0:T(8,128)(2,1)}, bf16[128,512]{1,0:T(8,128)(2,1)}, f32[...) custom-call(s32[6]{0:T(128)S(1)} %stack.9.refs_0_, ...), custom_call_target="tpu_custom_call" | custom-call | flops 2500000000 | bytes 10000000 | tf_op jit(solution)/shard_map/pallas_call | solution.py:216
  143.6 5.9 %shard_map.398 = (bf16[4608,512]{1,0:T(8,128)(2,1)}, f32[8,128]{1,0:T(8,128)}) custom-call(s32[6]{0:T(128)S(1)} %stack.9.refs_0_, bf16[8,64,128]{2,1,0:T(8,128)(2,1)S(1)} %all-to-all-done.4.refs_1_, bf16[128,2048]{1,0:T(8,128)(2,1)} %get-tuple-element.187.refs_2_, bf16[128,2048]{1,0:T(8,128)(2,1)} %get-tuple-element.188.refs_3_, ...), custom_call_target="tpu_custom_call" | custom-call | flops 2000000000 | bytes 8000000 | tf_op jit(solution)/shard_map/pallas_call | solution.py:216
  150.5 7.6 %shard_map.399 = (bf16[8,192,128]{2,1,0:T(8,128)(2,1)}, f32[32,128]{1,0:T(8,128)S(1)}) custom-call(s32[6]{0:T(128)S(1)} %stack.9.refs_0_, s32[8,1024]{1,0:T(8,128)S(1)} %pad.18.clone.refs_2_.refs_1_, bf16[8,192,128]{2,1,0:T(8,128)(2,1)S(1)} %all-to-all-done.3.refs_4_.refs_2_, bf16[4,1024,256]{2,1,0:T(8,128)(2,1)} %get-tuple-element.184.refs_3_, ...), custom_call_target="tpu_custom_call" | custom-call | flops 3000000000 | bytes 12000000 | tf_op jit(solution)/shard_map/pallas_call | solution.py:216
  158.1 5.2 %all-to-all-start.6 = ((bf16[8,192,128]{2,1,0:T(8,128)(2,1)}), bf16[8,192,128]{2,1,0:T(8,128)(2,1)S(1)}, u32[]{:S(2)}, u32[]{:S(2)}) async-start(bf16[8,192,128]{2,1,0:T(8,128)(2,1)} %get-tuple-element.192), calls=%async_computation.6 | async-start | bytes 786432 | tf_op jit(solution)/shard_map/all_to_all | solution.py:1768
  163.3 9.4 %all-to-all-done.6.refs_1_ = bf16[8,192,128]{2,1,0:T(8,128)(2,1)S(1)} async-done(((bf16[8,192,128]{2,1,0:T(8,128)(2,1)}), bf16[8,192,128]{2,1,0:T(8,128)(2,1)S(1)}, u32[]{:S(2)}, u32[]{:S(2)}) %all-to-all-start.6) | async-done | bytes 393248 | tf_op jit(solution)/shard_map/all_to_all | solution.py:1768
  195.5 11.0 %shard_map.403 = (f32[32,8192]{1,0:T(8,128)}, bf16[32,8192]{1,0:T(8,128)(2,1)S(1)}, bf16[32,5632]{1,0:T(8,128)(2,1)S(1)}, bf16[32,5632]{1,0:T(8,128)(2,1)S(1)}, f32[8,128]{1,0:T(8,128)}) custom-call(s32[6]{0:T(128)S(1)} %stack.9.refs_0_, s32[1024,8]{1,0:T(8,128)S(1)} %pad_bitcast_fusion.refs_1_.refs_3_, bf16[1024,128]{1,0:T(8,128)(2,1)S(1)} %bitcast.69, ...), custom_call_target="tpu_custom_call" | custom-call | flops 7000000000 | bytes 28000000 | tf_op jit(solution)/shard_map/pallas_call | solution.py:216
  210.2 11.0 %shard_map.404 = (f32[64,4608]{1,0:T(8,128)}, f32[128,1024]{1,0:T(8,128)}, bf16[256,128]{1,0:T(8,128)(2,1)S(1)}, bf16[64,2048]{1,0:T(8,128)(2,1)}, bf16[128,512]{1,0:T(8,128)(2,1)}, /*index=5*/f32[8,128]{1,0:T(8,128)}) custom-call(s32[6]{0:T(128)S(1)} %stack.9.refs_0_, bf16[32,5632]{1,0:T(8,128)(2,1)S(1)} %get-tuple-element.208.refs_1_, ...), custom_call_target="tpu_custom_call" | custom-call | flops 4499999744 | bytes 18000000 | tf_op jit(solution)/shard_map/pallas_call | solution.py:216
  222.1 6.2 %all-to-all-start.8 = ((bf16[8,256,128]{2,1,0:T(8,128)(2,1)}), bf16[8,256,128]{2,1,0:T(8,128)(2,1)S(1)}, u32[]{:S(2)}, u32[]{:S(2)}) async-start(bf16[8,256,128]{2,1,0:T(8,128)(2,1)} %broadcast_in_dim.22), calls=%async_computation.8 | async-start | bytes 1048576 | tf_op jit(solution)/shard_map/all_to_all | solution.py:1655
  231.1 4.9 %shard_map.405.refs_1_ = f32[3,32,192]{2,1,0:T(8,128)S(1)} custom-call(s32[6]{0:T(128)S(1)} %stack.9.refs_0_, bf16[64,2560]{1,0:T(8,128)(2,1)} %get-tuple-element.219.refs_1_, bf16[32,8192]{1,0:T(8,128)(2,1)S(1)} %copy-done.21, f32[8,128]{1,0:T(8,128)} %get-tuple-element.220.refs_3_), custom_call_target="tpu_custom_call" | custom-call | flops 2000000000 | bytes 8000000 | tf_op jit(solution)/shard_map/pallas_call | solution.py:216
  236.0 10.1 %collective-permute-done.4.refs_2_ = bf16[256,512]{1,0:T(8,128)(2,1)S(1)} collective-permute-done((bf16[256,512]{1,0:T(8,128)(2,1)S(1)}, bf16[256,512]{1,0:T(8,128)(2,1)S(1)}, u32[]{:S(2)}, u32[]{:S(2)}) %collective-permute-start.4) | collective-permute-done | bytes 262176 | tf_op jit(solution)/shard_map/ppermute | solution.py:1691
  246.7 5.8 %shard_map.408 = (bf16[1536,256]{1,0:T(8,128)(2,1)}, f32[8,128]{1,0:T(8,128)}) custom-call(s32[6]{0:T(128)S(1)} %stack.9.refs_0_, f32[3,32,192]{2,1,0:T(8,128)S(1)} %shard_map.405.refs_1_, bf16[128,1024]{1,0:T(8,128)(2,1)} %get-tuple-element.221.refs_2_, bf16[64,2048]{1,0:T(8,128)(2,1)} %get-tuple-element.222.refs_3_, ...), custom_call_target="tpu_custom_call" | custom-call | flops 2000000000 | bytes 8000000 | tf_op jit(solution)/shard_map/pallas_call | solution.py:216
  252.5 4.8 %all-to-all-start.12 = ((bf16[32,48,256]{2,1,0:T(8,128)(2,1)}), bf16[32,48,256]{2,1,0:T(8,128)(2,1)S(1)}, u32[]{:S(2)}, u32[]{:S(2)}) async-start(bf16[32,48,256]{2,1,0:T(8,128)(2,1)} %bitcast.36), calls=%async_computation.13 | async-start | bytes 1572864 | tf_op jit(solution)/shard_map/all_to_all | solution.py:2017
  257.3 11.4 %shard_map.409 = (bf16[256,1024]{1,0:T(8,128)(2,1)S(1)}, bf16[512,256]{1,0:T(8,128)(2,1)S(1)}, bf16[256,1024]{1,0:T(8,128)(2,1)S(1)}, f32[128,384]{1,0:T(8,128)}, f32[8,128]{1,0:T(8,128)}) custom-call(s32[6]{0:T(128)S(1)} %stack.9.refs_0_, bf16[8,256,128]{2,1,0:T(8,128)(2,1)S(1)} %all-to-all-done.8.refs_1_, bf16[256,1024]{1,0:T(8,128)(2,1)} %get-tuple-element.216.refs_2_, ...), custom_call_target="tpu_custom_call" | custom-call | flops 5000000000 | bytes 20000000 | tf_op jit(solution)/shard_map/pallas_call | solution.py:216
  268.7 7.2 %shard_map.410 = (bf16[4,176,512]{2,1,0:T(8,128)(2,1)}, f32[8,128]{1,0:T(8,128)}) custom-call(s32[6]{0:T(128)S(1)} %stack.9.refs_0_, bf16[256,1024]{1,0:T(8,128)(2,1)S(1)} %get-tuple-element.236.refs_1_, bf16[512,256]{1,0:T(8,128)(2,1)} %get-tuple-element.237.refs_2_, bf16[512,256]{1,0:T(8,128)(2,1)S(1)} %get-tuple-element.238.refs_3_, ...), custom_call_target="tpu_custom_call" | custom-call | flops 3000000000 | bytes 12000000 | tf_op jit(solution)/shard_map/pallas_call | solution.py:216
  275.9 6.5 %all-to-all-done.12.refs_1_ = bf16[32,48,256]{2,1,0:T(8,128)(2,1)S(1)} async-done(((bf16[32,48,256]{2,1,0:T(8,128)(2,1)}), bf16[32,48,256]{2,1,0:T(8,128)(2,1)S(1)}, u32[]{:S(2)}, u32[]{:S(2)}) %all-to-all-start.12) | async-done | bytes 786464 | tf_op jit(solution)/shard_map/all_to_all | solution.py:2017
  286.4 9.4 %collective-permute-done.5.refs_2_ = bf16[128,512]{1,0:T(8,128)(2,1)S(1)} collective-permute-done((bf16[128,512]{1,0:T(8,128)(2,1)S(1)}, bf16[128,512]{1,0:T(8,128)(2,1)S(1)}, u32[]{:S(2)}, u32[]{:S(2)}) %collective-permute-start.5) | collective-permute-done | bytes 131104 | tf_op jit(solution)/shard_map/ppermute | solution.py:1691
  304.8 5.8 %shard_map.411 = (bf16[128,512]{1,0:T(8,128)(2,1)S(1)}, bf16[64,2048]{1,0:T(8,128)(2,1)S(1)}, bf16[32,8192]{1,0:T(8,128)(2,1)S(1)}) custom-call(s32[6]{0:T(128)S(1)} %stack.9.refs_0_, f32[128,384]{1,0:T(8,128)} %get-tuple-element.232.refs_1_, f32[128,1024]{1,0:T(8,128)} %get-tuple-element.233.refs_2_, bf16[128,1280]{1,0:T(8,128)(2,1)} %get-tuple-element.176.refs_2_.refs_3_, ...), custom_call_target="tpu_custom_call" | custom-call | flops 2000000000 | bytes 8000000 | tf_op jit(solution)/shard_map/pallas_call | solution.py:216
  314.1 18.4 %all_to_all.65 = bf16[32,16,256]{2,1,0:T(8,128)(2,1)S(1)} all-to-all(bf16[32,16,256]{2,1,0:T(8,128)(2,1)S(1)} %bitcast.70), channel_id=1, replica_groups=mesh['x'=2,'core'=2,'tile'=8] {'x','core','tile'}, dimensions={0} | all-to-all | bytes 524288 | tf_op jit(solution)/shard_map/all_to_all | solution.py:2047
  332.5 17.0 %all_to_all.66 = bf16[32,16,256]{2,1,0:T(8,128)(2,1)S(1)} all-to-all(bf16[32,16,256]{2,1,0:T(8,128)(2,1)S(1)} %broadcast_in_dim.46), channel_id=1, replica_groups=mesh['x'=2,'core'=2,'tile'=8] {'x','core','tile'}, dimensions={0} | all-to-all | bytes 524288 | tf_op jit(solution)/shard_map/all_to_all | solution.py:2052
  352.3 59.5 %all-gather.3.cloned.1.call-done = bf16[13312,512]{1,0:T(8,128)(2,1)} async-done(((bf16[416,512]{1,0:T(8,128)(2,1)}), bf16[13312,512]{1,0:T(8,128)(2,1)}) %all-gather.3.cloned.1.call-update) | async-done | bytes 13631504 | tf_op jit(solution)/shard_map/all_gather | solution.py:2059
  411.8 15.2 %shard_map.417 = (f32[9,256,512]{2,1,0:T(8,128)}, f32[9,512,256]{2,1,0:T(8,128)}, f32[9,256,128]{2,1,0:T(8,128)}, f32[2048,512]{1,0:T(8,128)}, f32[512,2048]{1,0...) custom-call(bf16[32,416,512]{2,1,0:T(8,128)(2,1)} %bitcast.97), custom_call_target="tpu_custom_call" | custom-call | flops 7000000000 | bytes 28000000 | tf_op jit(solution)/shard_map/pallas_call | solution.py:1093
  (175 shorter events, 86.4 us)
Async XLA Ops:
  9.8 20.0 %all-to-all-start = ((bf16[8,24,1088]{2,1,0:T(8,128)(2,1)}), bf16[8,24,1088]{2,1,0:T(8,128)(2,1)S(1)}, u32[]{:S(2)}, u32[]{:S(2)}) async-start(bf16[8,24,1088]{2,1,0:T(8,128)(2,1)} %broadcast_in_dim.17), calls=%async_computation | async-start | bytes 884736 | tf_op jit(solution)/shard_map/all_to_all | solution.py:1655
  41.9 12.8 %all-to-all-start.1 = ((bf16[8,128,128]{2,1,0:T(8,128)(2,1)}), bf16[8,128,128]{2,1,0:T(8,128)(2,1)S(1)}, u32[]{:S(2)}, u32[]{:S(2)}) async-start(bf16[8,128,128]{2,1,0:T(8,128)(2,1)} %broadcast_in_dim.18), calls=%async_computation.1 | async-start | bytes 524288 | tf_op jit(solution)/shard_map/all_to_all | solution.py:1655
  73.3 20.0 %copy-start.4 = (bf16[512,512]{1,0:T(8,128)(2,1)S(1)}, bf16[512,512]{1,0:T(8,128)(2,1)}, u32[]{:S(2)}) copy-start(bf16[512,512]{1,0:T(8,128)(2,1)} %refs_5_.6) | copy-start | bytes 1572868
  73.3 20.0 %copy-start.5 = (bf16[512,512]{1,0:T(8,128)(2,1)S(1)}, bf16[512,512]{1,0:T(8,128)(2,1)}, u32[]{:S(2)}) copy-start(bf16[512,512]{1,0:T(8,128)(2,1)} %refs_6_.6) | copy-start | bytes 1572868
  73.3 20.0 %copy-start.14 = (bf16[1,128,512]{2,1,0:T(8,128)(2,1)S(1)}, bf16[1,128,512]{2,1,0:T(8,128)(2,1)}, u32[]{:S(2)}) copy-start(bf16[1,128,512]{2,1,0:T(8,128)(2,1)} %param.34) | copy-start | bytes 393220
  73.3 20.0 %copy-start.16 = (bf16[128,512]{1,0:T(8,128)(2,1)S(1)}, bf16[128,512]{1,0:T(8,128)(2,1)}, u32[]{:S(2)}) copy-start(bf16[128,512]{1,0:T(8,128)(2,1)} %refs_8_.2) | copy-start | bytes 393220
  81.1 12.1 %all-to-all-start.2 = ((bf16[8,128,128]{2,1,0:T(8,128)(2,1)}), bf16[8,128,128]{2,1,0:T(8,128)(2,1)S(1)}, u32[]{:S(2)}, u32[]{:S(2)}) async-start(bf16[8,128,128]{2,1,0:T(8,128)(2,1)} %bitcast.13), calls=%async_computation.2 | async-start | bytes 524288 | tf_op jit(solution)/shard_map/all_to_all | solution.py:1739
  96.9 14.8 %all-to-all-start.3 = ((bf16[8,192,128]{2,1,0:T(8,128)(2,1)}), bf16[8,192,128]{2,1,0:T(8,128)(2,1)S(1)}, u32[]{:S(2)}, u32[]{:S(2)}) async-start(bf16[8,192,128]{2,1,0:T(8,128)(2,1)} %get-tuple-element.180), calls=%async_computation.3 | async-start | bytes 786432 | tf_op jit(solution)/shard_map/all_to_all | solution.py:1750
  100.7 25.0 %copy-start.28 = (bf16[512]{0:T(512)(128)(2,1)S(1)}, bf16[512]{0:T(512)(128)(2,1)}, u32[]{:S(2)}) copy-start(bf16[512]{0:T(512)(128)(2,1)} %param.54) | copy-start | bytes 3076
  100.7 32.3 %copy-start.3 = (bf16[512,512]{1,0:T(8,128)(2,1)S(1)}, bf16[512,512]{1,0:T(8,128)(2,1)}, u32[]{:S(2)}) copy-start(bf16[512,512]{1,0:T(8,128)(2,1)} %refs_4_.3) | copy-start | bytes 1572868
  100.7 32.3 %copy-start.15 = (bf16[1,128,512]{2,1,0:T(8,128)(2,1)S(1)}, bf16[1,128,512]{2,1,0:T(8,128)(2,1)}, u32[]{:S(2)}) copy-start(bf16[1,128,512]{2,1,0:T(8,128)(2,1)} %param.57) | copy-start | bytes 393220
  100.7 32.3 %copy-start.17 = (f32[128,512]{1,0:T(8,128)S(1)}, f32[128,512]{1,0:T(8,128)}, u32[]{:S(2)}) copy-start(f32[128,512]{1,0:T(8,128)} %get-tuple-element.182.refs_2_) | copy-start | bytes 786436
  122.0 11.0 %all-to-all-start.4 = ((bf16[8,64,128]{2,1,0:T(8,128)(2,1)}), bf16[8,64,128]{2,1,0:T(8,128)(2,1)S(1)}, u32[]{:S(2)}, u32[]{:S(2)}) async-start(bf16[8,64,128]{2,1,0:T(8,128)(2,1)} %get-tuple-element.181), calls=%async_computation.4 | async-start | bytes 262144 | tf_op jit(solution)/shard_map/all_to_all | solution.py:1754
  139.8 10.7 %all-to-all-start.5 = ((bf16[8,64,128]{2,1,0:T(8,128)(2,1)}), bf16[8,64,128]{2,1,0:T(8,128)(2,1)S(1)}, u32[]{:S(2)}, u32[]{:S(2)}) async-start(bf16[8,64,128]{2,1,0:T(8,128)(2,1)} %get-tuple-element.186), calls=%async_computation.5 | async-start | bytes 262144 | tf_op jit(solution)/shard_map/all_to_all | solution.py:1758
  143.2 158.8 %reduce-scatter.2.cloned.1.call-start = ((), (), s32[]{:S(2)}) async-start(), calls=%async_computation.14 | async-start | bytes 4866048 | tf_op jit(solution)/shard_map/reduce_scatter | solution.py:1762
  150.5 22.2 %copy-start.6 = (bf16[512,512]{1,0:T(8,128)(2,1)S(1)}, bf16[512,512]{1,0:T(8,128)(2,1)}, u32[]{:S(2)}) copy-start(bf16[512,512]{1,0:T(8,128)(2,1)} %refs_6_.6) | copy-start | bytes 1572868
  158.1 18.7 %copy-start.18 = (bf16[128,512]{1,0:T(8,128)(2,1)S(1)}, bf16[128,512]{1,0:T(8,128)(2,1)}, u32[]{:S(2)}) copy-start(bf16[128,512]{1,0:T(8,128)(2,1)} %get-tuple-element.198.refs_1_) | copy-start | bytes 393220
  158.1 18.7 %copy-start.19 = (bf16[128,128]{1,0:T(8,128)(2,1)S(1)}, bf16[128,128]{1,0:T(8,128)(2,1)}, u32[]{:S(2)}) copy-start(bf16[128,128]{1,0:T(8,128)(2,1)} %get-tuple-element.200.refs_3_) | copy-start | bytes 98308
  158.1 14.6 %all-to-all-start.6 = ((bf16[8,192,128]{2,1,0:T(8,128)(2,1)}), bf16[8,192,128]{2,1,0:T(8,128)(2,1)S(1)}, u32[]{:S(2)}, u32[]{:S(2)}) async-start(bf16[8,192,128]{2,1,0:T(8,128)(2,1)} %get-tuple-element.192), calls=%async_computation.6 | async-start | bytes 786432 | tf_op jit(solution)/shard_map/all_to_all | solution.py:1768
  179.2 12.2 %collective-permute-start = (bf16[1024,512]{1,0:T(8,128)(2,1)}, bf16[1024,512]{1,0:T(8,128)(2,1)S(1)}, u32[]{:S(2)}, u32[]{:S(2)}) collective-permute-start(bf16[1024,512]{1,0:T(8,128)(2,1)} %get-tuple-element.206), channel_id=1, source_target_pairs={{0,8},{8,0},{1,9},{9,1},{2,10},{10,2},{3,11},{11,3},{4,12},{12,4},... | collective-permute-start | bytes 3145736 | tf_op jit(solution)/shard_map/ppermute | solution.py:1691
  179.9 15.6 %all-to-all-start.7 = ((bf16[8,128,128]{2,1,0:T(8,128)(2,1)}), bf16[8,128,128]{2,1,0:T(8,128)(2,1)S(1)}, u32[]{:S(2)}, u32[]{:S(2)}) async-start(bf16[8,128,128]{2,1,0:T(8,128)(2,1)} %broadcast_in_dim.21), calls=%async_computation.7 | async-start | bytes 524288 | tf_op jit(solution)/shard_map/all_to_all | solution.py:1655
  185.5 24.7 %collective-permute-start.1 = (bf16[32,5632]{1,0:T(8,128)(2,1)}, bf16[32,5632]{1,0:T(8,128)(2,1)}, u32[]{:S(2)}, u32[]{:S(2)}) collective-permute-start(bf16[32,5632]{1,0:T(8,128)(2,1)} %copy-done.12), channel_id=1, source_target_pairs={{0,1},{1,2},{2,3},{3,4},{4,5},{5,6},{6,7},{8,9},{9,10},{10,11},{11... | collective-permute-start | bytes 1081352 | tf_op jit(solution)/shard_map/ppermute | solution.py:1668
  190.1 20.1 %collective-permute-start.2 = (bf16[32,5632]{1,0:T(8,128)(2,1)}, bf16[32,5632]{1,0:T(8,128)(2,1)}, u32[]{:S(2)}, u32[]{:S(2)}) collective-permute-start(bf16[32,5632]{1,0:T(8,128)(2,1)} %copy-done.11), channel_id=1, source_target_pairs={{1,0},{2,1},{3,2},{4,3},{5,4},{6,5},{7,6},{9,8},{10,9},{11,10},{12... | collective-permute-start | bytes 1081352 | tf_op jit(solution)/shard_map/ppermute | solution.py:1668
  194.0 34.4 %collective-permute-start.3 = (bf16[512,512]{1,0:T(8,128)(2,1)}, bf16[512,512]{1,0:T(8,128)(2,1)S(1)}, u32[]{:S(2)}, u32[]{:S(2)}) collective-permute-start(bf16[512,512]{1,0:T(8,128)(2,1)} %get-tuple-element.226), channel_id=1, source_target_pairs={{0,16},{16,0},{1,17},{17,1},{2,18},{18,2},{3,19},{19,3},{4,20},{20... | collective-permute-start | bytes 1572872 | tf_op jit(solution)/shard_map/ppermute | solution.py:1691
  210.2 18.1 %copy-start.10 = (bf16[512,512]{1,0:T(8,128)(2,1)S(1)}, bf16[512,512]{1,0:T(8,128)(2,1)}, u32[]{:S(2)}) copy-start(bf16[512,512]{1,0:T(8,128)(2,1)} %copy-done.9) | copy-start | bytes 1572868
  222.1 30.4 %all-to-all-start.8 = ((bf16[8,256,128]{2,1,0:T(8,128)(2,1)}), bf16[8,256,128]{2,1,0:T(8,128)(2,1)S(1)}, u32[]{:S(2)}, u32[]{:S(2)}) async-start(bf16[8,256,128]{2,1,0:T(8,128)(2,1)} %broadcast_in_dim.22), calls=%async_computation.8 | async-start | bytes 1048576 | tf_op jit(solution)/shard_map/all_to_all | solution.py:1655
  229.0 17.1 %collective-permute-start.4 = (bf16[256,512]{1,0:T(8,128)(2,1)S(1)}, bf16[256,512]{1,0:T(8,128)(2,1)S(1)}, u32[]{:S(2)}, u32[]{:S(2)}) collective-permute-start(bf16[256,512]{1,0:T(8,128)(2,1)S(1)} %get-tuple-element.229), channel_id=1, source_target_pairs={{0,1},{1,0},{2,3},{3,2},{4,5},{5,4},{6,7},{7,6},{8,9},{9,8},{10,11... | collective-permute-start | bytes 786440 | tf_op jit(solution)/shard_map/ppermute | solution.py:1691
  252.5 29.9 %all-to-all-start.12 = ((bf16[32,48,256]{2,1,0:T(8,128)(2,1)}), bf16[32,48,256]{2,1,0:T(8,128)(2,1)S(1)}, u32[]{:S(2)}, u32[]{:S(2)}) async-start(bf16[32,48,256]{2,1,0:T(8,128)(2,1)} %bitcast.36), calls=%async_computation.13 | async-start | bytes 1572864 | tf_op jit(solution)/shard_map/all_to_all | solution.py:2017
  282.4 19.5 %all-to-all-start.11 = ((bf16[4,176,512]{2,1,0:T(8,128)(2,1)}), bf16[4,176,512]{2,1,0:T(8,128)(2,1)S(1)}, u32[]{:S(2)}, u32[]{:S(2)}) async-start(bf16[4,176,512]{2,1,0:T(8,128)(2,1)} %get-tuple-element.247), calls=%async_computation.11 | async-start | bytes 1441792 | tf_op jit(solution)/shard_map/all_to_all | solution.py:2057
  285.9 125.9 %all-gather.3.cloned.1.call-start = ((), (), s32[]{:S(2)}) async-start(), calls=%async_computation.15 | async-start | bytes 14057472 | tf_op jit(solution)/shard_map/all_gather | solution.py:2059
  286.2 9.5 %collective-permute-start.5 = (bf16[128,512]{1,0:T(8,128)(2,1)S(1)}, bf16[128,512]{1,0:T(8,128)(2,1)S(1)}, u32[]{:S(2)}, u32[]{:S(2)}) collective-permute-start(bf16[128,512]{1,0:T(8,128)(2,1)S(1)} %get-tuple-element.250), channel_id=1, source_target_pairs={{0,4},{1,5},{2,6},{3,7},{4,0},{5,1},{6,2},{7,3},{8,12},{9,13},{10,... | collective-permute-start | bytes 393224 | tf_op jit(solution)/shard_map/ppermute | solution.py:1691
  296.3 4.3 collective-permute-start.6
  (17 other events, 137.5 us)
Sparse Core Ops, SparseCore 0:
  150.1 125.8 reduce-scatter.1
  304.4 107.3 all-gather.2
